TPU v7x, 32 devices: a whole 2x2x4 slice. The times are simulated.
32 devices in a mesh: dp: 32 (over z, y, x, core).
Axes of the slice: x: 2, y: 2, z: 4, core: 2. Of those that a mesh axis runs over, the one named last changes fastest.
Arguments:
- sequence_elements: bfloat16 [5120, 1536], P('dp'), may hold values from -6 to 6
- result_sensitivity: bfloat16 [5120, 1536], P('dp'), may hold values from -6 to 6
- mixer_gain: bfloat16 [1536], replicated, may hold values from 0.5 to 1.5
- mixer_offset: bfloat16 [1536], replicated, may hold values from -1.5 to 1.5
- question_matrix: bfloat16 [1536, 1536], replicated, may hold values from -0.15625 to 0.15625
- lookup_matrix: bfloat16 [1536, 1536], replicated, may hold values from -0.15625 to 0.15625
- content_matrix: bfloat16 [1536, 1536], replicated, may hold values from -0.15625 to 0.15625
- mixer_projection_matrix: bfloat16 [1536, 1536], replicated, may hold values from -0.625 to 0.625
- feedforward_gain: bfloat16 [1536], replicated, may hold values from 0.5 to 1.5
- feedforward_offset: bfloat16 [1536], replicated, may hold values from -1.5 to 1.5
- expand_matrix: bfloat16 [1536, 6144], P('dp'), may hold values from -0.15625 to 0.15625
- inner_neuron_offset: bfloat16 [6144], P('dp'), may hold values from -2.5 to 2.5
- contract_matrix: bfloat16 [6144, 1536], P('dp'), may hold values from -0.15625 to 0.15625
- feedforward_result_offset: bfloat16 [1536], P('dp'), may hold values from -1.5 to 1.5
- sequence_level_choice: int32 [32], P('dp'), may hold values from 0 to 3, as said below
- servers_per_level: int32 [4], replicated, may hold values from 6 to 10, as said below
- accepted_row_limit: int32 [4], replicated, may hold values from 128 to 213, as said below
- server_selection: int32 [32, 160], P('dp'), may hold values from 0 to 318, as said below
Outputs:
- layer_output: bfloat16 [5120, 1536], P('dp')
- layer_input_gradient: bfloat16 [5120, 1536], P('dp')
- leading_norm_gradient: float32 [1536], P('dp')
- leading_bias_gradient: float32 [1536], P('dp')
- query_weight_gradient: float32 [1536, 1536], P('dp')
- key_weight_gradient: float32 [1536, 1536], P('dp')
- value_weight_gradient: float32 [1536, 1536], P('dp')
- attention_output_gradient: float32 [1536, 1536], P('dp')
- middle_norm_gradient: float32 [1536], P('dp')
- middle_bias_gradient: float32 [1536], P('dp')
- up_weight_gradient: float32 [1536, 6144], P('dp')
- hidden_bias_gradient: float32 [6144], P('dp')
- down_weight_gradient: float32 [6144, 1536], P('dp')
- output_bias_gradient: float32 [1536], P('dp')
Inputs may be any that keep to these rules, and one draw needn't show every extreme that they name: `sequence_level_choice`: the 1 sequence of one device have different granularity indices. `servers_per_level`: each group holds 3, 4 or 5 sixteenths of the devices, and the groups together hold all devices. `accepted_row_limit`: some prefix has capacity 213. `server_selection`: within each sequence the values are 160 consecutive integers, each once.
All inputs are finite; a program needn't handle non-finite values.
Results may differ from a plain program's by a relative error of at most 0.013.
Values may be sent and summed in bfloat16 or wider, within the bound.
No kernel may reach another device: no remote copies, remote signals or barrier semaphores. Data moves between devices by JAX's collectives and lax.ppermute only.
A program may use at most 384 MiB of HBM per device.

v0:
```python
import jax
import jax.numpy as jnp
from jax import lax
from jax.sharding import PartitionSpec as P

HEAD_DIM = 128
LEVELS = 4


EPSILON = 1e-05
NEGATIVE = -1e30


def as_sent(shard):
    return jax.tree.map(lambda a: a.astype(jnp.bfloat16) if a.dtype == jnp.float32 else a, shard)


def standardize_rows(values, gain, shift):
    center = values - jnp.mean(values, axis=-1, keepdims=True)
    spread = jnp.mean(center * center, axis=-1, keepdims=True)
    return center * lax.rsqrt(spread + EPSILON) * gain + shift


def rope_tables(length, head_size):
    half = head_size // 2
    places = jnp.arange(length).astype(jnp.float32)
    rates = 10000.0 ** (-(jnp.arange(half).astype(jnp.float32) * 2.0 / head_size))
    angles = places[:, None] * rates[None, :]
    return (jnp.cos(angles), jnp.sin(angles))


def rotate(values, cosine, sine, turning):
    half = values.shape[-1] // 2
    first = values[..., :half]
    second = values[..., half:]
    cosine = cosine[None, :, None, :]
    sine = sine[None, :, None, :] * turning
    return jnp.concatenate(
        [first * cosine - second * sine, second * cosine + first * sine], axis=-1
    )


def contract_last(left, right):
    return lax.dot_general(
        left, right, (((1,), (1,)), ((), ())), preferred_element_type=jnp.float32
    )


def contract_first(left, right):
    return lax.dot_general(
        left, right, (((0,), (0,)), ((), ())), preferred_element_type=jnp.float32
    )


def gelu_tanh(values):
    return jax.nn.gelu(values, approximate=True)


def serve_rows(row_block, expand_full, hidden_full, contract_full, result_full, prefix_width):
    hidden = jnp.dot(row_block, expand_full[:, :prefix_width], preferred_element_type=jnp.float32)
    hidden = hidden + hidden_full[:prefix_width].astype(jnp.float32)
    active = gelu_tanh(hidden).astype(jnp.bfloat16)
    output = jnp.dot(active, contract_full[:prefix_width], preferred_element_type=jnp.float32)
    return (output + result_full.astype(jnp.float32)).astype(jnp.bfloat16)


def serve_grads(row_block, row_grads, expand_full, hidden_full, contract_full, prefix_width):
    full_width = expand_full.shape[1]
    padding = full_width - prefix_width
    hidden = jnp.dot(row_block, expand_full[:, :prefix_width], preferred_element_type=jnp.float32)
    hidden = hidden + hidden_full[:prefix_width].astype(jnp.float32)
    active_full, gelu_back = jax.vjp(gelu_tanh, hidden)
    active = active_full.astype(jnp.bfloat16)
    active_grad = contract_last(row_grads, contract_full[:prefix_width])
    hidden_grad = gelu_back(active_grad)[0].astype(jnp.bfloat16)
    contract_grad = contract_first(active, row_grads)
    expand_grad = contract_first(row_block, hidden_grad)
    bias_grad = jnp.sum(hidden_grad.astype(jnp.float32), axis=0)
    result_grad = jnp.sum(row_grads.astype(jnp.float32), axis=0)
    rows_grad = contract_last(hidden_grad, expand_full[:, :prefix_width]).astype(jnp.bfloat16)
    return (
        rows_grad,
        jnp.pad(expand_grad, ((0, 0), (0, padding))),
        jnp.pad(bias_grad, (0, padding)),
        jnp.pad(contract_grad, ((0, padding), (0, 0))),
        result_grad,
    )


def per_device(
    sequence_elements,
    result_sensitivity,
    mixer_gain,
    mixer_offset,
    question_matrix,
    lookup_matrix,
    content_matrix,
    mixer_projection_matrix,
    feedforward_gain,
    feedforward_offset,
    expand_matrix,
    inner_neuron_offset,
    contract_matrix,
    feedforward_result_offset,
    sequence_level_choice,
    servers_per_level,
    accepted_row_limit,
    server_selection,
):
    devices = lax.axis_size("dp")
    device_index = lax.axis_index("dp")
    seq_count, seq_len = server_selection.shape
    tok_count = seq_count * seq_len
    model_width = sequence_elements.shape[1]
    head_count = model_width // HEAD_DIM
    pair_slots = (seq_len * 16 + 3 * devices - 1) // (3 * devices)
    cap_rows = tok_count * 4 // 3
    expand_full, hidden_full, contract_full, result_full = (
        lax.all_gather(expand_matrix, "dp", axis=0, tiled=True),
        lax.all_gather(inner_neuron_offset, "dp", axis=0, tiled=True),
        lax.all_gather(contract_matrix, "dp", axis=0, tiled=True),
        lax.all_gather(feedforward_result_offset, "dp", axis=0, tiled=True),
    )
    feed_width = expand_full.shape[1]
    prefix_widths = [feed_width // 8 * (1 << prefix_level) for prefix_level in range(LEVELS)]

    def make_forward(prefix_width):

        def apply_prefix(row_block):
            return serve_rows(
                row_block, expand_full, hidden_full, contract_full, result_full, prefix_width
            )

        return apply_prefix

    def make_backward(prefix_width):

        def apply_reverse(row_block, row_grads):
            return serve_grads(
                row_block, row_grads, expand_full, hidden_full, contract_full, prefix_width
            )

        return apply_reverse

    forward_branches = [make_forward(prefix_width) for prefix_width in prefix_widths]
    backward_branches = [make_backward(prefix_width) for prefix_width in prefix_widths]
    block_arguments = sequence_elements.astype(jnp.float32)
    gain_first = mixer_gain.astype(jnp.float32)
    first_shift_amount = mixer_offset.astype(jnp.float32)
    gain_second = feedforward_gain.astype(jnp.float32)
    shift_second = feedforward_offset.astype(jnp.float32)
    shape_heads = (seq_count, seq_len, head_count, HEAD_DIM)
    cosine, sine = rope_tables(seq_len, HEAD_DIM)
    scale = HEAD_DIM ** (-0.5)
    causal = jnp.arange(seq_len)[:, None] >= jnp.arange(seq_len)[None, :]
    first_standardized = standardize_rows(block_arguments, gain_first, first_shift_amount).astype(
        jnp.bfloat16
    )
    query_rows = jnp.dot(
        first_standardized, question_matrix, preferred_element_type=jnp.float32
    ).reshape(shape_heads)
    key_rows = jnp.dot(
        first_standardized, lookup_matrix, preferred_element_type=jnp.float32
    ).reshape(shape_heads)
    query_rot = rotate(query_rows, cosine, sine, 1.0).astype(jnp.bfloat16)
    key_rot = rotate(key_rows, cosine, sine, 1.0).astype(jnp.bfloat16)
    value_rows = (
        jnp.dot(first_standardized, content_matrix, preferred_element_type=jnp.float32)
        .astype(jnp.bfloat16)
        .reshape(shape_heads)
    )

    def scores_of(queries, keys_rot):
        raw = (
            jnp.einsum("slhe,smhe->shlm", queries, keys_rot, preferred_element_type=jnp.float32)
            * scale
        )
        return jnp.where(causal, raw, NEGATIVE)

    scores = scores_of(query_rot, key_rot)
    row_top = jnp.max(scores, axis=-1, keepdims=True)
    log_total = row_top + jnp.log(jnp.sum(jnp.exp(scores - row_top), axis=-1, keepdims=True))
    probs_low = jnp.exp(scores - log_total).astype(jnp.bfloat16)
    context = jnp.einsum(
        "shlm,smhe->slhe", probs_low, value_rows, preferred_element_type=jnp.float32
    )
    context = context.reshape(tok_count, model_width).astype(jnp.bfloat16)
    mixed = block_arguments + jnp.dot(
        context, mixer_projection_matrix, preferred_element_type=jnp.float32
    )
    normed_second = standardize_rows(mixed, gain_second, shift_second).astype(jnp.bfloat16)
    upper = jnp.cumsum(servers_per_level)
    lower = upper - servers_per_level
    level_rows = jnp.repeat(sequence_level_choice, seq_len)
    level_hot = (level_rows[:, None] == jnp.arange(LEVELS)[None, :]).astype(jnp.int32)
    size_rows = jnp.sum(level_hot * servers_per_level[None, :], axis=1)
    start_rows = jnp.sum(level_hot * lower[None, :], axis=1)
    target = start_rows + server_selection.reshape(-1) % size_rows
    target_hot = (target[:, None] == jnp.arange(devices)[None, :]).astype(jnp.int32)
    slot_rows = jnp.sum((jnp.cumsum(target_hot, axis=0) - target_hot) * target_hot, axis=1)
    sent_counts = jnp.sum(target_hot, axis=0)
    flat_place = target * pair_slots + slot_rows
    my_level = jnp.sum((device_index >= upper).astype(jnp.int32))
    my_limit = jnp.sum(jnp.where(jnp.arange(LEVELS) == my_level, accepted_row_limit, 0))

    def to_slots(row_values):
        buffer = (
            jnp.zeros((devices * pair_slots, model_width), jnp.bfloat16)
            .at[flat_place]
            .set(row_values)
        )
        return buffer.reshape(devices, pair_slots, model_width)

    arrived, arrived_counts = (
        lax.all_to_all(to_slots(normed_second), "dp", split_axis=0, concat_axis=0, tiled=True),
        lax.all_to_all(sent_counts, "dp", split_axis=0, concat_axis=0, tiled=True),
    )
    filled = (
        (jnp.arange(pair_slots)[None, :] < arrived_counts[:, None]).reshape(-1).astype(jnp.int32)
    )
    order_rank = jnp.cumsum(filled) - filled
    kept_slot = (filled > 0) & (order_rank < my_limit)
    compact_place = jnp.where(kept_slot, order_rank, cap_rows)
    compact = (
        jnp.zeros((cap_rows, model_width), jnp.bfloat16)
        .at[compact_place]
        .set(arrived.reshape(-1, model_width), mode="drop")
    )
    served = lax.switch(my_level, forward_branches, compact)
    answer = jnp.take(served, compact_place, axis=0, mode="fill", fill_value=0)
    answered = lax.all_to_all(
        as_sent(answer.reshape(devices, pair_slots, model_width)),
        "dp",
        split_axis=0,
        concat_axis=0,
        tiled=True,
    )
    branch_out = answered.reshape(-1, model_width)[flat_place]
    arrived_grad = lax.all_to_all(
        to_slots(result_sensitivity), "dp", split_axis=0, concat_axis=0, tiled=True
    )
    compact_grad = (
        jnp.zeros((cap_rows, model_width), jnp.bfloat16)
        .at[compact_place]
        .set(arrived_grad.reshape(-1, model_width), mode="drop")
    )
    rows_grad, expand_grad, bias_grad, contract_grad, result_grad = lax.switch(
        my_level, backward_branches, compact, compact_grad
    )
    sent_back = jnp.take(rows_grad, compact_place, axis=0, mode="fill", fill_value=0)
    returned_grad = lax.all_to_all(
        as_sent(sent_back.reshape(devices, pair_slots, model_width)),
        "dp",
        split_axis=0,
        concat_axis=0,
        tiled=True,
    )
    second_grad = returned_grad.reshape(-1, model_width)[flat_place]
    layer_output = (mixed + branch_out.astype(jnp.float32)).astype(jnp.bfloat16)
    _, second_back = jax.vjp(standardize_rows, mixed, gain_second, shift_second)
    mixed_part, midnorm_grad, midshift_grad = second_back(second_grad.astype(jnp.float32))
    mixed_grad = result_sensitivity.astype(jnp.float32) + mixed_part
    mixed_low = mixed_grad.astype(jnp.bfloat16)
    mixing_grad = contract_first(context, mixed_low)
    context_grad = (
        contract_last(mixed_low, mixer_projection_matrix).astype(jnp.bfloat16).reshape(shape_heads)
    )
    probs_grad = jnp.einsum(
        "slhe,smhe->shlm", context_grad, value_rows, preferred_element_type=jnp.float32
    )
    probs = jnp.exp(scores_of(query_rot, key_rot) - log_total)
    value_grad = jnp.einsum(
        "shlm,slhe->smhe",
        probs.astype(jnp.bfloat16),
        context_grad,
        preferred_element_type=jnp.float32,
    ).astype(jnp.bfloat16)
    scores_grad = (
        probs * (probs_grad - jnp.sum(probs_grad * probs, axis=-1, keepdims=True))
    ).astype(jnp.bfloat16)
    query_turned = (
        jnp.einsum("shlm,smhe->slhe", scores_grad, key_rot, preferred_element_type=jnp.float32)
        * scale
    )
    key_turned = (
        jnp.einsum("shlm,slhe->smhe", scores_grad, query_rot, preferred_element_type=jnp.float32)
        * scale
    )
    query_grad = (
        rotate(query_turned, cosine, sine, -1.0)
        .astype(jnp.bfloat16)
        .reshape(tok_count, model_width)
    )
    key_grad = (
        rotate(key_turned, cosine, sine, -1.0).astype(jnp.bfloat16).reshape(tok_count, model_width)
    )
    value_flat = value_grad.reshape(tok_count, model_width)
    query_wgrad = contract_first(first_standardized, query_grad)
    key_wgrad = contract_first(first_standardized, key_grad)
    value_wgrad = contract_first(first_standardized, value_flat)
    leading_gradient = (
        contract_last(query_grad, question_matrix)
        + contract_last(key_grad, lookup_matrix)
        + contract_last(value_flat, content_matrix)
    )
    _, leading_backward = jax.vjp(standardize_rows, block_arguments, gain_first, first_shift_amount)
    input_portion, leading_norm_grad, leading_bias_grad = leading_backward(leading_gradient)
    layer_input_gradient = (mixed_grad + input_portion).astype(jnp.bfloat16)
    (
        share_prenorm,
        leading_bias_share,
        share_query,
        share_key,
        share_value,
        share_mixing,
        share_midnorm,
        share_midshift,
    ) = (
        lax.psum_scatter(leading_norm_grad, "dp", scatter_dimension=0, tiled=True),
        lax.psum_scatter(leading_bias_grad, "dp", scatter_dimension=0, tiled=True),
        lax.psum_scatter(query_wgrad, "dp", scatter_dimension=0, tiled=True),
        lax.psum_scatter(key_wgrad, "dp", scatter_dimension=0, tiled=True),
        lax.psum_scatter(value_wgrad, "dp", scatter_dimension=0, tiled=True),
        lax.psum_scatter(mixing_grad, "dp", scatter_dimension=0, tiled=True),
        lax.psum_scatter(midnorm_grad, "dp", scatter_dimension=0, tiled=True),
        lax.psum_scatter(midshift_grad, "dp", scatter_dimension=0, tiled=True),
    )
    share_expand, share_hidden = (
        lax.psum_scatter(expand_grad, "dp", scatter_dimension=0, tiled=True),
        lax.psum_scatter(bias_grad, "dp", scatter_dimension=0, tiled=True),
    )
    share_contract, share_result = (
        lax.psum_scatter(contract_grad, "dp", scatter_dimension=0, tiled=True),
        lax.psum_scatter(result_grad, "dp", scatter_dimension=0, tiled=True),
    )
    return (
        layer_output,
        layer_input_gradient,
        share_prenorm,
        leading_bias_share,
        share_query,
        share_key,
        share_value,
        share_mixing,
        share_midnorm,
        share_midshift,
        share_expand,
        share_hidden,
        share_contract,
        share_result,
    )


def solution(mesh):
    placed = (
        P("dp", None),
        P("dp", None),
        P(),
        P(),
        P(),
        P(),
        P(),
        P(),
        P(),
        P(),
        P("dp", None),
        P("dp"),
        P("dp", None),
        P("dp"),
        P("dp"),
        P(),
        P(),
        P("dp", None),
    )
    return jax.shard_map(
        per_device,
        mesh=mesh,
        in_specs=placed,
        out_specs=(
            P("dp", None),
            P("dp", None),
            P("dp"),
            P("dp"),
            P("dp", None),
            P("dp", None),
            P("dp", None),
            P("dp", None),
            P("dp"),
            P("dp"),
            P("dp", None),
            P("dp"),
            P("dp", None),
            P("dp"),
        ),
        check_vma=False,
    )
```

profile of v0, /device:TPU:0, one launch (start us, length us, event | category | flops | bytes accessed | tf_op | source)
XLA Modules:
  0.0 1944.2 jit_solution(8058070395264297273)
XLA Ops:
  10.1 1.3 bitcast_subtract_fusion
  14.7 7.3 all-to-all-start
  22.9 2.9 scatter_custom_fusion.2
  25.8 2.6 reshape.523
  29.2 5.3 all-to-all-start.3
  35.6 3.3 fusion.279
  39.1 4.3 fusion.277
  43.4 1.4 reshape.510
  46.8 1.3 fusion.217
  53.6 3.5 scatter_custom_fusion
  57.1 4.4 reshape.519
  61.6 96.3 %all-to-all-done.3 = bf16[32,27,1536]{2,1,0:T(8,128)(2,1)} async-done(((bf16[32,27,1536]{2,1,0:T(8,128)(2,1)}), bf16[32,27,1536]{2,1,0:T(8,128)(2,1)}, u32[]{:S(2)}, u32[]{:S(2)}) %all-to-all-start.3) | async-done | bytes 2654240 | tf_op jit(solution)/shard_map/all_to_all | solution.py:239
  157.9 4.3 all-to-all-start.1
  163.4 120.6 %all-reduce.20 = (bf16[6144]{0:T(1024)(128)(2,1)S(1)}, bf16[1536]{0:T(1024)(128)(2,1)S(1)}) all-reduce(bf16[6144]{0:T(1024)(128)(2,1)S(1)} %dynamic-update-slice, bf16[1536]{0:T(1024)(128)(2,1)S(1)} %dynamic-update-slice.1), channel_id=1, replica_groups=mesh['dp'=32] {'dp'}, use_global_device_ids=true, to_apply=%add.11 | all-reduce | flops 7680 | bytes 30720
  284.0 1.3 fusion.269
  286.7 1.2 compare_and_fusion
  288.5 3.0 reshape.591
  291.6 6.1 scatter_custom_fusion.3
  297.6 4.7 reshape.575
  302.4 7.4 scatter_custom_fusion.1
  309.8 49.9 %all-gather.3.cloned.1.call-done = bf16[1536,6144]{1,0:T(8,128)(2,1)} async-done(((bf16[48,6144]{1,0:T(8,128)(2,1)}), bf16[1536,6144]{1,0:T(8,128)(2,1)}) %all-gather.3.cloned.1.call-update) | async-done | bytes 18874384 | tf_op jit(solution)/shard_map/all_gather | solution.py:119
  359.7 4.1 conditional.4
  359.7 3.9 fusion
  364.9 42.3 %conditional.5 = (bf16[213,1536]{1,0:T(8,128)(2,1)S(1)}, f32[1536,6144]{0,1:T(8,128)}, f32[6144]{0:T(1024)S(1)}, f32[6144,1536]{1,0:T(8,128)}, f32[]{:T(128)}, /*index=5*/bf16[213,1536]{1,0:T(8,128)(2,1)S(1)}) conditional(s32[]{:T(128)} %clamp.4, (bf16[6144,1536]{1,0:T(8,128)(2,1)}, bf16[213,1536]{1,0:T(8,128)(2,1)S(1)}, ...), branch_computations={%region_25.29_spmd.clone, %region_28.32_spmd.clone, %region_31.35_... | conditional | flops 20143079424 | bytes 272016640
  364.9 2.4 fusion.99
  367.3 2.8 convert_reduce_fusion
  370.0 2.5 fusion.95
  372.6 3.1 convolution_bitcast_fusion
  375.6 14.7 pad.45
  391.2 12.9 pad.47
  407.3 4.4 gather_fusion.3
  411.8 4.4 gather_fusion.2
  416.3 4.5 broadcast_select_fusion
  420.8 4.4 reshape.525
  425.2 67.3 %all-to-all-start.4 = ((bf16[32,27,1536]{2,1,0:T(8,128)(2,1)}), bf16[32,27,1536]{2,1,0:T(8,128)(2,1)}, u32[]{:S(2)}, u32[]{:S(2)}) async-start(bf16[32,27,1536]{2,1,0:T(8,128)(2,1)} %reshape.525), calls=%async_computation.4 | async-start | bytes 6291456 | tf_op jit(solution)/shard_map/all_to_all | solution.py:251
  492.6 2.6 reshape.521
  495.1 68.9 %all-to-all-done.4 = bf16[32,27,1536]{2,1,0:T(8,128)(2,1)} async-done(((bf16[32,27,1536]{2,1,0:T(8,128)(2,1)}), bf16[32,27,1536]{2,1,0:T(8,128)(2,1)}, u32[]{:S(2)}, u32[]{:S(2)}) %all-to-all-start.4) | async-done | bytes 2654240 | tf_op jit(solution)/shard_map/all_to_all | solution.py:251
  564.0 4.0 all-to-all-start.2
  568.4 4.5 reshape.526
  572.9 3.6 gather_fusion.1
  577.1 62.5 %all-to-all-done.2 = bf16[32,27,1536]{2,1,0:T(8,128)(2,1)} async-done(((bf16[32,27,1536]{2,1,0:T(8,128)(2,1)}), bf16[32,27,1536]{2,1,0:T(8,128)(2,1)}, u32[]{:S(2)}, u32[]{:S(2)}) %all-to-all-start.2) | async-done | bytes 2654240 | tf_op jit(solution)/shard_map/all_to_all | solution.py:231
  639.5 4.5 reshape.522
  644.1 3.5 gather_fusion
  647.6 1.1 fusion.284
  650.0 4.2 fusion.204
  657.9 1.6 subtract_convert_fusion
  660.9 5.1 fusion.227
  666.4 1.5 pad_maximum_fusion.3
  668.9 5.2 fusion.224
  674.1 1.5 fusion.202
  676.7 5.2 fusion.221
  683.1 5.1 fusion.231
  688.3 37.4 %copy.113 = f32[1536,6144]{1,0:T(8,128)} copy(f32[1536,6144]{0,1:T(8,128)} %get-tuple-element.161) | data formatting | bytes 75497472
  726.9 4.1 fusion.229
  731.0 4.2 convolution_add_fusion.3
  735.2 4.4 fusion.282
  740.1 39.2 %all-reduce.19 = (f32[1536]{0:T(1024)S(1)}, f32[1536]{0:T(1024)S(1)}, f32[1536]{0:T(1024)S(1)}, f32[1536]{0:T(1024)S(1)}, f32[6144]{0:T(1024)S(1)}, /*index=5*/f32[1536]{0:T(1024)S(1)}) all-reduce(f32[1536]{0:T(1024)S(1)} %get-tuple-element.211, f32[1536]{0:T(1024)S(1)} %get-tuple-element.215, ...), channel_id=2, replica_groups=mesh['dp'=32] {'dp'}, use_global_device_ids=true, to_apply=%region_43.45.clone | all-reduce | flops 13824 | bytes 110592
  782.9 1.3 add_convert_fusion.1
  784.2 17.5 reduce-scatter.7.cloned.1.call-done
  801.6 142.1 %reduce-scatter.9.cloned.1.call-done = f32[48,1536]{1,0:T(8,128)} async-done(((f32[1536,1536]{1,0:T(8,128)}), f32[48,1536]{1,0:T(8,128)}) %reduce-scatter.9.cloned.1.call-update) | async-done | bytes 294928 | tf_op jit(solution)/shard_map/reduce_scatter | solution.py:322
  943.7 140.9 %reduce-scatter.11.cloned.1.call-done = f32[48,1536]{1,0:T(8,128)} async-done(((f32[1536,1536]{1,0:T(8,128)}), f32[48,1536]{1,0:T(8,128)}) %reduce-scatter.11.cloned.1.call-update) | async-done | bytes 294928 | tf_op jit(solution)/shard_map/reduce_scatter | solution.py:323
  1084.6 142.1 %reduce-scatter.13.cloned.1.call-done = f32[48,1536]{1,0:T(8,128)} async-done(((f32[1536,1536]{1,0:T(8,128)}), f32[48,1536]{1,0:T(8,128)}) %reduce-scatter.13.cloned.1.call-update) | async-done | bytes 294928 | tf_op jit(solution)/shard_map/reduce_scatter | solution.py:324
  1226.7 354.5 %reduce-scatter.15.cloned.1.call-done = f32[48,6144]{1,0:T(8,128)} async-done(((f32[1536,6144]{1,0:T(8,128)}), f32[48,6144]{1,0:T(8,128)}) %reduce-scatter.15.cloned.1.call-update) | async-done | bytes 1179664 | tf_op jit(solution)/shard_map/reduce_scatter | solution.py:329
  1581.2 355.9 %reduce-scatter.17.cloned.1.call-done = f32[192,1536]{1,0:T(8,128)} async-done(((f32[6144,1536]{1,0:T(8,128)}), f32[192,1536]{1,0:T(8,128)}) %reduce-scatter.17.cloned.1.call-update) | async-done | bytes 1179664 | tf_op jit(solution)/shard_map/reduce_scatter | solution.py:333
  (246 shorter events, 36.1 us)
Async XLA Ops:
  7.2 302.6 %all-gather.5.cloned.1.call-start = ((), (), s32[]{:S(2)}) async-start(), calls=%async_computation.12 | async-start | bytes 19464192 | tf_op jit(solution)/shard_map/all_gather | solution.py:121
  7.9 351.8 %all-gather.3.cloned.1.call-start = ((), (), s32[]{:S(2)}) async-start(), calls=%async_computation.11 | async-start | bytes 19464192 | tf_op jit(solution)/shard_map/all_gather | solution.py:119
  14.7 14.5 all-to-all-start
  22.9 30.7 %copy-start.66 = (s32[160,1]{0,1:T(1,128)}, s32[160,1]{0,1:T(1,128)S(1)}, u32[]{:S(2)}) copy-start(s32[160,1]{0,1:T(1,128)S(1)} %compare_select_fusion.1) | copy-start | bytes 1924
  28.4 6.2 copy-start
  28.4 6.3 copy-start.62
  28.4 6.3 copy-start.63
  29.2 128.7 %all-to-all-start.3 = ((bf16[32,27,1536]{2,1,0:T(8,128)(2,1)}), bf16[32,27,1536]{2,1,0:T(8,128)(2,1)}, u32[]{:S(2)}, u32[]{:S(2)}) async-start(bf16[32,27,1536]{2,1,0:T(8,128)(2,1)} %reshape.523), calls=%async_computation.3 | async-start | bytes 6291456 | tf_op jit(solution)/shard_map/all_to_all | solution.py:239
  34.7 14.7 copy-start.40
  34.7 14.6 copy-start.36
  34.8 14.6 copy-start.45
  35.6 13.8 copy-start.49
  45.9 3.5 slice-start.2
  46.8 2.7 slice-start.3
  49.0 1.5 copy-start.2
  49.0 3.1 slice-start
  49.4 2.8 slice-start.1
  50.5 2.8 copy-start.32
  50.5 1.5 copy-start.64
  50.5 1.5 copy-start.65
  52.0 1.6 copy-start.47
  53.3 8.3 copy-start.4
  53.3 8.3 copy-start.53
  53.6 8.0 copy-start.59
  53.6 8.0 copy-start.55
  61.6 101.3 %copy-start.68 = (bf16[192]{0:T(256)(128)(2,1)S(1)}, bf16[192]{0:T(256)(128)(2,1)}, u32[]{:S(2)}) copy-start(bf16[192]{0:T(256)(128)(2,1)} %param.39) | copy-start | bytes 1156
  61.6 101.5 %copy-start.69 = (bf16[48]{0:T(256)(128)(2,1)S(1)}, bf16[48]{0:T(256)(128)(2,1)}, u32[]{:S(2)}) copy-start(bf16[48]{0:T(256)(128)(2,1)} %param.41) | copy-start | bytes 292
  61.6 222.4 %copy-start.70 = (s32[4]{0:T(128)S(1)}, s32[4]{0:T(128)}, u32[]{:S(2)}) copy-start(s32[4]{0:T(128)} %param.44) | copy-start | bytes 52
  157.9 139.7 %all-to-all-start.1 = ((bf16[32,27,1536]{2,1,0:T(8,128)(2,1)}), bf16[32,27,1536]{2,1,0:T(8,128)(2,1)}, u32[]{:S(2)}, u32[]{:S(2)}) async-start(bf16[32,27,1536]{2,1,0:T(8,128)(2,1)} %reshape.519), calls=%async_computation.1 | async-start | bytes 6291456 | tf_op jit(solution)/shard_map/all_to_all | solution.py:215
  364.5 42.7 %copy-start.51 = (s32[1024]{0:T(1024)S(1)}, s32[1024]{0:T(1024)}, u32[]{:S(2)}) copy-start(s32[1024]{0:T(1024)} %pad_clamp_fusion.1) | copy-start | bytes 12292
  407.3 4.5 copy-start.35
  407.3 4.5 copy-start.52
  411.8 4.5 copy-start.61
  425.2 138.8 %all-to-all-start.4 = ((bf16[32,27,1536]{2,1,0:T(8,128)(2,1)}), bf16[32,27,1536]{2,1,0:T(8,128)(2,1)}, u32[]{:S(2)}, u32[]{:S(2)}) async-start(bf16[32,27,1536]{2,1,0:T(8,128)(2,1)} %reshape.525), calls=%async_computation.4 | async-start | bytes 6291456 | tf_op jit(solution)/shard_map/all_to_all | solution.py:251
  495.1 73.2 %copy-start.67 = (s32[160,1]{0,1:T(1,128)S(1)}, s32[160,1]{0,1:T(1,128)}, u32[]{:S(2)}) copy-start(s32[160,1]{0,1:T(1,128)} %copy-done.66) | copy-start | bytes 1924
  564.0 75.5 %all-to-all-start.2 = ((bf16[32,27,1536]{2,1,0:T(8,128)(2,1)}), bf16[32,27,1536]{2,1,0:T(8,128)(2,1)}, u32[]{:S(2)}, u32[]{:S(2)}) async-start(bf16[32,27,1536]{2,1,0:T(8,128)(2,1)} %reshape.521), calls=%async_computation.2 | async-start | bytes 6291456 | tf_op jit(solution)/shard_map/all_to_all | solution.py:231
  568.1 233.5 %reduce-scatter.7.cloned.1.call-start = ((), (), s32[]{:S(2)}) async-start(), calls=%async_computation.13 | async-start | bytes 9732096 | tf_op jit(solution)/shard_map/reduce_scatter | solution.py:321
  572.9 3.6 copy-start.5
  572.9 3.7 copy-start.48
  572.9 3.7 copy-start.54
  572.9 3.7 copy-start.56
  572.9 4.2 copy-start.60
  647.6 2.1 copy-start.30
  649.9 4.3 copy-start.20
  649.9 4.3 copy-start.3
  649.9 4.3 copy-start.33
  649.9 4.3 copy-start.43
  655.9 1.9 copy-start.39
  655.9 1.9 copy-start.44
  657.9 3.0 copy-start.37
  657.9 3.0 copy-start.41
  657.9 3.0 copy-start.46
  657.9 3.0 copy-start.50
  659.6 1.4 copy-start.1
  666.1 277.7 %reduce-scatter.9.cloned.1.call-start = ((), (), s32[]{:S(2)}) async-start(), calls=%async_computation.14 | async-start | bytes 9732096 | tf_op jit(solution)/shard_map/reduce_scatter | solution.py:322
  674.1 410.5 %reduce-scatter.11.cloned.1.call-start = ((), (), s32[]{:S(2)}) async-start(), calls=%async_computation.15 | async-start | bytes 9732096 | tf_op jit(solution)/shard_map/reduce_scatter | solution.py:323
  681.9 544.9 %reduce-scatter.13.cloned.1.call-start = ((), (), s32[]{:S(2)}) async-start(), calls=%async_computation.16 | async-start | bytes 9732096 | tf_op jit(solution)/shard_map/reduce_scatter | solution.py:324
  688.2 893.0 %reduce-scatter.15.cloned.1.call-start = ((), (), s32[]{:S(2)}) async-start(), calls=%async_computation.17 | async-start | bytes 38928384 | tf_op jit(solution)/shard_map/reduce_scatter | solution.py:329
  725.7 1211.4 %reduce-scatter.17.cloned.1.call-start = ((), (), s32[]{:S(2)}) async-start(), calls=%async_computation.18 | async-start | bytes 38928384 | tf_op jit(solution)/shard_map/reduce_scatter | solution.py:333
  726.9 4.1 copy-start.25
  731.0 4.2 copy-start.27
  735.2 4.4 copy-start.58
  735.2 47.7 %copy-start.8 = (f32[160,1536]{1,0:T(8,128)S(1)}, f32[160,1536]{1,0:T(8,128)}, u32[]{:S(2)}) copy-start(f32[160,1536]{1,0:T(8,128)} %copy-done.7) | copy-start | bytes 2949124
  735.2 47.7 %copy-start.31 = (bf16[160,1536]{1,0:T(8,128)(2,1)S(1)}, bf16[160,1536]{1,0:T(8,128)(2,1)}, u32[]{:S(2)}) copy-start(bf16[160,1536]{1,0:T(8,128)(2,1)} %param.29) | copy-start | bytes 1474564
  (21 other events, 22.0 us)
Sparse Core Ops, SparseCore 0:
  10.9 208.2 all-gather.4
  222.2 137.5 all-gather.2
  666.2 135.4 reduce-scatter.6
  809.0 134.7 reduce-scatter.8
  950.1 134.4 reduce-scatter.10
  1091.9 134.7 reduce-scatter.12
  1233.7 347.4 reduce-scatter.14
  1589.4 347.6 reduce-scatter.16
where the time goes:
time: 1950 us; the launch traced here: 1940 us
  waiting for transfers between devices  1430 us (73%)
  blocking collectives  160 us (8%)
  local copies, waits for them, and re-layouts  145 us (7%)
  starting transfers between devices  89 us (5%)
  matrix products  67.3 us (3%)
  other arithmetic  29.2 us (1%)
    reduce_scatter x1, waiting for transfers between devices, per_device(): lax.psum_scatter(contract_grad, 'dp', scatter_dimension=0, tiled=True)  356 us
    reduce_scatter x1, waiting for transfers between devices, per_device(): lax.psum_scatter(expand_grad, 'dp', scatter_dimension=0, tiled=True)  354 us
    unnamed x2, blocking collectives  160 us
    reduce_scatter x1, waiting for transfers between devices, per_device(): lax.psum_scatter(mixing_grad, 'dp', scatter_dimension=0, tiled=True)  142 us
    reduce_scatter x1, waiting for transfers between devices, per_device(): lax.psum_scatter(key_wgrad, 'dp', scatter_dimension=0, tiled=True)  142 us
    reduce_scatter x1, waiting for transfers between devices, per_device(): lax.psum_scatter(value_wgrad, 'dp', scatter_dimension=0, tiled=True)  141 us
    all_to_all x1, waiting for transfers between devices, per_device(): lax.all_to_all(to_slots(result_sensitivity), 'dp', split_axis=0, concat_a...  96.3 us
    all_to_all x1, waiting for transfers between devices, per_device(): lax.all_to_all(as_sent(sent_back.reshape(devices, pair_slots, model_width...  68.9 us
  transfers between devices with their start and end apart: 13, of which 11 were waited for; matrix products, arithmetic and copies ran while one was open for 8% of the time, Pallas kernels for 0%

commit v1 on v0

v1 whole, which is shorter than its diff:
```python
import jax
import jax.numpy as jnp
import numpy as np
from jax import lax
from jax.sharding import PartitionSpec as P

HEAD_DIM = 128
LEVELS = 4
GROUP = 8
EPSILON = 1e-05
NEGATIVE = -1e30
BF = jnp.bfloat16
F32 = jnp.float32


def dot(left, right, dims=((1,), (0,))):
    return lax.dot_general(left, right, (dims, ((), ())), preferred_element_type=F32)


def dot_t(left, right):
    return dot(left, right, ((1,), (1,)))


def t_dot(left, right):
    return dot(left, right, ((0,), (0,)))


def rope_tables(length):
    half = HEAD_DIM // 2
    rates = (10000.0 ** (-(np.arange(half, dtype=np.float64) * 2.0 / HEAD_DIM))).astype(np.float32)
    angles = np.arange(length, dtype=np.float32)[:, None] * rates[None, :]
    return np.cos(angles).astype(np.float32), np.sin(angles).astype(np.float32)


def rotate(values, cosine, sine):
    half = values.shape[-1] // 2
    first, second = values[..., :half], values[..., half:]
    cosine, sine = cosine[:, None, :], sine[:, None, :]
    return jnp.concatenate(
        [first * cosine - second * sine, second * cosine + first * sine], axis=-1
    )


def norm_stats(values):
    center = values - jnp.mean(values, axis=-1, keepdims=True)
    inverse = lax.rsqrt(jnp.mean(center * center, axis=-1, keepdims=True) + EPSILON)
    return center * inverse, inverse


def norm_back(incoming, gain, normal, inverse):
    scaled = incoming * gain
    part = inverse * (
        scaled
        - jnp.mean(scaled, axis=-1, keepdims=True)
        - normal * jnp.mean(scaled * normal, axis=-1, keepdims=True)
    )
    return part, jnp.sum(incoming * normal, axis=0), jnp.sum(incoming, axis=0)


def swap(value, bit):
    count = lax.axis_size("dp")
    return lax.ppermute(value, "dp", [(i, i ^ bit) for i in range(count)])


def hop(value, step, near, far):
    groups = lax.axis_size("dp") // GROUP
    pairs = [
        (z * GROUP + t, (z + step) * GROUP + t)
        for z in range(max(near, 0), min(far, groups))
        if 0 <= z + step < groups
        for t in range(GROUP)
    ]
    return lax.ppermute(value, "dp", pairs)


def sum_all(value):
    bit = 1
    while bit < lax.axis_size("dp"):
        value = value + swap(value, bit)
        bit *= 2
    return value


def plane_gather(own):
    half = own.shape[0] // 2
    slots = [own] + [None] * 7
    slots[2], slots[4], slots[1] = swap(own, 2), swap(own, 4), swap(own, 1)
    slots[6] = jnp.concatenate([swap(slots[2][:half], 4), swap(slots[4][half:], 2)], axis=0)
    for k in (2, 4, 6):
        slots[k + 1] = swap(slots[k], 1)
    return jnp.stack(slots)


def plane_scatter_sum(parts):
    half = parts.shape[1] // 2
    sent = swap(parts[1::2].astype(BF), 1)
    total = [parts[2 * j].astype(F32) + sent[j].astype(F32) for j in range(4)]
    corner = total[3].astype(BF)
    by_x, by_y = swap(corner[:half], 2), swap(corner[half:], 4)
    to_y = jnp.concatenate([total[2][:half] + by_x.astype(F32), total[2][half:]], axis=0)
    to_x = jnp.concatenate([total[1][:half], total[1][half:] + by_y.astype(F32)], axis=0)
    return total[0] + swap(to_x.astype(BF), 2).astype(F32) + swap(to_y.astype(BF), 4).astype(F32)


def plane_exchange(chunks):
    place = lax.axis_index("dp") % GROUP
    got = []
    for k in range(GROUP):
        chunk = lax.dynamic_index_in_dim(chunks, place ^ k, 0, keepdims=False)
        got.append(chunk if k == 0 else swap(chunk, k))
    return jnp.stack(got)


def in_order(slots):
    place = lax.axis_index("dp") % GROUP
    return jnp.take(slots, place ^ jnp.arange(GROUP), axis=0)


def line_gather(own):
    groups = lax.axis_size("dp") // GROUP
    z = lax.axis_index("dp") // GROUP
    up = down = own
    spare = jnp.zeros((groups + 1,) + own.shape, own.dtype)
    found = [(z, own)]
    for s in range(1, groups):
        up = hop(up, 1, s - 1, groups - 1)
        down = hop(down, -1, 1, groups - s + 1)
        found.append((jnp.where(z - s >= 0, z - s, groups), up))
        found.append((jnp.where(z + s < groups, z + s, groups), down))
    for slot, value in found:
        spare = lax.dynamic_update_index_in_dim(spare, value, slot, 0)
    return spare[:groups]


def line_scatter_sum(parts):
    groups = parts.shape[0]
    z = lax.axis_index("dp") // GROUP

    def part(offset):
        slot = jnp.clip(z + offset, 0, groups - 1)
        return lax.dynamic_index_in_dim(parts, slot, 0, keepdims=False).astype(F32)

    up = down = None
    for s in range(1, groups):
        far = groups - s
        up_send, down_send = part(far), part(-far)
        if up is not None:
            up_send, down_send = up_send + up.astype(F32), down_send + down.astype(F32)
        up = hop(up_send.astype(BF), 1, 0, s)
        down = hop(down_send.astype(BF), -1, groups - s, groups)
    return part(0) + up.astype(F32) + down.astype(F32)


def per_device(
    sequence_elements,
    result_sensitivity,
    mixer_gain,
    mixer_offset,
    question_matrix,
    lookup_matrix,
    content_matrix,
    mixer_projection_matrix,
    feedforward_gain,
    feedforward_offset,
    expand_matrix,
    inner_neuron_offset,
    contract_matrix,
    feedforward_result_offset,
    sequence_level_choice,
    servers_per_level,
    accepted_row_limit,
    server_selection,
):
    devices = lax.axis_size("dp")
    me = lax.axis_index("dp")
    groups = devices // GROUP
    z, place = me // GROUP, me % GROUP
    tokens, width = sequence_elements.shape
    heads = width // HEAD_DIM
    rows, feed = expand_matrix.shape
    cols = contract_matrix.shape[0]
    offset_len = feedforward_result_offset.shape[0]
    levels = jnp.arange(LEVELS)

    level = sequence_level_choice[0]
    choice = server_selection.reshape(-1)
    info = jnp.concatenate(
        [
            feedforward_result_offset.astype(F32),
            inner_neuron_offset.astype(F32),
            level.astype(F32)[None],
            jnp.min(choice).astype(F32)[None],
        ]
    )
    info = jnp.pad(info, (0, -info.shape[0] % 128))
    table = sum_all(jnp.where(jnp.arange(devices)[:, None] == me, info[None, :], 0.0))
    result_offset = table[:, :offset_len].reshape(-1)
    hidden_offsets = table[:, offset_len : offset_len + cols]
    all_levels = table[:, offset_len + cols].astype(jnp.int32)
    all_lowest = table[:, offset_len + cols + 1].astype(jnp.int32)

    size = jnp.sum(jnp.where(levels == level, servers_per_level, 0))
    limit = jnp.sum(jnp.where(levels == level, accepted_row_limit, 0))
    server = choice % size
    before = jnp.arange(tokens)[None, :] < jnp.arange(tokens)[:, None]
    local = jnp.sum((before & (server[None, :] == server[:, None])).astype(jnp.int32), axis=1)
    low = all_lowest[None, :]
    seen = (low + tokens - 1 - server[:, None] + size) // size - (low - 1 - server[:, None] + size) // size
    earlier = (jnp.arange(devices) < me) & (all_levels == level)
    arrival = local + jnp.sum(jnp.where(earlier[None, :], seen, 0), axis=1)
    kept = (arrival < limit).astype(F32)[:, None]

    expand_chunks = expand_matrix.reshape(rows, groups, GROUP, cols).transpose(2, 0, 1, 3)
    expand_plane = plane_exchange(expand_chunks.reshape(GROUP, rows, groups * cols))
    expand_plane = in_order(expand_plane).reshape(GROUP * rows, groups * cols)
    first_weight = line_gather(expand_plane).reshape(width, groups * cols)
    second_weight = line_gather(contract_matrix).reshape(groups * cols, width)

    gain_first = mixer_gain.astype(F32)
    gain_second = feedforward_gain.astype(F32)
    values_in = sequence_elements.astype(F32)
    normal_first, inverse_first = norm_stats(values_in)
    normed_first = (normal_first * gain_first + mixer_offset.astype(F32)).astype(BF)
    cosine, sine = rope_tables(tokens)
    scale = HEAD_DIM ** (-0.5)
    shape_heads = (tokens, heads, HEAD_DIM)
    query_rot = rotate(dot(normed_first, question_matrix).reshape(shape_heads), cosine, sine).astype(BF)
    key_rot = rotate(dot(normed_first, lookup_matrix).reshape(shape_heads), cosine, sine).astype(BF)
    value_rows = dot(normed_first, content_matrix).astype(BF).reshape(shape_heads)
    causal = jnp.arange(tokens)[:, None] >= jnp.arange(tokens)[None, :]
    scores = jnp.einsum("lhe,mhe->hlm", query_rot, key_rot, preferred_element_type=F32) * scale
    scores = jnp.where(causal, scores, NEGATIVE)
    weight = jnp.exp(scores - jnp.max(scores, axis=-1, keepdims=True))
    probs = weight / jnp.sum(weight, axis=-1, keepdims=True)
    probs_low = probs.astype(BF)
    context = jnp.einsum("hlm,mhe->lhe", probs_low, value_rows, preferred_element_type=F32)
    context = context.reshape(tokens, width).astype(BF)
    mixed = values_in + dot(context, mixer_projection_matrix)
    normal_second, inverse_second = norm_stats(mixed)
    normed_second = (normal_second * gain_second + feedforward_offset.astype(F32)).astype(BF)

    sensitivity = result_sensitivity.astype(F32)
    kept_sensitivity = (sensitivity * kept).astype(BF)
    group_grad = plane_gather(kept_sensitivity).reshape(GROUP * tokens, width)
    group_rows = plane_gather(normed_second).reshape(GROUP * tokens, width)
    slot_levels = jnp.take(all_levels, z * GROUP + (place ^ jnp.arange(GROUP)))
    starts = (jnp.arange(groups) * GROUP + place) * cols
    active_block = starts[None, :] < (feed // 8) * (1 << slot_levels[:, None])
    mask = jnp.broadcast_to(
        active_block[:, None, :, None], (GROUP, tokens, groups, cols)
    ).reshape(GROUP * tokens, groups * cols)
    hidden_offset = lax.dynamic_index_in_dim(
        hidden_offsets.reshape(groups, GROUP, cols), place, 1, keepdims=False
    ).reshape(-1)
    hidden = dot(group_rows, first_weight) + hidden_offset
    inner = 0.7978845608 * (hidden + 0.044715 * hidden * hidden * hidden)
    bent = jnp.tanh(inner)
    active = jnp.where(mask, 0.5 * hidden * (1.0 + bent), 0.0).astype(BF)
    slope = 0.5 * (1.0 + bent) + 0.5 * hidden * (1.0 - bent * bent) * 0.7978845608 * (
        1.0 + 3.0 * 0.044715 * hidden * hidden
    )
    active_grad = dot_t(group_grad, second_weight)
    hidden_grad = jnp.where(mask, active_grad * slope, 0.0).astype(BF)
    second_parts = dot_t(hidden_grad, first_weight).reshape(GROUP, tokens, width)
    second_grad = plane_scatter_sum(second_parts).astype(BF).astype(F32)
    branch_parts = dot(active, second_weight).reshape(GROUP, tokens, width)
    branch = (plane_scatter_sum(branch_parts) + result_offset).astype(BF).astype(F32)
    layer_output = (mixed + kept * branch).astype(BF)
    contract_part = t_dot(active, group_grad).reshape(groups, cols, width)
    share_contract = line_scatter_sum(contract_part)
    expand_part = t_dot(group_rows, hidden_grad).reshape(groups, GROUP * rows, groups * cols)
    expand_rows = line_scatter_sum(expand_part)
    hidden_sum = jnp.sum(hidden_grad.astype(F32), axis=0)

    def rows_home(summed):
        swapped = plane_exchange(summed.astype(BF).reshape(GROUP, rows, groups * cols))
        return in_order(swapped).astype(F32)

    share_expand = (
        rows_home(expand_rows)
        .reshape(GROUP, rows, groups, cols)
        .transpose(1, 2, 0, 3)
        .reshape(rows, feed)
    )

    mixed_part, midnorm_sum, midshift_sum = norm_back(second_grad, gain_second, normal_second, inverse_second)
    mixed_grad = sensitivity + mixed_part
    mixed_low = mixed_grad.astype(BF)
    context_grad = dot_t(mixed_low, mixer_projection_matrix).astype(BF).reshape(shape_heads)
    value_grad = jnp.einsum("hlm,lhe->mhe", probs_low, context_grad, preferred_element_type=F32)
    value_grad = value_grad.astype(BF).reshape(tokens, width)
    probs_grad = jnp.einsum("lhe,mhe->hlm", context_grad, value_rows, preferred_element_type=F32)
    scores_grad = (probs * (probs_grad - jnp.sum(probs_grad * probs, axis=-1, keepdims=True))).astype(BF)
    query_turned = jnp.einsum("hlm,mhe->lhe", scores_grad, key_rot, preferred_element_type=F32) * scale
    key_turned = jnp.einsum("hlm,lhe->mhe", scores_grad, query_rot, preferred_element_type=F32) * scale
    query_grad = rotate(query_turned, cosine, -sine).astype(BF).reshape(tokens, width)
    key_grad = rotate(key_turned, cosine, -sine).astype(BF).reshape(tokens, width)
    leading = dot_t(query_grad, question_matrix) + dot_t(key_grad, lookup_matrix) + dot_t(value_grad, content_matrix)
    input_part, leadnorm_sum, leadshift_sum = norm_back(leading, gain_first, normal_first, inverse_first)
    layer_input_gradient = (mixed_grad + input_part).astype(BF)

    share = width // GROUP
    group_first = plane_gather(normed_first).reshape(GROUP * tokens, width)
    group_context = plane_gather(context).reshape(GROUP * tokens, width)

    def split_columns(grad):
        chunks = grad.reshape(tokens, GROUP, share).transpose(1, 0, 2)
        return plane_exchange(chunks).reshape(GROUP * tokens, share)

    weight_parts = jnp.concatenate(
        [
            t_dot(group_context, split_columns(mixed_low)),
            t_dot(group_first, split_columns(value_grad)),
            t_dot(group_first, split_columns(key_grad)),
            t_dot(group_first, split_columns(query_grad)),
        ],
        axis=1,
    )
    weight_rows = line_scatter_sum(weight_parts.reshape(groups, GROUP * rows, 4 * share))
    swapped = plane_exchange(weight_rows.astype(BF).reshape(GROUP, rows, 4 * share))
    weight_home = (
        in_order(swapped)
        .astype(F32)
        .reshape(GROUP, rows, 4, share)
        .transpose(2, 1, 0, 3)
        .reshape(4, rows, width)
    )
    share_mixing, share_value, share_key, share_query = (weight_home[i] for i in range(4))

    hidden_spot = (jnp.arange(GROUP)[None, :, None] == place).astype(F32)
    hidden_full = (hidden_spot * hidden_sum.reshape(groups, 1, cols)).reshape(-1)
    result_sum = jnp.sum(kept_sensitivity.astype(F32), axis=0)
    vectors = sum_all(
        jnp.concatenate(
            [midnorm_sum, midshift_sum, leadnorm_sum, leadshift_sum, result_sum, hidden_full]
        ).reshape(-1, 128)
    ).reshape(-1)
    small = vectors[: 5 * width].reshape(5, devices, width // devices)
    small = lax.dynamic_index_in_dim(small, me, 1, keepdims=False)
    share_hidden = lax.dynamic_slice_in_dim(vectors, 5 * width + me * cols, cols)
    return (
        layer_output,
        layer_input_gradient,
        small[2],
        small[3],
        share_query,
        share_key,
        share_value,
        share_mixing,
        small[0],
        small[1],
        share_expand,
        share_hidden,
        share_contract,
        small[4],
    )


def solution(mesh):
    split, line, whole = P("dp", None), P("dp"), P()
    return jax.shard_map(
        per_device,
        mesh=mesh,
        in_specs=(split, split) + (whole,) * 8 + (split, line, split, line, line, whole, whole, split),
        out_specs=(split, split, line, line, split, split, split, split, line, line, split, line, split, line),
        check_vma=False,
    )
```

time: 1950 us -> 712 us (0.37)
  waiting for transfers between devices: 1430 us -> 218 us
  blocking collectives: 160 us -> 0 us
  starting transfers between devices: 89 us -> 152 us
  local copies, waits for them, and re-layouts: 145 us -> 191 us
  other arithmetic: 29.2 us -> 62.6 us
    reduce_scatter x6 -> x0, waiting for transfers between devices: 1150 us -> none  [the longest x1 356 us: per_device(): lax.psum_scatter(contract_grad, 'dp', scatter_dimension=0, tiled=True)]
    all_to_all x5 -> x0, waiting for transfers between devices: 228 us -> none  [the longest x1 96.3 us: per_device(): lax.all_to_all(to_slots(result_sensitivity), 'dp', split_axis=0, concat_a...]
    ppermute x0 -> x131, waiting for transfers between devices: none -> 218 us  [the longest x101 171 us: swap(): return lax.ppermute(value, 'dp', [(i, i ^ bit) for i in range(count)])]
    unnamed x2 -> x0, blocking collectives: 160 us -> none
    ppermute x0 -> x131, starting transfers between devices: none -> 152 us  [the longest x101 84.9 us: swap(): return lax.ppermute(value, 'dp', [(i, i ^ bit) for i in range(count)])]
    all_to_all x5 -> x0, starting transfers between devices: 88.2 us -> none  [the longest x1 67.3 us: per_device(): lax.all_to_all(as_sent(sent_back.reshape(devices, pair_slots, model_width...]
    all_gather x2 -> x0, waiting for transfers between devices: 49.9 us -> none  [the longest x1 49.9 us: per_device(): lax.all_gather(expand_matrix, 'dp', axis=0, tiled=True)]
    dynamic_slice x0 -> x9, local copies, waits for them, and re-layouts: none -> 43.8 us  [the longest x7 43.1 us: part(): return lax.dynamic_index_in_dim(parts, slot, 0, keepdims=False).astype(F32)]
  transfers between devices with their start and end apart: 13 -> 131, of which waited for: 11 -> 52; matrix products, arithmetic and copies ran while one was open for 8% -> 39% of each run, Pallas kernels for 0% -> 0%
where the time goes in v1:
time: 712 us; the launch traced here: 703 us
  waiting for transfers between devices  218 us (31%)
  local copies, waits for them, and re-layouts  191 us (27%)
  starting transfers between devices  152 us (21%)
  matrix products  72.9 us (10%)
  other arithmetic  62.6 us (9%)
    ppermute x101, waiting for transfers between devices, swap(): return lax.ppermute(value, 'dp', [(i, i ^ bit) for i in range(count)])  171 us
    ppermute x101, starting transfers between devices, swap(): return lax.ppermute(value, 'dp', [(i, i ^ bit) for i in range(count)])  84.9 us
    ppermute x30, starting transfers between devices, hop(): return lax.ppermute(value, 'dp', pairs)  66.7 us
    dot_general x18, matrix products, dot(): lax.dot_general(left, right, (dims, ((), ())), preferred_element_type=F32)  64.5 us
    unnamed x271, local copies, waits for them, and re-layouts  48.4 us
    ppermute x30, waiting for transfers between devices, hop(): return lax.ppermute(value, 'dp', pairs)  47.6 us
    dynamic_slice x7, local copies, waits for them, and re-layouts, part(): return lax.dynamic_index_in_dim(parts, slot, 0, keepdims=False).astype(F32)  43.1 us
    dynamic_update_slice x14, local copies, waits for them, and re-layouts, line_gather(): spare = lax.dynamic_update_index_in_dim(spare, value, slot, 0)  17.4 us
  transfers between devices with their start and end apart: 131, of which 52 were waited for; matrix products, arithmetic and copies ran while one was open for 39% of the time, Pallas kernels for 0%

profile of v1, /device:TPU:0, one launch (start us, length us, event | category | flops | bytes accessed | tf_op | source)
XLA Modules:
  0.0 703.2 jit_solution(40211673456663448)
XLA Ops:
  18.8 4.3 collective-permute-start.26
  28.9 4.2 fusion.14
  34.2 4.2 fusion.125
  48.3 3.4 fusion.122
  87.8 3.9 collective-permute-done.19
  114.4 4.2 reshape.462
  130.9 8.8 %collective-permute-done.6 = bf16[160,1536]{1,0:T(8,128)(2,1)S(1)} collective-permute-done((bf16[160,1536]{1,0:T(8,128)(2,1)S(1)}, bf16[160,1536]{1,0:T(8,128)(2,1)S(1)}, u32[]{:S(2)}, u32[]{:S(2)}) %collective-permute-start.6) | collective-permute-done | bytes 491552 | tf_op jit(solution)/shard_map/ppermute | solution.py:62
  146.1 6.0 collective-permute-start.20
  161.6 4.8 collective-permute-done.40
  167.6 4.5 collective-permute-done.38
  189.8 4.9 collective-permute-done.42
  194.7 5.6 collective-permute-start.59
  224.2 6.2 copy.180
  243.7 12.7 %collective-permute-done.31 = bf16[192,1536]{1,0:T(8,128)(2,1)S(1)} collective-permute-done((bf16[192,1536]{1,0:T(8,128)(2,1)}, bf16[192,1536]{1,0:T(8,128)(2,1)S(1)}, u32[]{:S(2)}, u32[]{:S(2)}) %collective-permute-start.31) | collective-permute-done | bytes 589856 | tf_op jit(solution)/shard_map/ppermute | solution.py:73
  260.0 8.6 %collective-permute-done.25 = bf16[384,768]{1,0:T(8,128)(2,1)S(1)} collective-permute-done((bf16[384,768]{1,0:T(8,128)(2,1)}, bf16[384,768]{1,0:T(8,128)(2,1)S(1)}, u32[]{:S(2)}, u32[]{:S(2)}) %collective-permute-start.25) | collective-permute-done | bytes 589856 | tf_op jit(solution)/shard_map/ppermute | solution.py:73
  271.4 7.1 %select_convert_fusion.1 = (bf16[1280,768]{0,1:T(8,128)(2,1)S(1)}, f32[1280,768]{0,1:T(8,128)S(1)}) fusion(pred[1280,768]{0,1:T(32,128)(4,1)S(1)} %copy-done.26, f32[768]{0:T(1024)S(1)} %copy-done.71, bf16[1280,1536]{1,0:T(8,128)(2,1)} %bitcast.15, bf16[1536,768]{1,0:T(8,128)(2,1)S(1)} %bitcast.619), kind=kOutput, calls=%fused_computation.16 | convolution fusion | flops 3030712320 | bytes 13175808 | tf_op jit(solution)/shard_map/dot_general | solution.py:17
  278.5 5.6 convert_reduce_fusion
  297.2 5.7 collective-permute-done.112
  303.0 4.4 collective-permute-start.113
  307.4 8.1 %collective-permute-done.125 = bf16[192,1536]{1,0:T(8,128)(2,1)S(1)} collective-permute-done((bf16[192,1536]{1,0:T(8,128)(2,1)S(1)}, bf16[192,1536]{1,0:T(8,128)(2,1)S(1)}, u32[]{:S(2)}, u32[]{:S(2)}) %collective-permute-start.125) | collective-permute-done | bytes 589856 | tf_op jit(solution)/shard_map/ppermute | solution.py:73
  315.6 4.6 collective-permute-start.126
  320.2 5.6 fusion.123
  330.9 8.6 %collective-permute-done.126 = bf16[192,1536]{1,0:T(8,128)(2,1)S(1)} collective-permute-done((bf16[192,1536]{1,0:T(8,128)(2,1)S(1)}, bf16[192,1536]{1,0:T(8,128)(2,1)S(1)}, u32[]{:S(2)}, u32[]{:S(2)}) %collective-permute-start.126) | collective-permute-done | bytes 589856 | tf_op jit(solution)/shard_map/ppermute | solution.py:73
  342.4 6.1 fusion.124
  352.2 4.2 collective-permute-start.114
  356.5 4.6 collective-permute-start.127
  373.5 3.6 collective-permute-done.46
  378.6 5.4 collective-permute-done.48
  385.6 4.7 collective-permute-done.33
  392.6 3.9 collective-permute-done.35
  407.8 13.1 %collective-permute-done.119 = bf16[48,768]{1,0:T(8,128)(2,1)S(1)} collective-permute-done((bf16[48,768]{1,0:T(8,128)(2,1)S(1)}, bf16[48,768]{1,0:T(8,128)(2,1)S(1)}, u32[]{:S(2)}, u32[]{:S(2)}) %collective-permute-start.119) | collective-permute-done | bytes 73760 | tf_op jit(solution)/shard_map/ppermute | solution.py:62
  421.0 4.5 collective-permute-done.120
  426.1 3.8 collective-permute-done.121
  429.9 3.8 collective-permute-done.122
  435.1 3.8 collective-permute-done.123
  438.9 4.6 collective-permute-done.124
  447.9 3.4 fusion.114
  451.3 4.0 fusion.15
  486.3 4.4 convolution_add_fusion.2
  490.7 5.7 fusion.46
  514.5 4.6 collective-permute-done.94
  519.8 3.7 collective-permute-done.95
  523.6 4.0 collective-permute-done.96
  529.0 3.9 collective-permute-done.97
  532.9 4.8 collective-permute-done.98
  540.3 3.3 collective-permute-done.86
  544.1 4.2 collective-permute-done.87
  549.4 3.3 collective-permute-done.88
  552.7 4.4 collective-permute-done.89
  558.6 3.9 collective-permute-done.90
  562.5 4.8 collective-permute-done.91
  579.6 6.2 reshape.478
  585.7 6.9 constant_dynamic-slice_fusion.7
  592.7 3.4 copy.225
  599.9 5.1 collective-permute-start.99
  605.1 15.7 %constant_dynamic-slice_fusion.8 = (f32[1,384,768]{1,0,2:T(1,128)}, f32[1,384,768]{1,0,2:T(1,128)}, f32[1,384,768]{1,0,2:T(1,128)}, f32[1,384,768]{1,0,2:T(1,128)}, f32[1,384,768]{1,0,2:T(1,128)S(1)}) fusion(f32[4,384,768]{1,0,2:T(4,128)} %reshape.478, s32[]{:T(128)S(6)} %min.38, s32[]{:T(128)S(6)} %min.41, s32[]{:T(128)S(6)} %min.40, s32[]{:T(128)S(6)} %min.37, ...), kind=kLoop, calls=%fused_computation.389 | loop fusion | bytes 11796500 | tf_op jit(solution)/shard_map/jit(dynamic_index_in_dim)/dynamic_slice | solution.py:141
  620.8 4.7 copy.171
  625.5 4.7 copy.174
  639.1 4.7 copy.173
  643.8 4.8 copy.170
  655.6 5.6 collective-permute-start.101
  665.9 6.8 collective-permute-done.54
  680.7 3.9 collective-permute-done.106
  684.7 4.4 collective-permute-done.107
  (697 shorter events, 355.4 us)
Async XLA Ops:
  6.6 116.0 %collective-permute-start.71 = (bf16[160,1536]{1,0:T(8,128)(2,1)S(1)}, bf16[160,1536]{1,0:T(8,128)(2,1)}, u32[]{:S(2)}, u32[]{:S(2)}) collective-permute-start(bf16[160,1536]{1,0:T(8,128)(2,1)S(1)} %get-tuple-element.27), channel_id=1, source_target_pairs={{0,2},{1,3},{2,0},{3,1},{4,6},{5,7},{6,4},{7,5},{8,10},{9,11},{10,... | collective-permute-start | bytes 1474568 | tf_op jit(solution)/shard_map/ppermute | solution.py:62
  9.6 111.2 %collective-permute-start.70 = (bf16[160,1536]{1,0:T(8,128)(2,1)S(1)}, bf16[160,1536]{1,0:T(8,128)(2,1)}, u32[]{:S(2)}, u32[]{:S(2)}) collective-permute-start(bf16[160,1536]{1,0:T(8,128)(2,1)S(1)} %get-tuple-element.27), channel_id=1, source_target_pairs={{0,1},{1,0},{2,3},{3,2},{4,5},{5,4},{6,7},{7,6},{8,9},{9,8},{10,11... | collective-permute-start | bytes 1474568 | tf_op jit(solution)/shard_map/ppermute | solution.py:62
  9.6 134.3 %collective-permute-start.73 = (bf16[160,1536]{1,0:T(8,128)(2,1)S(1)}, bf16[160,1536]{1,0:T(8,128)(2,1)}, u32[]{:S(2)}, u32[]{:S(2)}) collective-permute-start(bf16[160,1536]{1,0:T(8,128)(2,1)S(1)} %get-tuple-element.27), channel_id=1, source_target_pairs={{0,4},{1,5},{2,6},{3,7},{4,0},{5,1},{6,2},{7,3},{8,12},{9,13},{10,... | collective-permute-start | bytes 1474568 | tf_op jit(solution)/shard_map/ppermute | solution.py:62
  18.6 41.2 %collective-permute-start = (f32[32,256]{1,0:T(8,128)}, f32[32,256]{1,0:T(8,128)S(1)}, u32[]{:S(2)}, u32[]{:S(2)}) collective-permute-start(f32[32,256]{1,0:T(8,128)} %broadcast_select_fusion.1), channel_id=1, source_target_pairs={{0,1},{1,0},{2,3},{3,2},{4,5},{5,4},{6,7},{7,6},{8,9},{9,8},{10,11... | collective-permute-start | bytes 98312 | tf_op jit(solution)/shard_map/ppermute | solution.py:62
  18.8 134.7 %collective-permute-start.26 = (bf16[192,1536]{1,0:T(8,128)(2,1)}, bf16[192,1536]{1,0:T(8,128)(2,1)}, u32[]{:S(2)}, u32[]{:S(2)}) collective-permute-start(bf16[192,1536]{1,0:T(8,128)(2,1)} %param.40), channel_id=1, source_target_pairs={{0,8},{1,9},{2,10},{3,11},{4,12},{5,13},{6,14},{7,15},{8,16},{9,17... | collective-permute-start | bytes 1769480 | tf_op jit(solution)/shard_map/ppermute | solution.py:73
  104.4 21.9 %collective-permute-start.56 = (bf16[160,1536]{1,0:T(8,128)(2,1)}, bf16[160,1536]{1,0:T(8,128)(2,1)}, u32[]{:S(2)}, u32[]{:S(2)}) collective-permute-start(bf16[160,1536]{1,0:T(8,128)(2,1)} %copy_bitcast_fusion.2), channel_id=1, source_target_pairs={{0,2},{1,3},{2,0},{3,1},{4,6},{5,7},{6,4},{7,5},{8,10},{9,11},{10,... | collective-permute-start | bytes 1474568 | tf_op jit(solution)/shard_map/ppermute | solution.py:62
  122.6 23.5 %collective-permute-start.58 = (bf16[160,1536]{1,0:T(8,128)(2,1)}, bf16[160,1536]{1,0:T(8,128)(2,1)S(1)}, u32[]{:S(2)}, u32[]{:S(2)}) collective-permute-start(bf16[160,1536]{1,0:T(8,128)(2,1)} %copy_bitcast_fusion.2), channel_id=1, source_target_pairs={{0,4},{1,5},{2,6},{3,7},{4,0},{5,1},{6,2},{7,3},{8,12},{9,13},{10,... | collective-permute-start | bytes 1474568 | tf_op jit(solution)/shard_map/ppermute | solution.py:62
  129.3 22.9 %collective-permute-start.8 = (bf16[160,1536]{1,0:T(8,128)(2,1)S(1)}, bf16[160,1536]{1,0:T(8,128)(2,1)S(1)}, u32[]{:S(2)}, u32[]{:S(2)}) collective-permute-start(bf16[160,1536]{1,0:T(8,128)(2,1)S(1)} %copy-done.30), channel_id=1, source_target_pairs={{0,4},{1,5},{2,6},{3,7},{4,0},{5,1},{6,2},{7,3},{8,12},{9,13},{10,... | collective-permute-start | bytes 1474568 | tf_op jit(solution)/shard_map/ppermute | solution.py:62
  139.8 18.1 %collective-permute-start.27 = (bf16[192,1536]{1,0:T(8,128)(2,1)S(1)}, bf16[192,1536]{1,0:T(8,128)(2,1)S(1)}, u32[]{:S(2)}, u32[]{:S(2)}) collective-permute-start(bf16[192,1536]{1,0:T(8,128)(2,1)S(1)} %copy-done.27), channel_id=1, source_target_pairs={{8,0},{9,1},{10,2},{11,3},{12,4},{13,5},{14,6},{15,7},{16,8},{17,9... | collective-permute-start | bytes 1769480 | tf_op jit(solution)/shard_map/ppermute | solution.py:73
  143.9 33.0 %collective-permute-start.21 = (bf16[384,768]{1,0:T(8,128)(2,1)S(1)}, bf16[384,768]{1,0:T(8,128)(2,1)S(1)}, u32[]{:S(2)}, u32[]{:S(2)}) collective-permute-start(bf16[384,768]{1,0:T(8,128)(2,1)S(1)} %bitcast.622), channel_id=1, source_target_pairs={{8,0},{9,1},{10,2},{11,3},{12,4},{13,5},{14,6},{15,7},{16,8},{17,9... | collective-permute-start | bytes 1769480 | tf_op jit(solution)/shard_map/ppermute | solution.py:73
  146.1 28.0 %collective-permute-start.20 = (bf16[384,768]{1,0:T(8,128)(2,1)S(1)}, bf16[384,768]{1,0:T(8,128)(2,1)}, u32[]{:S(2)}, u32[]{:S(2)}) collective-permute-start(bf16[384,768]{1,0:T(8,128)(2,1)S(1)} %bitcast.623), channel_id=1, source_target_pairs={{0,8},{1,9},{2,10},{3,11},{4,12},{5,13},{6,14},{7,15},{8,16},{9,17... | collective-permute-start | bytes 1769480 | tf_op jit(solution)/shard_map/ppermute | solution.py:73
  152.2 14.2 %collective-permute-start.40 = (bf16[160,1536]{1,0:T(8,128)(2,1)S(1)}, bf16[160,1536]{1,0:T(8,128)(2,1)S(1)}, u32[]{:S(2)}, u32[]{:S(2)}) collective-permute-start(bf16[160,1536]{1,0:T(8,128)(2,1)S(1)} %copy-done.21), channel_id=1, source_target_pairs={{0,4},{1,5},{2,6},{3,7},{4,0},{5,1},{6,2},{7,3},{8,12},{9,13},{10,... | collective-permute-start | bytes 1474568 | tf_op jit(solution)/shard_map/ppermute | solution.py:62
  157.9 14.2 %collective-permute-start.38 = (bf16[160,1536]{1,0:T(8,128)(2,1)S(1)}, bf16[160,1536]{1,0:T(8,128)(2,1)S(1)}, u32[]{:S(2)}, u32[]{:S(2)}) collective-permute-start(bf16[160,1536]{1,0:T(8,128)(2,1)S(1)} %copy-done.21), channel_id=1, source_target_pairs={{0,2},{1,3},{2,0},{3,1},{4,6},{5,7},{6,4},{7,5},{8,10},{9,11},{10,... | collective-permute-start | bytes 1474568 | tf_op jit(solution)/shard_map/ppermute | solution.py:62
  159.9 19.0 %collective-permute-start.75 = (bf16[80,1536]{1,0:T(8,128)(2,1)S(1)}, bf16[80,1536]{1,0:T(8,128)(2,1)S(1)}, u32[]{:S(2)}, u32[]{:S(2)}) collective-permute-start(bf16[80,1536]{1,0:T(8,128)(2,1)S(1)} %slice.329), channel_id=1, source_target_pairs={{0,4},{1,5},{2,6},{3,7},{4,0},{5,1},{6,2},{7,3},{8,12},{9,13},{10,... | collective-permute-start | bytes 737288 | tf_op jit(solution)/shard_map/ppermute | solution.py:62
  166.4 19.6 %collective-permute-start.76 = (bf16[80,1536]{1,0:T(8,128)(2,1)S(1)}, bf16[80,1536]{1,0:T(8,128)(2,1)S(1)}, u32[]{:S(2)}, u32[]{:S(2)}) collective-permute-start(bf16[80,1536]{1,0:T(8,128)(2,1)S(1)} %slice.330), channel_id=1, source_target_pairs={{0,2},{1,3},{2,0},{3,1},{4,6},{5,7},{6,4},{7,5},{8,10},{9,11},{10,... | collective-permute-start | bytes 737288 | tf_op jit(solution)/shard_map/ppermute | solution.py:62
  179.8 20.9 %collective-permute-start.72 = (bf16[160,1536]{1,0:T(8,128)(2,1)}, bf16[160,1536]{1,0:T(8,128)(2,1)S(1)}, u32[]{:S(2)}, u32[]{:S(2)}) collective-permute-start(bf16[160,1536]{1,0:T(8,128)(2,1)} %collective-permute-done.71), channel_id=1, source_target_pairs={{0,1},{1,0},{2,3},{3,2},{4,5},{5,4},{6,7},{7,6},{8,9},{9,8},{10,11... | collective-permute-start | bytes 1474568 | tf_op jit(solution)/shard_map/ppermute | solution.py:62
  183.0 20.7 %collective-permute-start.74 = (bf16[160,1536]{1,0:T(8,128)(2,1)}, bf16[160,1536]{1,0:T(8,128)(2,1)S(1)}, u32[]{:S(2)}, u32[]{:S(2)}) collective-permute-start(bf16[160,1536]{1,0:T(8,128)(2,1)} %collective-permute-done.73), channel_id=1, source_target_pairs={{0,1},{1,0},{2,3},{3,2},{4,5},{5,4},{6,7},{7,6},{8,9},{9,8},{10,11... | collective-permute-start | bytes 1474568 | tf_op jit(solution)/shard_map/ppermute | solution.py:62
  186.0 20.6 %collective-permute-start.57 = (bf16[160,1536]{1,0:T(8,128)(2,1)}, bf16[160,1536]{1,0:T(8,128)(2,1)S(1)}, u32[]{:S(2)}, u32[]{:S(2)}) collective-permute-start(bf16[160,1536]{1,0:T(8,128)(2,1)} %collective-permute-done.56), channel_id=1, source_target_pairs={{0,1},{1,0},{2,3},{3,2},{4,5},{5,4},{6,7},{7,6},{8,9},{9,8},{10,11... | collective-permute-start | bytes 1474568 | tf_op jit(solution)/shard_map/ppermute | solution.py:62
  194.7 14.2 %collective-permute-start.59 = (bf16[160,1536]{1,0:T(8,128)(2,1)S(1)}, bf16[160,1536]{1,0:T(8,128)(2,1)S(1)}, u32[]{:S(2)}, u32[]{:S(2)}) collective-permute-start(bf16[160,1536]{1,0:T(8,128)(2,1)S(1)} %collective-permute-done.58), channel_id=1, source_target_pairs={{0,1},{1,0},{2,3},{3,2},{4,5},{5,4},{6,7},{7,6},{8,9},{9,8},{10,11... | collective-permute-start | bytes 1474568 | tf_op jit(solution)/shard_map/ppermute | solution.py:62
  203.7 18.3 %collective-permute-start.29 = (bf16[192,1536]{1,0:T(8,128)(2,1)S(1)}, bf16[192,1536]{1,0:T(8,128)(2,1)S(1)}, u32[]{:S(2)}, u32[]{:S(2)}) collective-permute-start(bf16[192,1536]{1,0:T(8,128)(2,1)S(1)} %collective-permute-done.27), channel_id=1, source_target_pairs={{8,0},{9,1},{10,2},{11,3},{12,4},{13,5},{14,6},{15,7},{16,8},{17,9... | collective-permute-start | bytes 1769480 | tf_op jit(solution)/shard_map/ppermute | solution.py:73
  206.6 14.4 %collective-permute-start.28 = (bf16[192,1536]{1,0:T(8,128)(2,1)}, bf16[192,1536]{1,0:T(8,128)(2,1)S(1)}, u32[]{:S(2)}, u32[]{:S(2)}) collective-permute-start(bf16[192,1536]{1,0:T(8,128)(2,1)} %collective-permute-done.26), channel_id=1, source_target_pairs={{8,16},{9,17},{10,18},{11,19},{12,20},{13,21},{14,22},{15,23},{16,... | collective-permute-start | bytes 1769480 | tf_op jit(solution)/shard_map/ppermute | solution.py:73
  212.7 21.3 %collective-permute-start.23 = (bf16[384,768]{1,0:T(8,128)(2,1)S(1)}, bf16[384,768]{1,0:T(8,128)(2,1)}, u32[]{:S(2)}, u32[]{:S(2)}) collective-permute-start(bf16[384,768]{1,0:T(8,128)(2,1)S(1)} %collective-permute-done.21), channel_id=1, source_target_pairs={{8,0},{9,1},{10,2},{11,3},{12,4},{13,5},{14,6},{15,7},{16,8},{17,9... | collective-permute-start | bytes 1769480 | tf_op jit(solution)/shard_map/ppermute | solution.py:73
  215.7 19.1 %collective-permute-start.22 = (bf16[384,768]{1,0:T(8,128)(2,1)}, bf16[384,768]{1,0:T(8,128)(2,1)}, u32[]{:S(2)}, u32[]{:S(2)}) collective-permute-start(bf16[384,768]{1,0:T(8,128)(2,1)} %collective-permute-done.20), channel_id=1, source_target_pairs={{8,16},{9,17},{10,18},{11,19},{12,20},{13,21},{14,22},{15,23},{16,... | collective-permute-start | bytes 1769480 | tf_op jit(solution)/shard_map/ppermute | solution.py:73
  222.0 71.9 %collective-permute-start.62 = (bf16[160,1536]{1,0:T(8,128)(2,1)S(1)}, bf16[160,1536]{1,0:T(8,128)(2,1)}, u32[]{:S(2)}, u32[]{:S(2)}) collective-permute-start(bf16[160,1536]{1,0:T(8,128)(2,1)S(1)} %constant_dynamic-update-slice_fusion.13), channel_id=1, source_target_pairs={{0,1},{1,0},{2,3},{3,2},{4,5},{5,4},{6,7},{7,6},{8,9},{9,8},{10,11... | collective-permute-start | bytes 1474568 | tf_op jit(solution)/shard_map/ppermute | solution.py:62
  223.2 16.7 %collective-permute-start.44 = (bf16[160,1536]{1,0:T(8,128)(2,1)S(1)}, bf16[160,1536]{1,0:T(8,128)(2,1)}, u32[]{:S(2)}, u32[]{:S(2)}) collective-permute-start(bf16[160,1536]{1,0:T(8,128)(2,1)S(1)} %constant_dynamic-update-slice_fusion.10), channel_id=1, source_target_pairs={{0,1},{1,0},{2,3},{3,2},{4,5},{5,4},{6,7},{7,6},{8,9},{9,8},{10,11... | collective-permute-start | bytes 1474568 | tf_op jit(solution)/shard_map/ppermute | solution.py:62
  230.3 26.1 %collective-permute-start.31 = (bf16[192,1536]{1,0:T(8,128)(2,1)}, bf16[192,1536]{1,0:T(8,128)(2,1)S(1)}, u32[]{:S(2)}, u32[]{:S(2)}) collective-permute-start(bf16[192,1536]{1,0:T(8,128)(2,1)} %copy-done.28), channel_id=1, source_target_pairs={{8,0},{9,1},{10,2},{11,3},{12,4},{13,5},{14,6},{15,7}} | collective-permute-start | bytes 1769480 | tf_op jit(solution)/shard_map/ppermute | solution.py:73
  234.8 33.9 %collective-permute-start.25 = (bf16[384,768]{1,0:T(8,128)(2,1)}, bf16[384,768]{1,0:T(8,128)(2,1)S(1)}, u32[]{:S(2)}, u32[]{:S(2)}) collective-permute-start(bf16[384,768]{1,0:T(8,128)(2,1)} %collective-permute-done.23), channel_id=1, source_target_pairs={{8,0},{9,1},{10,2},{11,3},{12,4},{13,5},{14,6},{15,7}} | collective-permute-start | bytes 1769480 | tf_op jit(solution)/shard_map/ppermute | solution.py:73
  239.9 19.2 %collective-permute-start.24 = (bf16[384,768]{1,0:T(8,128)(2,1)}, bf16[384,768]{1,0:T(8,128)(2,1)S(1)}, u32[]{:S(2)}, u32[]{:S(2)}) collective-permute-start(bf16[384,768]{1,0:T(8,128)(2,1)} %collective-permute-done.22), channel_id=1, source_target_pairs={{16,24},{17,25},{18,26},{19,27},{20,28},{21,29},{22,30},{23,31}} | collective-permute-start | bytes 1769480 | tf_op jit(solution)/shard_map/ppermute | solution.py:73
  287.6 15.3 %collective-permute-start.112 = (bf16[384,768]{1,0:T(8,128)(2,1)S(1)}, bf16[384,768]{1,0:T(8,128)(2,1)S(1)}, u32[]{:S(2)}, u32[]{:S(2)}) collective-permute-start(bf16[384,768]{1,0:T(8,128)(2,1)S(1)} %get-tuple-element.47), channel_id=1, source_target_pairs={{0,8},{1,9},{2,10},{3,11},{4,12},{5,13},{6,14},{7,15}} | collective-permute-start | bytes 1769480 | tf_op jit(solution)/shard_map/ppermute | solution.py:73
  292.5 23.0 %collective-permute-start.125 = (bf16[192,1536]{1,0:T(8,128)(2,1)S(1)}, bf16[192,1536]{1,0:T(8,128)(2,1)S(1)}, u32[]{:S(2)}, u32[]{:S(2)}) collective-permute-start(bf16[192,1536]{1,0:T(8,128)(2,1)S(1)} %get-tuple-element.43), channel_id=1, source_target_pairs={{0,8},{1,9},{2,10},{3,11},{4,12},{5,13},{6,14},{7,15}} | collective-permute-start | bytes 1769480 | tf_op jit(solution)/shard_map/ppermute | solution.py:73
  295.8 31.4 %collective-permute-start.115 = (bf16[384,768]{1,0:T(8,128)(2,1)S(1)}, bf16[384,768]{1,0:T(8,128)(2,1)S(1)}, u32[]{:S(2)}, u32[]{:S(2)}) collective-permute-start(bf16[384,768]{1,0:T(8,128)(2,1)S(1)} %get-tuple-element.48), channel_id=1, source_target_pairs={{24,16},{25,17},{26,18},{27,19},{28,20},{29,21},{30,22},{31,23}} | collective-permute-start | bytes 1769480 | tf_op jit(solution)/shard_map/ppermute | solution.py:73
  296.5 34.4 %collective-permute-start.128 = (bf16[192,1536]{1,0:T(8,128)(2,1)S(1)}, bf16[192,1536]{1,0:T(8,128)(2,1)S(1)}, u32[]{:S(2)}, u32[]{:S(2)}) collective-permute-start(bf16[192,1536]{1,0:T(8,128)(2,1)S(1)} %get-tuple-element.44), channel_id=1, source_target_pairs={{24,16},{25,17},{26,18},{27,19},{28,20},{29,21},{30,22},{31,23}} | collective-permute-start | bytes 1769480 | tf_op jit(solution)/shard_map/ppermute | solution.py:73
  303.0 25.1 %collective-permute-start.113 = (bf16[384,768]{1,0:T(8,128)(2,1)S(1)}, bf16[384,768]{1,0:T(8,128)(2,1)S(1)}, u32[]{:S(2)}, u32[]{:S(2)}) collective-permute-start(bf16[384,768]{1,0:T(8,128)(2,1)S(1)} %fusion.23), channel_id=1, source_target_pairs={{0,8},{1,9},{2,10},{3,11},{4,12},{5,13},{6,14},{7,15},{8,16},{9,17... | collective-permute-start | bytes 1769480 | tf_op jit(solution)/shard_map/ppermute | solution.py:73
  315.6 23.9 %collective-permute-start.126 = (bf16[192,1536]{1,0:T(8,128)(2,1)S(1)}, bf16[192,1536]{1,0:T(8,128)(2,1)S(1)}, u32[]{:S(2)}, u32[]{:S(2)}) collective-permute-start(bf16[192,1536]{1,0:T(8,128)(2,1)S(1)} %fusion.18), channel_id=1, source_target_pairs={{0,8},{1,9},{2,10},{3,11},{4,12},{5,13},{6,14},{7,15},{8,16},{9,17... | collective-permute-start | bytes 1769480 | tf_op jit(solution)/shard_map/ppermute | solution.py:73
  327.2 38.3 %collective-permute-start.45 = (bf16[4,160,1536]{2,1,0:T(8,128)(2,1)}, bf16[4,160,1536]{2,1,0:T(8,128)(2,1)S(1)}, u32[]{:S(2)}, u32[]{:S(2)}) collective-permute-start(bf16[4,160,1536]{2,1,0:T(8,128)(2,1)} %slice.240), channel_id=1, source_target_pairs={{0,1},{1,0},{2,3},{3,2},{4,5},{5,4},{6,7},{7,6},{8,9},{9,8},{10,11... | collective-permute-start | bytes 5898248 | tf_op jit(solution)/shard_map/ppermute | solution.py:62
  329.4 27.0 %collective-permute-start.116 = (bf16[384,768]{1,0:T(8,128)(2,1)}, bf16[384,768]{1,0:T(8,128)(2,1)}, u32[]{:S(2)}, u32[]{:S(2)}) collective-permute-start(bf16[384,768]{1,0:T(8,128)(2,1)} %get-tuple-element.46), channel_id=1, source_target_pairs={{16,8},{17,9},{18,10},{19,11},{20,12},{21,13},{22,14},{23,15},{24,... | collective-permute-start | bytes 1769480 | tf_op jit(solution)/shard_map/ppermute | solution.py:73
  340.9 21.7 %collective-permute-start.129 = (bf16[192,1536]{1,0:T(8,128)(2,1)}, bf16[192,1536]{1,0:T(8,128)(2,1)}, u32[]{:S(2)}, u32[]{:S(2)}) collective-permute-start(bf16[192,1536]{1,0:T(8,128)(2,1)} %get-tuple-element.42), channel_id=1, source_target_pairs={{16,8},{17,9},{18,10},{19,11},{20,12},{21,13},{22,14},{23,15},{24,... | collective-permute-start | bytes 1769480 | tf_op jit(solution)/shard_map/ppermute | solution.py:73
  351.5 17.8 %collective-permute-start.32 = (bf16[4,160,1536]{2,1,0:T(8,128)(2,1)}, bf16[4,160,1536]{2,1,0:T(8,128)(2,1)}, u32[]{:S(2)}, u32[]{:S(2)}) collective-permute-start(bf16[4,160,1536]{2,1,0:T(8,128)(2,1)} %slice.222), channel_id=1, source_target_pairs={{0,1},{1,0},{2,3},{3,2},{4,5},{5,4},{6,7},{7,6},{8,9},{9,8},{10,11... | collective-permute-start | bytes 5898248 | tf_op jit(solution)/shard_map/ppermute | solution.py:62
  352.2 47.4 %collective-permute-start.114 = (bf16[384,768]{1,0:T(8,128)(2,1)}, bf16[384,768]{1,0:T(8,128)(2,1)S(1)}, u32[]{:S(2)}, u32[]{:S(2)}) collective-permute-start(bf16[384,768]{1,0:T(8,128)(2,1)} %get-tuple-element.45), channel_id=1, source_target_pairs={{0,8},{1,9},{2,10},{3,11},{4,12},{5,13},{6,14},{7,15},{8,16},{9,17... | collective-permute-start | bytes 1769480 | tf_op jit(solution)/shard_map/ppermute | solution.py:73
  356.5 46.8 %collective-permute-start.127 = (bf16[192,1536]{1,0:T(8,128)(2,1)}, bf16[192,1536]{1,0:T(8,128)(2,1)S(1)}, u32[]{:S(2)}, u32[]{:S(2)}) collective-permute-start(bf16[192,1536]{1,0:T(8,128)(2,1)} %get-tuple-element.41), channel_id=1, source_target_pairs={{0,8},{1,9},{2,10},{3,11},{4,12},{5,13},{6,14},{7,15},{8,16},{9,17... | collective-permute-start | bytes 1769480 | tf_op jit(solution)/shard_map/ppermute | solution.py:73
  362.6 38.5 %collective-permute-start.117 = (bf16[384,768]{1,0:T(8,128)(2,1)S(1)}, bf16[384,768]{1,0:T(8,128)(2,1)S(1)}, u32[]{:S(2)}, u32[]{:S(2)}) collective-permute-start(bf16[384,768]{1,0:T(8,128)(2,1)S(1)} %fusion.22), channel_id=1, source_target_pairs={{8,0},{9,1},{10,2},{11,3},{12,4},{13,5},{14,6},{15,7},{16,8},{17,9... | collective-permute-start | bytes 1769480 | tf_op jit(solution)/shard_map/ppermute | solution.py:73
  365.5 38.4 %collective-permute-start.130 = (bf16[192,1536]{1,0:T(8,128)(2,1)S(1)}, bf16[192,1536]{1,0:T(8,128)(2,1)S(1)}, u32[]{:S(2)}, u32[]{:S(2)}) collective-permute-start(bf16[192,1536]{1,0:T(8,128)(2,1)S(1)} %fusion.17), channel_id=1, source_target_pairs={{8,0},{9,1},{10,2},{11,3},{12,4},{13,5},{14,6},{15,7},{16,8},{17,9... | collective-permute-start | bytes 1769480 | tf_op jit(solution)/shard_map/ppermute | solution.py:73
  396.4 48.7 %collective-permute-start.49 = (bf16[160,1536]{1,0:T(8,128)(2,1)}, bf16[160,1536]{1,0:T(8,128)(2,1)S(1)}, u32[]{:S(2)}, u32[]{:S(2)}) collective-permute-start(bf16[160,1536]{1,0:T(8,128)(2,1)} %pad_maximum_fusion.6), channel_id=1, source_target_pairs={{0,4},{1,5},{2,6},{3,7},{4,0},{5,1},{6,2},{7,3},{8,12},{9,13},{10,... | collective-permute-start | bytes 1474568 | tf_op jit(solution)/shard_map/ppermute | solution.py:62
  399.6 45.5 %collective-permute-start.47 = (bf16[160,1536]{1,0:T(8,128)(2,1)}, bf16[160,1536]{1,0:T(8,128)(2,1)}, u32[]{:S(2)}, u32[]{:S(2)}) collective-permute-start(bf16[160,1536]{1,0:T(8,128)(2,1)} %pad_maximum_fusion.5), channel_id=1, source_target_pairs={{0,2},{1,3},{2,0},{3,1},{4,6},{5,7},{6,4},{7,5},{8,10},{9,11},{10,... | collective-permute-start | bytes 1474568 | tf_op jit(solution)/shard_map/ppermute | solution.py:62
  401.1 46.8 %collective-permute-start.36 = (bf16[160,1536]{1,0:T(8,128)(2,1)}, bf16[160,1536]{1,0:T(8,128)(2,1)}, u32[]{:S(2)}, u32[]{:S(2)}) collective-permute-start(bf16[160,1536]{1,0:T(8,128)(2,1)} %pad_maximum_fusion.4), channel_id=1, source_target_pairs={{0,4},{1,5},{2,6},{3,7},{4,0},{5,1},{6,2},{7,3},{8,12},{9,13},{10,... | collective-permute-start | bytes 1474568 | tf_op jit(solution)/shard_map/ppermute | solution.py:62
  403.2 44.7 %collective-permute-start.34 = (bf16[160,1536]{1,0:T(8,128)(2,1)S(1)}, bf16[160,1536]{1,0:T(8,128)(2,1)}, u32[]{:S(2)}, u32[]{:S(2)}) collective-permute-start(bf16[160,1536]{1,0:T(8,128)(2,1)S(1)} %pad_maximum_fusion.3), channel_id=1, source_target_pairs={{0,2},{1,3},{2,0},{3,1},{4,6},{5,7},{6,4},{7,5},{8,10},{9,11},{10,... | collective-permute-start | bytes 1474568 | tf_op jit(solution)/shard_map/ppermute | solution.py:62
  406.4 14.6 %collective-permute-start.119 = (bf16[48,768]{1,0:T(8,128)(2,1)S(1)}, bf16[48,768]{1,0:T(8,128)(2,1)S(1)}, u32[]{:S(2)}, u32[]{:S(2)}) collective-permute-start(bf16[48,768]{1,0:T(8,128)(2,1)S(1)} %get-tuple-element.110), channel_id=1, source_target_pairs={{0,2},{1,3},{2,0},{3,1},{4,6},{5,7},{6,4},{7,5},{8,10},{9,11},{10,... | collective-permute-start | bytes 221192 | tf_op jit(solution)/shard_map/ppermute | solution.py:62
  474.6 25.9 %collective-permute-start.78 = (bf16[160,192]{1,0:T(8,128)(2,1)}, bf16[160,192]{1,0:T(8,128)(2,1)}, u32[]{:S(2)}, u32[]{:S(2)}) collective-permute-start(bf16[160,192]{1,0:T(8,128)(2,1)} %bitcast.604), channel_id=1, source_target_pairs={{0,1},{1,0},{2,3},{3,2},{4,5},{5,4},{6,7},{7,6},{8,9},{9,8},{10,11... | collective-permute-start | bytes 184328 | tf_op jit(solution)/shard_map/ppermute | solution.py:62
  474.6 28.3 %collective-permute-start.79 = (bf16[160,192]{1,0:T(8,128)(2,1)}, bf16[160,192]{1,0:T(8,128)(2,1)S(1)}, u32[]{:S(2)}, u32[]{:S(2)}) collective-permute-start(bf16[160,192]{1,0:T(8,128)(2,1)} %bitcast.603), channel_id=1, source_target_pairs={{0,2},{1,3},{2,0},{3,1},{4,6},{5,7},{6,4},{7,5},{8,10},{9,11},{10,... | collective-permute-start | bytes 184328 | tf_op jit(solution)/shard_map/ppermute | solution.py:62
  475.9 28.5 %collective-permute-start.80 = (bf16[160,192]{1,0:T(8,128)(2,1)}, bf16[160,192]{1,0:T(8,128)(2,1)S(1)}, u32[]{:S(2)}, u32[]{:S(2)}) collective-permute-start(bf16[160,192]{1,0:T(8,128)(2,1)} %bitcast.602), channel_id=1, source_target_pairs={{0,3},{1,2},{2,1},{3,0},{4,7},{5,6},{6,5},{7,4},{8,11},{9,10},{10,... | collective-permute-start | bytes 184328 | tf_op jit(solution)/shard_map/ppermute | solution.py:62
  476.5 28.2 %collective-permute-start.81 = (bf16[160,192]{1,0:T(8,128)(2,1)}, bf16[160,192]{1,0:T(8,128)(2,1)S(1)}, u32[]{:S(2)}, u32[]{:S(2)}) collective-permute-start(bf16[160,192]{1,0:T(8,128)(2,1)} %bitcast.601), channel_id=1, source_target_pairs={{0,4},{1,5},{2,6},{3,7},{4,0},{5,1},{6,2},{7,3},{8,12},{9,13},{10,... | collective-permute-start | bytes 184328 | tf_op jit(solution)/shard_map/ppermute | solution.py:62
  477.8 28.2 %collective-permute-start.82 = (bf16[160,192]{1,0:T(8,128)(2,1)}, bf16[160,192]{1,0:T(8,128)(2,1)S(1)}, u32[]{:S(2)}, u32[]{:S(2)}) collective-permute-start(bf16[160,192]{1,0:T(8,128)(2,1)} %bitcast.600), channel_id=1, source_target_pairs={{0,5},{1,4},{2,7},{3,6},{4,1},{5,0},{6,3},{7,2},{8,13},{9,12},{10,... | collective-permute-start | bytes 184328 | tf_op jit(solution)/shard_map/ppermute | solution.py:62
  504.4 63.9 %collective-permute-start.63 = (bf16[160,192]{1,0:T(8,128)(2,1)S(1)}, bf16[160,192]{1,0:T(8,128)(2,1)S(1)}, u32[]{:S(2)}, u32[]{:S(2)}) collective-permute-start(bf16[160,192]{1,0:T(8,128)(2,1)S(1)} %bitcast.639), channel_id=1, source_target_pairs={{0,1},{1,0},{2,3},{3,2},{4,5},{5,4},{6,7},{7,6},{8,9},{9,8},{10,11... | collective-permute-start | bytes 184328 | tf_op jit(solution)/shard_map/ppermute | solution.py:62
  504.7 65.1 %collective-permute-start.64 = (bf16[160,192]{1,0:T(8,128)(2,1)S(1)}, bf16[160,192]{1,0:T(8,128)(2,1)S(1)}, u32[]{:S(2)}, u32[]{:S(2)}) collective-permute-start(bf16[160,192]{1,0:T(8,128)(2,1)S(1)} %bitcast.638), channel_id=1, source_target_pairs={{0,2},{1,3},{2,0},{3,1},{4,6},{5,7},{6,4},{7,5},{8,10},{9,11},{10,... | collective-permute-start | bytes 184328 | tf_op jit(solution)/shard_map/ppermute | solution.py:62
  506.0 65.6 %collective-permute-start.65 = (bf16[160,192]{1,0:T(8,128)(2,1)S(1)}, bf16[160,192]{1,0:T(8,128)(2,1)S(1)}, u32[]{:S(2)}, u32[]{:S(2)}) collective-permute-start(bf16[160,192]{1,0:T(8,128)(2,1)S(1)} %bitcast.637), channel_id=1, source_target_pairs={{0,3},{1,2},{2,1},{3,0},{4,7},{5,6},{6,5},{7,4},{8,11},{9,10},{10,... | collective-permute-start | bytes 184328 | tf_op jit(solution)/shard_map/ppermute | solution.py:62
  506.5 65.3 %collective-permute-start.66 = (bf16[160,192]{1,0:T(8,128)(2,1)S(1)}, bf16[160,192]{1,0:T(8,128)(2,1)S(1)}, u32[]{:S(2)}, u32[]{:S(2)}) collective-permute-start(bf16[160,192]{1,0:T(8,128)(2,1)S(1)} %bitcast.636), channel_id=1, source_target_pairs={{0,4},{1,5},{2,6},{3,7},{4,0},{5,1},{6,2},{7,3},{8,12},{9,13},{10,... | collective-permute-start | bytes 184328 | tf_op jit(solution)/shard_map/ppermute | solution.py:62
  571.7 25.9 %collective-permute-start.50 = (f32[108,128]{1,0:T(8,128)S(1)}, f32[108,128]{1,0:T(8,128)S(1)}, u32[]{:S(2)}, u32[]{:S(2)}) collective-permute-start(f32[108,128]{1,0:T(8,128)S(1)} %bitcast.631), channel_id=1, source_target_pairs={{0,1},{1,0},{2,3},{3,2},{4,5},{5,4},{6,7},{7,6},{8,9},{9,8},{10,11... | collective-permute-start | bytes 165896 | tf_op jit(solution)/shard_map/ppermute | solution.py:62
  596.0 34.1 %collective-permute-start.102 = (bf16[384,768]{1,0:T(8,128)(2,1)S(1)}, bf16[384,768]{1,0:T(8,128)(2,1)}, u32[]{:S(2)}, u32[]{:S(2)}) collective-permute-start(bf16[384,768]{1,0:T(8,128)(2,1)S(1)} %bitcast.628), channel_id=1, source_target_pairs={{24,16},{25,17},{26,18},{27,19},{28,20},{29,21},{30,22},{31,23}} | collective-permute-start | bytes 1769480 | tf_op jit(solution)/shard_map/ppermute | solution.py:73
  597.6 40.1 %collective-permute-start.51 = (f32[108,128]{1,0:T(8,128)S(1)}, f32[108,128]{1,0:T(8,128)S(1)}, u32[]{:S(2)}, u32[]{:S(2)}) collective-permute-start(f32[108,128]{1,0:T(8,128)S(1)} %bitcast_add_fusion.15), channel_id=1, source_target_pairs={{0,2},{1,3},{2,0},{3,1},{4,6},{5,7},{6,4},{7,5},{8,10},{9,11},{10,... | collective-permute-start | bytes 165896 | tf_op jit(solution)/shard_map/ppermute | solution.py:62
  599.9 34.0 %collective-permute-start.99 = (bf16[384,768]{1,0:T(8,128)(2,1)S(1)}, bf16[384,768]{1,0:T(8,128)(2,1)}, u32[]{:S(2)}, u32[]{:S(2)}) collective-permute-start(bf16[384,768]{1,0:T(8,128)(2,1)S(1)} %bitcast.629), channel_id=1, source_target_pairs={{0,8},{1,9},{2,10},{3,11},{4,12},{5,13},{6,14},{7,15}} | collective-permute-start | bytes 1769480 | tf_op jit(solution)/shard_map/ppermute | solution.py:73
  632.5 17.0 %collective-permute-start.103 = (bf16[384,768]{1,0:T(8,128)(2,1)}, bf16[384,768]{1,0:T(8,128)(2,1)}, u32[]{:S(2)}, u32[]{:S(2)}) collective-permute-start(bf16[384,768]{1,0:T(8,128)(2,1)} %fusion.27), channel_id=1, source_target_pairs={{16,8},{17,9},{18,10},{19,11},{20,12},{21,13},{22,14},{23,15},{24,... | collective-permute-start | bytes 1769480 | tf_op jit(solution)/shard_map/ppermute | solution.py:73
  635.5 17.7 %collective-permute-start.100 = (bf16[384,768]{1,0:T(8,128)(2,1)S(1)}, bf16[384,768]{1,0:T(8,128)(2,1)}, u32[]{:S(2)}, u32[]{:S(2)}) collective-permute-start(bf16[384,768]{1,0:T(8,128)(2,1)S(1)} %fusion.29), channel_id=1, source_target_pairs={{0,8},{1,9},{2,10},{3,11},{4,12},{5,13},{6,14},{7,15},{8,16},{9,17... | collective-permute-start | bytes 1769480 | tf_op jit(solution)/shard_map/ppermute | solution.py:73
  651.9 21.6 %collective-permute-start.104 = (bf16[384,768]{1,0:T(8,128)(2,1)}, bf16[384,768]{1,0:T(8,128)(2,1)}, u32[]{:S(2)}, u32[]{:S(2)}) collective-permute-start(bf16[384,768]{1,0:T(8,128)(2,1)} %fusion.28), channel_id=1, source_target_pairs={{8,0},{9,1},{10,2},{11,3},{12,4},{13,5},{14,6},{15,7},{16,8},{17,9... | collective-permute-start | bytes 1769480 | tf_op jit(solution)/shard_map/ppermute | solution.py:73
  655.6 17.9 %collective-permute-start.101 = (bf16[384,768]{1,0:T(8,128)(2,1)}, bf16[384,768]{1,0:T(8,128)(2,1)}, u32[]{:S(2)}, u32[]{:S(2)}) collective-permute-start(bf16[384,768]{1,0:T(8,128)(2,1)} %fusion.30), channel_id=1, source_target_pairs={{0,8},{1,9},{2,10},{3,11},{4,12},{5,13},{6,14},{7,15},{8,16},{9,17... | collective-permute-start | bytes 1769480 | tf_op jit(solution)/shard_map/ppermute | solution.py:73
  (147 other events, 1378.7 us)

commit v2 on v1

--- a/solution.py
+++ b/solution.py
@@ -7,6 +7,7 @@
 HEAD_DIM = 128
 LEVELS = 4
 GROUP = 8
+CHIPS = 4
 EPSILON = 1e-05
 NEGATIVE = -1e30
 BF = jnp.bfloat16
@@ -73,82 +74,72 @@
     return lax.ppermute(value, "dp", pairs)
 
 
-def sum_all(value):
-    bit = 1
-    while bit < lax.axis_size("dp"):
-        value = value + swap(value, bit)
-        bit *= 2
-    return value
-
-
-def plane_gather(own):
-    half = own.shape[0] // 2
-    slots = [own] + [None] * 7
-    slots[2], slots[4], slots[1] = swap(own, 2), swap(own, 4), swap(own, 1)
-    slots[6] = jnp.concatenate([swap(slots[2][:half], 4), swap(slots[4][half:], 2)], axis=0)
-    for k in (2, 4, 6):
-        slots[k + 1] = swap(slots[k], 1)
-    return jnp.stack(slots)
-
-
-def plane_scatter_sum(parts):
-    half = parts.shape[1] // 2
-    sent = swap(parts[1::2].astype(BF), 1)
-    total = [parts[2 * j].astype(F32) + sent[j].astype(F32) for j in range(4)]
-    corner = total[3].astype(BF)
-    by_x, by_y = swap(corner[:half], 2), swap(corner[half:], 4)
-    to_y = jnp.concatenate([total[2][:half] + by_x.astype(F32), total[2][half:]], axis=0)
-    to_x = jnp.concatenate([total[1][:half], total[1][half:] + by_y.astype(F32)], axis=0)
-    return total[0] + swap(to_x.astype(BF), 2).astype(F32) + swap(to_y.astype(BF), 4).astype(F32)
-
-
-def plane_exchange(chunks):
-    place = lax.axis_index("dp") % GROUP
+def lines():
+    groups = lax.axis_size("dp") // GROUP
+    return [[z * GROUP + t for z in range(groups)] for t in range(GROUP)]
+
+
+def spread(own):
+    return [own, swap(own, 2), swap(own, 4), swap(own, 6)]
+
+
+def gather_sum(parts):
+    total = parts[0].astype(F32)
+    for j in (1, 2, 3):
+        total = total + swap(parts[j].astype(BF), 2 * j).astype(F32)
+    return total
+
+
+def exchange(chunks):
+    chip = lax.axis_index("dp") % GROUP // 2
     got = []
-    for k in range(GROUP):
-        chunk = lax.dynamic_index_in_dim(chunks, place ^ k, 0, keepdims=False)
-        got.append(chunk if k == 0 else swap(chunk, k))
-    return jnp.stack(got)
+    for j in range(CHIPS):
+        chunk = lax.dynamic_index_in_dim(chunks, chip ^ j, 0, keepdims=False)
+        got.append(chunk if j == 0 else swap(chunk, 2 * j))
+    return got
 
 
 def in_order(slots):
-    place = lax.axis_index("dp") % GROUP
-    return jnp.take(slots, place ^ jnp.arange(GROUP), axis=0)
+    chip = lax.axis_index("dp") % GROUP // 2
+    odd, high = chip % 2 == 1, chip // 2 == 1
+    a, b, c, d = slots
+    a, b, c, d = jnp.where(odd, b, a), jnp.where(odd, a, b), jnp.where(odd, d, c), jnp.where(odd, c, d)
+    return [jnp.where(high, c, a), jnp.where(high, d, b), jnp.where(high, a, c), jnp.where(high, b, d)]
 
 
 def line_gather(own):
     groups = lax.axis_size("dp") // GROUP
     z = lax.axis_index("dp") // GROUP
-    up = down = own
-    spare = jnp.zeros((groups + 1,) + own.shape, own.dtype)
-    found = [(z, own)]
+    ups, downs = [own], [own]
     for s in range(1, groups):
-        up = hop(up, 1, s - 1, groups - 1)
-        down = hop(down, -1, 1, groups - s + 1)
-        found.append((jnp.where(z - s >= 0, z - s, groups), up))
-        found.append((jnp.where(z + s < groups, z + s, groups), down))
-    for slot, value in found:
-        spare = lax.dynamic_update_index_in_dim(spare, value, slot, 0)
-    return spare[:groups]
+        ups.append(hop(ups[-1], 1, s - 1, groups - 1))
+        downs.append(hop(downs[-1], -1, 1, groups - s + 1))
+    return jnp.stack(
+        [own] + [jnp.where(z + s < groups, downs[s], ups[groups - s]) for s in range(1, groups)]
+    )
 
 
 def line_scatter_sum(parts):
-    groups = parts.shape[0]
-    z = lax.axis_index("dp") // GROUP
-
-    def part(offset):
-        slot = jnp.clip(z + offset, 0, groups - 1)
-        return lax.dynamic_index_in_dim(parts, slot, 0, keepdims=False).astype(F32)
-
+    groups = lax.axis_size("dp") // GROUP
     up = down = None
     for s in range(1, groups):
-        far = groups - s
-        up_send, down_send = part(far), part(-far)
+        up_send, down_send = parts[groups - s].astype(F32), parts[s].astype(F32)
         if up is not None:
             up_send, down_send = up_send + up.astype(F32), down_send + down.astype(F32)
         up = hop(up_send.astype(BF), 1, 0, s)
         down = hop(down_send.astype(BF), -1, groups - s, groups)
-    return part(0) + up.astype(F32) + down.astype(F32)
+    return parts[0].astype(F32) + up.astype(F32) + down.astype(F32)
+
+
+def turn(value, shift, axis, parts):
+    step = value.shape[axis] // parts
+    return lax.dynamic_slice_in_dim(
+        jnp.concatenate([value, value], axis=axis), shift * step, value.shape[axis], axis
+    )
+
+
+def core_sum(mine, other):
+    return mine + swap(other.astype(BF), 1).astype(F32)
 
 
 def per_device(
@@ -174,7 +165,7 @@
     devices = lax.axis_size("dp")
     me = lax.axis_index("dp")
     groups = devices // GROUP
-    z, place = me // GROUP, me % GROUP
+    z, chip, core = me // GROUP, me % GROUP // 2, me % 2
     tokens, width = sequence_elements.shape
     heads = width // HEAD_DIM
     rows, feed = expand_matrix.shape
@@ -193,7 +184,8 @@
         ]
     )
     info = jnp.pad(info, (0, -info.shape[0] % 128))
-    table = sum_all(jnp.where(jnp.arange(devices)[:, None] == me, info[None, :], 0.0))
+    table = jnp.broadcast_to(info, (devices, 1) + info.shape)
+    table = lax.all_to_all(table, "dp", 0, 0, tiled=True).reshape(devices, -1)
     result_offset = table[:, :offset_len].reshape(-1)
     hidden_offsets = table[:, offset_len : offset_len + cols]
     all_levels = table[:, offset_len + cols].astype(jnp.int32)
@@ -210,11 +202,24 @@
     arrival = local + jnp.sum(jnp.where(earlier[None, :], seen, 0), axis=1)
     kept = (arrival < limit).astype(F32)[:, None]
 
-    expand_chunks = expand_matrix.reshape(rows, groups, GROUP, cols).transpose(2, 0, 1, 3)
-    expand_plane = plane_exchange(expand_chunks.reshape(GROUP, rows, groups * cols))
-    expand_plane = in_order(expand_plane).reshape(GROUP * rows, groups * cols)
-    first_weight = line_gather(expand_plane).reshape(width, groups * cols)
-    second_weight = line_gather(contract_matrix).reshape(groups * cols, width)
+    block = 2 * cols
+    units = groups * block
+    expand_chunks = expand_matrix.reshape(rows, groups, CHIPS, block).transpose(2, 0, 1, 3)
+    expand_plane = jnp.concatenate(in_order(exchange(expand_chunks.reshape(CHIPS, rows, units))), axis=0)
+    expand_mine = line_gather(expand_plane).reshape(groups, CHIPS, rows, units)
+    expand_other = swap(expand_mine, 1)
+    contract_mine = lax.all_gather(contract_matrix, "dp", axis_index_groups=lines())
+    contract_other = swap(contract_mine, 1)
+    first_weight = jnp.where(
+        core == 0,
+        jnp.stack([expand_mine, expand_other], axis=2),
+        jnp.stack([expand_other, expand_mine], axis=2),
+    ).reshape(width, units)
+    second_weight = jnp.where(
+        core == 0,
+        jnp.stack([contract_mine, contract_other], axis=1),
+        jnp.stack([contract_other, contract_mine], axis=1),
+    ).reshape(units, width)
 
     gain_first = mixer_gain.astype(F32)
     gain_second = feedforward_gain.astype(F32)
@@ -241,16 +246,16 @@
 
     sensitivity = result_sensitivity.astype(F32)
     kept_sensitivity = (sensitivity * kept).astype(BF)
-    group_grad = plane_gather(kept_sensitivity).reshape(GROUP * tokens, width)
-    group_rows = plane_gather(normed_second).reshape(GROUP * tokens, width)
-    slot_levels = jnp.take(all_levels, z * GROUP + (place ^ jnp.arange(GROUP)))
-    starts = (jnp.arange(groups) * GROUP + place) * cols
+    group_grad = jnp.concatenate(spread(kept_sensitivity), axis=0)
+    group_rows = jnp.concatenate(spread(turn(normed_second, z, 1, groups)), axis=0)
+    slot_levels = jnp.take(all_levels, me ^ (2 * jnp.arange(CHIPS)))
+    starts = (jnp.arange(groups) * CHIPS + chip) * block
     active_block = starts[None, :] < (feed // 8) * (1 << slot_levels[:, None])
     mask = jnp.broadcast_to(
-        active_block[:, None, :, None], (GROUP, tokens, groups, cols)
-    ).reshape(GROUP * tokens, groups * cols)
+        active_block[:, None, :, None], (CHIPS, tokens, groups, block)
+    ).reshape(CHIPS * tokens, units)
     hidden_offset = lax.dynamic_index_in_dim(
-        hidden_offsets.reshape(groups, GROUP, cols), place, 1, keepdims=False
+        hidden_offsets.reshape(groups, CHIPS, block), chip, 1, keepdims=False
     ).reshape(-1)
     hidden = dot(group_rows, first_weight) + hidden_offset
     inner = 0.7978845608 * (hidden + 0.044715 * hidden * hidden * hidden)
@@ -261,27 +266,36 @@
     )
     active_grad = dot_t(group_grad, second_weight)
     hidden_grad = jnp.where(mask, active_grad * slope, 0.0).astype(BF)
-    second_parts = dot_t(hidden_grad, first_weight).reshape(GROUP, tokens, width)
-    second_grad = plane_scatter_sum(second_parts).astype(BF).astype(F32)
-    branch_parts = dot(active, second_weight).reshape(GROUP, tokens, width)
-    branch = (plane_scatter_sum(branch_parts) + result_offset).astype(BF).astype(F32)
+    second_parts = dot_t(hidden_grad, first_weight).reshape(CHIPS, tokens, width)
+    second_grad = turn(gather_sum(second_parts), (groups - z) % groups, 1, groups)
+    second_grad = second_grad.astype(BF).astype(F32)
+    branch_parts = dot(active, second_weight).reshape(CHIPS, tokens, width)
+    branch = (gather_sum(branch_parts) + result_offset).astype(BF).astype(F32)
     layer_output = (mixed + kept * branch).astype(BF)
-    contract_part = t_dot(active, group_grad).reshape(groups, cols, width)
-    share_contract = line_scatter_sum(contract_part)
-    expand_part = t_dot(group_rows, hidden_grad).reshape(groups, GROUP * rows, groups * cols)
-    expand_rows = line_scatter_sum(expand_part)
+    contract_part = t_dot(active, group_grad).reshape(groups, 2, cols, width)
+    contract_sum = core_sum(
+        lax.dynamic_index_in_dim(contract_part, core, 1, keepdims=False),
+        lax.dynamic_index_in_dim(contract_part, 1 - core, 1, keepdims=False),
+    ).astype(BF)
+    share_contract = lax.psum_scatter(
+        contract_sum, "dp", scatter_dimension=0, axis_index_groups=lines()
+    ).astype(F32)
+
+    def rows_home(part):
+        part = part.reshape(groups, CHIPS, 2, rows, part.shape[1])
+        both = core_sum(
+            lax.dynamic_index_in_dim(part, core, 2, keepdims=False),
+            lax.dynamic_index_in_dim(part, 1 - core, 2, keepdims=False),
+        )
+        return in_order(exchange(line_scatter_sum(both).astype(BF)))
+
+    expand_home = rows_home(t_dot(group_rows, hidden_grad))
+    share_expand = (
+        jnp.stack([piece.reshape(rows, groups, block) for piece in expand_home], axis=2)
+        .astype(F32)
+        .reshape(rows, feed)
+    )
     hidden_sum = jnp.sum(hidden_grad.astype(F32), axis=0)
-
-    def rows_home(summed):
-        swapped = plane_exchange(summed.astype(BF).reshape(GROUP, rows, groups * cols))
-        return in_order(swapped).astype(F32)
-
-    share_expand = (
-        rows_home(expand_rows)
-        .reshape(GROUP, rows, groups, cols)
-        .transpose(1, 2, 0, 3)
-        .reshape(rows, feed)
-    )
 
     mixed_part, midnorm_sum, midshift_sum = norm_back(second_grad, gain_second, normal_second, inverse_second)
     mixed_grad = sensitivity + mixed_part
@@ -299,45 +313,39 @@
     input_part, leadnorm_sum, leadshift_sum = norm_back(leading, gain_first, normal_first, inverse_first)
     layer_input_gradient = (mixed_grad + input_part).astype(BF)
 
-    share = width // GROUP
-    group_first = plane_gather(normed_first).reshape(GROUP * tokens, width)
-    group_context = plane_gather(context).reshape(GROUP * tokens, width)
-
-    def split_columns(grad):
-        chunks = grad.reshape(tokens, GROUP, share).transpose(1, 0, 2)
-        return plane_exchange(chunks).reshape(GROUP * tokens, share)
-
-    weight_parts = jnp.concatenate(
-        [
-            t_dot(group_context, split_columns(mixed_low)),
-            t_dot(group_first, split_columns(value_grad)),
-            t_dot(group_first, split_columns(key_grad)),
-            t_dot(group_first, split_columns(query_grad)),
-        ],
-        axis=1,
-    )
-    weight_rows = line_scatter_sum(weight_parts.reshape(groups, GROUP * rows, 4 * share))
-    swapped = plane_exchange(weight_rows.astype(BF).reshape(GROUP, rows, 4 * share))
-    weight_home = (
-        in_order(swapped)
-        .astype(F32)
-        .reshape(GROUP, rows, 4, share)
-        .transpose(2, 1, 0, 3)
-        .reshape(4, rows, width)
-    )
-    share_mixing, share_value, share_key, share_query = (weight_home[i] for i in range(4))
-
-    hidden_spot = (jnp.arange(GROUP)[None, :, None] == place).astype(F32)
-    hidden_full = (hidden_spot * hidden_sum.reshape(groups, 1, cols)).reshape(-1)
+    share = width // CHIPS
+    group_first = jnp.concatenate(spread(turn(normed_first, z, 1, groups)), axis=0)
+    group_context = jnp.concatenate(spread(turn(context, z, 1, groups)), axis=0)
+
+    def split_columns(*grads):
+        chunks = jnp.concatenate([grad.reshape(tokens, CHIPS, share) for grad in grads], axis=2)
+        return jnp.concatenate(exchange(chunks.transpose(1, 0, 2)), axis=0)
+
+    first_pair = split_columns(mixed_low, value_grad)
+    second_pair = split_columns(key_grad, query_grad)
+    early = rows_home(
+        jnp.concatenate(
+            [t_dot(group_context, first_pair[:, :share]), t_dot(group_first, first_pair[:, share:])], axis=1
+        )
+    )
+    late = rows_home(t_dot(group_first, second_pair))
+
+    def join(pieces, low):
+        return jnp.concatenate([piece[:, low : low + share] for piece in pieces], axis=1).astype(F32)
+
+    share_mixing, share_value = join(early, 0), join(early, share)
+    share_key, share_query = join(late, 0), join(late, share)
+
+    hidden_spot = (jnp.arange(CHIPS)[None, :, None] == chip).astype(F32)
+    hidden_full = hidden_spot * hidden_sum.reshape(groups, 1, block)
     result_sum = jnp.sum(kept_sensitivity.astype(F32), axis=0)
-    vectors = sum_all(
-        jnp.concatenate(
-            [midnorm_sum, midshift_sum, leadnorm_sum, leadshift_sum, result_sum, hidden_full]
-        ).reshape(-1, 128)
-    ).reshape(-1)
-    small = vectors[: 5 * width].reshape(5, devices, width // devices)
-    small = lax.dynamic_index_in_dim(small, me, 1, keepdims=False)
-    share_hidden = lax.dynamic_slice_in_dim(vectors, 5 * width + me * cols, cols)
+    vectors = [midnorm_sum, midshift_sum, leadnorm_sum, leadshift_sum, result_sum, hidden_full]
+    vectors = jnp.concatenate([vector.reshape(devices, -1) for vector in vectors], axis=1)
+    vectors = jnp.pad(vectors, ((0, 0), (0, -vectors.shape[1] % 128)))
+    vectors = lax.all_to_all(vectors[:, None, :], "dp", 0, 0, tiled=True)
+    vectors = jnp.sum(vectors, axis=(0, 1))
+    small = [vectors[i * offset_len : (i + 1) * offset_len] for i in range(5)]
+    share_hidden = vectors[5 * offset_len : 5 * offset_len + cols]
     return (
         layer_output,
         layer_input_gradient,

time: 712 us -> 523 us (0.73)
  local copies, waits for them, and re-layouts: 191 us -> 55.9 us
  waiting for transfers between devices: 218 us -> 142 us
  between operations: 6.53 us -> 19.7 us
    ppermute x101 -> x42, waiting for transfers between devices: 171 us -> 67.2 us  [swap(): return lax.ppermute(value, 'dp', [(i, i ^ bit) for i in range(count)])]
    dynamic_slice x9 -> x1, local copies, waits for them, and re-layouts: 43.8 us -> 0.03 us  [per_device(): lax.dynamic_index_in_dim(hidden_offsets.reshape(groups, CHIPS, block), ch...]
    unnamed x271 -> x144, local copies, waits for them, and re-layouts: 48.4 us -> 8.5 us
    ppermute x101 -> x42, starting transfers between devices: 84.9 us -> 51 us  [swap(): return lax.ppermute(value, 'dp', [(i, i ^ bit) for i in range(count)])]
    ppermute x30 -> x24, starting transfers between devices: 66.7 us -> 88 us  [hop(): return lax.ppermute(value, 'dp', pairs)]
    all_to_all x0 -> x2, starting transfers between devices: none -> 20.1 us  [the longest x1 11.3 us: per_device(): vectors = lax.all_to_all(vectors[:, None, :], 'dp', 0, 0, tiled=True)]
    dynamic_update_slice x14 -> x0, local copies, waits for them, and re-layouts: 17.4 us -> none  [line_gather(): spare = lax.dynamic_update_index_in_dim(spare, value, slot, 0)]
    reshape x12 -> x10, local copies, waits for them, and re-layouts: 20.5 us -> 3.16 us  [the longest x2 1.77 us: per_device(): expand_matrix.reshape(rows, groups, CHIPS, block).transpose(2, 0, 1, 3)]
  transfers between devices with their start and end apart: 131 -> 70, of which waited for: 52 -> 26; matrix products, arithmetic and copies ran while one was open for 39% -> 36% of each run, Pallas kernels for 0% -> 0%
where the time goes in v2:
time: 523 us; the launch traced here: 513 us
  starting transfers between devices  159 us (30%)
  waiting for transfers between devices  142 us (27%)
  matrix products  77.6 us (15%)
  other arithmetic  59.3 us (11%)
  local copies, waits for them, and re-layouts  55.9 us (11%)
  between operations  19.7 us (4%)
    ppermute x24, starting transfers between devices, hop(): return lax.ppermute(value, 'dp', pairs)  88 us
    dot_general x17, matrix products, dot(): lax.dot_general(left, right, (dims, ((), ())), preferred_element_type=F32)  69.4 us
    ppermute x42, waiting for transfers between devices, swap(): return lax.ppermute(value, 'dp', [(i, i ^ bit) for i in range(count)])  67.2 us
    ppermute x24, waiting for transfers between devices, hop(): return lax.ppermute(value, 'dp', pairs)  64.6 us
    ppermute x42, starting transfers between devices, swap(): return lax.ppermute(value, 'dp', [(i, i ^ bit) for i in range(count)])  51 us
    all_to_all x1, starting transfers between devices, per_device(): vectors = lax.all_to_all(vectors[:, None, :], 'dp', 0, 0, tiled=True)  11.3 us
  transfers between devices with their start and end apart: 70, of which 26 were waited for; matrix products, arithmetic and copies ran while one was open for 36% of the time, Pallas kernels for 0%

profile of v2, /device:TPU:0, one launch (start us, length us, event | category | flops | bytes accessed | tf_op | source)
XLA Modules:
  0.0 513.3 jit_solution(1293758302062612192)
XLA Ops:
  10.2 3.9 collective-permute-start.3
  15.6 4.5 fusion.27
  21.2 3.3 fusion.156
  25.8 2.6 fusion.140
  29.7 3.1 fusion.151
  32.8 2.2 fusion.26
  35.1 3.4 fusion.152
  41.5 5.4 %collective-permute-start.7 = (bf16[192,1536]{1,0:T(8,128)(2,1)S(1)}, bf16[192,1536]{1,0:T(8,128)(2,1)}, u32[]{:S(2)}, u32[]{:S(2)}) collective-permute-start(bf16[192,1536]{1,0:T(8,128)(2,1)S(1)} %pad_maximum_fusion.6), channel_id=1, source_target_pairs={{0,8},{1,9},{2,10},{3,11},{4,12},{5,13},{6,14},{7,15},{8,16},{9,17... | collective-permute-start | bytes 1769480 | tf_op jit(solution)/shard_map/ppermute | solution.py:74
  47.2 9.4 %collective-permute-done.6 = bf16[192,1536]{1,0:T(8,128)(2,1)} collective-permute-done((bf16[192,1536]{1,0:T(8,128)(2,1)S(1)}, bf16[192,1536]{1,0:T(8,128)(2,1)}, u32[]{:S(2)}, u32[]{:S(2)}) %collective-permute-start.6) | collective-permute-done | bytes 589856 | tf_op jit(solution)/shard_map/ppermute | solution.py:74
  58.9 2.6 collective-permute-start.2
  69.3 8.8 %all-to-all-start = ((f32[32,1,256]{2,1,0:T(1,128)}), f32[32,1,256]{2,1,0:T(1,128)}, u32[]{:S(2)}, u32[]{:S(2)}) async-start(f32[32,1,256]{2,1,0:T(1,128)} %broadcast_in_dim.46), calls=%async_computation | async-start | bytes 65536 | tf_op jit(solution)/shard_map/all_to_all | solution.py:188
  84.7 23.5 %collective-permute-done.11 = bf16[192,1536]{1,0:T(8,128)(2,1)} collective-permute-done((bf16[192,1536]{1,0:T(8,128)(2,1)}, bf16[192,1536]{1,0:T(8,128)(2,1)}, u32[]{:S(2)}, u32[]{:S(2)}) %collective-permute-start.11) | collective-permute-done | bytes 589856 | tf_op jit(solution)/shard_map/ppermute | solution.py:74
  108.2 3.0 collective-permute-start.25
  125.6 9.0 %all-gather.3.cloned.1.call-done = bf16[768,1536]{1,0:T(8,128)(2,1)} async-done(((bf16[192,1536]{1,0:T(8,128)(2,1)}), bf16[768,1536]{1,0:T(8,128)(2,1)}) %all-gather.3.cloned.1.call-update) | async-done | bytes 2359312 | tf_op jit(solution)/shard_map/all_gather | solution.py:211
  134.7 4.5 maximum_select_fusion
  139.2 2.6 collective-permute-start.19
  142.7 4.8 fusion.111
  147.5 6.7 %collective-permute-done.19 = bf16[160,1536]{1,0:T(8,128)(2,1)S(1)} collective-permute-done((bf16[160,1536]{1,0:T(8,128)(2,1)S(1)}, bf16[160,1536]{1,0:T(8,128)(2,1)S(1)}, u32[]{:S(2)}, u32[]{:S(2)}) %collective-permute-start.19) | collective-permute-done | bytes 491552 | tf_op jit(solution)/shard_map/ppermute | solution.py:63
  155.9 8.5 %collective-permute-done.18 = bf16[160,1536]{1,0:T(8,128)(2,1)S(1)} collective-permute-done((bf16[160,1536]{1,0:T(8,128)(2,1)S(1)}, bf16[160,1536]{1,0:T(8,128)(2,1)S(1)}, u32[]{:S(2)}, u32[]{:S(2)}) %collective-permute-start.18) | collective-permute-done | bytes 491552 | tf_op jit(solution)/shard_map/ppermute | solution.py:63
  164.5 4.9 fusion.109
  174.1 5.9 %fusion.154 = (bf16[640,1536]{1,0:T(8,128)(2,1)S(1)}, f32[640,1536]{1,0:T(8,128)}) fusion(bf16[1536,1536]{1,0:T(8,128)(2,1)S(1)} %bitcast.328, pred[640,1536]{1,0:T(8,128)(4,1)S(1)} %bitcast.339, f32[640,1536]{1,0:T(8,128)S(1)} %fusion.111, f32[1536]{0:T(1024)S(1)} %copy-done.49), kind=kOutput, calls=%fused_computation.365 | convolution fusion | flops 3031695360 | bytes 15538176 | tf_op jit(solution)/shard_map/dot_general | solution.py:18
  180.0 7.8 %convert_reduce_fusion = (f32[1536]{0:T(1024)}, bf16[640,1536]{1,0:T(8,128)(2,1)S(1)}) fusion(pred[640,1536]{1,0:T(8,128)(4,1)S(1)} %bitcast.340, f32[640,1536]{1,0:T(8,128)S(1)} %fusion.111, f32[1536]{0:T(1024)S(1)} %copy-done.49, bf16[1536,1536]{1,0:T(8,128)(2,1)S(1)} %bitcast.329, bf16[160,1536]{1,0:T(8,128)(2,1)S(1)} %collective-permute-done.19, ...), kind=kOutput, calls=%fused_computation.20 | convolution fusion | flops 3050371584 | bytes 13578240 | tf_op jit(solution)/shard_map/dot_general | solution.py:18
  187.8 5.2 %fusion.153 = (bf16[640,1536]{1,0:T(8,128)(2,1)S(1)}, f32[640,1536]{1,0:T(8,128)}) fusion(bf16[640,1536]{1,0:T(8,128)(2,1)S(1)} %get-tuple-element.143, bf16[1536,1536]{1,0:T(8,128)(2,1)S(1)} %bitcast.327), kind=kOutput, calls=%fused_computation.364 | convolution fusion | flops 3020881920 | bytes 12582912 | tf_op jit(solution)/shard_map/dot_general | solution.py:18
  194.2 2.3 collective-permute-start.22
  201.8 6.3 %fusion.110 = f32[1536,1536]{1,0:T(8,128)S(1)} fusion(bf16[640,1536]{1,0:T(8,128)(2,1)} %copy-done.61, bf16[160,1536]{1,0:T(8,128)(2,1)} %collective-permute-done.2, bf16[160,1536]{1,0:T(8,128)(2,1)} %collective-permute-done.1, bf16[160,1536]{1,0:T(8,128)(2,1)} %collective-permute-done, bf16[160,1536]{1,0:T(8,128)(2,1)} %fusion.87), kind=kOutput, calls=%fused_computation.212 | convolution fusion | flops 3027763200 | bytes 13369344 | tf_op jit(solution)/shard_map/dot_general | solution.py:18
  209.9 2.3 collective-permute-start.16
  212.3 7.7 %collective-permute-done.21 = bf16[160,1536]{1,0:T(8,128)(2,1)} collective-permute-done((bf16[160,1536]{1,0:T(8,128)(2,1)}, bf16[160,1536]{1,0:T(8,128)(2,1)}, u32[]{:S(2)}, u32[]{:S(2)}) %collective-permute-start.21) | collective-permute-done | bytes 491552 | tf_op jit(solution)/shard_map/ppermute | solution.py:63
  222.8 2.0 fusion.59
  226.1 4.5 collective-permute-done.16
  232.0 7.8 %collective-permute-done.15 = bf16[160,1536]{1,0:T(8,128)(2,1)S(1)} collective-permute-done((bf16[160,1536]{1,0:T(8,128)(2,1)S(1)}, bf16[160,1536]{1,0:T(8,128)(2,1)S(1)}, u32[]{:S(2)}, u32[]{:S(2)}) %collective-permute-start.15) | collective-permute-done | bytes 491552 | tf_op jit(solution)/shard_map/ppermute | solution.py:63
  241.1 2.7 fusion.136
  250.4 2.7 fusion.92
  255.3 5.3 %convolution_add_fusion.1 = f32[160,1536]{1,0:T(8,128)} fusion(f32[160,1536]{1,0:T(8,128)} %fusion.92, bf16[1536,1536]{1,0:T(8,128)(2,1)} %param.31, bf16[160,12,64]{2,0,1:T(8,128)(2,1)S(1)} %get-tuple-element.63, bf16[160,12,64]{2,0,1:T(8,128)(2,1)S(1)} %get-tuple-element.62), kind=kOutput, calls=%fused_computation.23 | convolution fusion | flops 756203520 | bytes 7176192 | tf_op jit(solution)/shard_map/dot_general | solution.py:18
  260.9 5.3 %fusion.49 = (f32[1536]{0:T(1024)S(1)}, f32[160]{0:T(256)S(1)}, f32[160]{0:T(256)S(1)}, f32[1536]{0:T(1024)S(1)}, f32[160,1536]{1,0:T(8,128)}) fusion(bf16[160,1536]{1,0:T(8,128)(2,1)S(1)} %copy-done.2, f32[160]{0:T(256)S(1)} %copy-done.47, f32[160]{0:T(256)S(1)} %copy-done.41, f32[1536]{0:T(1024)S(1)} %convert_element_type.372, ...), kind=kOutput, calls=%fused_computation.99 | convolution fusion | flops 757674752 | bytes 7688704 | tf_op jit(solution)/shard_map/dot_general | solution.py:18
  267.2 11.3 %all-to-all-start.1 = ((f32[32,1,512]{2,1,0:T(1,128)}), f32[32,1,512]{2,1,0:T(1,128)S(1)}, u32[]{:S(2)}, u32[]{:S(2)}) async-start(f32[32,1,512]{2,1,0:T(1,128)} %broadcast_in_dim.52), calls=%async_computation.1 | async-start | bytes 131072 | tf_op jit(solution)/shard_map/all_to_all | solution.py:345
  283.2 1.8 convert_element_type.421
  285.3 2.0 constant_dynamic-slice_fusion.7
  288.0 2.7 collective-permute-start.28
  295.2 2.0 constant_dynamic-slice_fusion.3
  297.5 2.7 collective-permute-start.41
  303.5 2.0 collective-permute-start.43
  306.7 3.7 fusion.64
  311.6 8.9 %collective-permute-done.44 = bf16[160,768]{1,0:T(8,128)(2,1)S(1)} collective-permute-done((bf16[160,768]{1,0:T(8,128)(2,1)S(1)}, bf16[160,768]{1,0:T(8,128)(2,1)S(1)}, u32[]{:S(2)}, u32[]{:S(2)}) %collective-permute-start.44) | collective-permute-done | bytes 245792 | tf_op jit(solution)/shard_map/ppermute | solution.py:63
  321.1 13.0 %collective-permute-done.43 = bf16[160,768]{1,0:T(8,128)(2,1)S(1)} collective-permute-done((bf16[160,768]{1,0:T(8,128)(2,1)S(1)}, bf16[160,768]{1,0:T(8,128)(2,1)S(1)}, u32[]{:S(2)}, u32[]{:S(2)}) %collective-permute-start.43) | collective-permute-done | bytes 245792 | tf_op jit(solution)/shard_map/ppermute | solution.py:63
  334.7 2.6 fusion.100
  338.6 2.4 pad_maximum_fusion
  341.0 6.4 %copy.163 = f32[1536,768]{1,0:T(8,128)} copy(f32[1536,768]{0,1:T(8,128)} %pad_maximum_fusion) | data formatting | bytes 9437184 | tf_op jit(solution)/shard_map/concatenate | solution.py:327
  347.4 2.8 fusion.30
  353.2 2.5 bitcast_add_fusion.3
  356.7 3.6 collective-permute-start.30
  365.4 5.2 %fusion.1 = bf16[4,192,1536]{2,1,0:T(8,128)(2,1)} fusion(bf16[4,192,1536]{2,1,0:T(8,128)(2,1)} %collective-permute-done.65, f32[4,2,192,1536]{3,2,1,0:T(8,128)} %bitcast.325, s32[]{:T(128)S(6)} %select_n.436), kind=kLoop, calls=%fused_computation.9 | loop fusion | flops 3538944 | bytes 9437188 | tf_op jit(solution)/shard_map/convert_element_type | solution.py:279
  374.3 4.7 collective-permute-start.47
  379.8 3.8 bitcast_add_fusion.1
  386.4 15.4 %collective-permute-start.32 = (bf16[4,48,768]{2,1,0:T(8,128)(2,1)S(1)}, bf16[4,48,768]{2,1,0:T(8,128)(2,1)S(1)}, u32[]{:S(2)}, u32[]{:S(2)}) collective-permute-start(bf16[4,48,768]{2,1,0:T(8,128)(2,1)S(1)} %get-tuple-element.46), channel_id=1, source_target_pairs={{0,8},{1,9},{2,10},{3,11},{4,12},{5,13},{6,14},{7,15},{8,16},{9,17... | collective-permute-start | bytes 884744 | tf_op jit(solution)/shard_map/ppermute | solution.py:74
  402.0 3.9 collective-permute-start.56
  409.5 19.4 %collective-permute-start.48 = (bf16[4,48,768]{2,1,0:T(8,128)(2,1)S(1)}, bf16[4,48,768]{2,1,0:T(8,128)(2,1)S(1)}, u32[]{:S(2)}, u32[]{:S(2)}) collective-permute-start(bf16[4,48,768]{2,1,0:T(8,128)(2,1)S(1)} %get-tuple-element.40), channel_id=1, source_target_pairs={{0,8},{1,9},{2,10},{3,11},{4,12},{5,13},{6,14},{7,15},{8,16},{9,17... | collective-permute-start | bytes 884744 | tf_op jit(solution)/shard_map/ppermute | solution.py:74
  429.0 2.4 collective-permute-start.36
  432.0 17.1 %collective-permute-done.48 = bf16[4,48,768]{2,1,0:T(8,128)(2,1)S(1)} collective-permute-done((bf16[4,48,768]{2,1,0:T(8,128)(2,1)S(1)}, bf16[4,48,768]{2,1,0:T(8,128)(2,1)S(1)}, u32[]{:S(2)}, u32[]{:S(2)}) %collective-permute-start.48) | collective-permute-done | bytes 294944 | tf_op jit(solution)/shard_map/ppermute | solution.py:74
  458.2 4.4 collective-permute-start.57
  464.1 5.9 %collective-permute-done.57 = bf16[4,48,1536]{2,1,0:T(8,128)(2,1)S(1)} collective-permute-done((bf16[4,48,1536]{2,1,0:T(8,128)(2,1)S(1)}, bf16[4,48,1536]{2,1,0:T(8,128)(2,1)S(1)}, u32[]{:S(2)}, u32[]{:S(2)}) %collective-permute-start.57) | collective-permute-done | bytes 589856 | tf_op jit(solution)/shard_map/ppermute | solution.py:74
  471.6 13.9 %collective-permute-start.58 = (bf16[4,48,1536]{2,1,0:T(8,128)(2,1)S(1)}, bf16[4,48,1536]{2,1,0:T(8,128)(2,1)S(1)}, u32[]{:S(2)}, u32[]{:S(2)}) collective-permute-start(bf16[4,48,1536]{2,1,0:T(8,128)(2,1)S(1)} %get-tuple-element.30), channel_id=1, source_target_pairs={{0,8},{1,9},{2,10},{3,11},{4,12},{5,13},{6,14},{7,15},{8,16},{9,17... | collective-permute-start | bytes 1769480 | tf_op jit(solution)/shard_map/ppermute | solution.py:74
  487.0 4.4 collective-permute-done.61
  497.5 1.9 collective-permute-done.62
  503.8 2.2 bitcast_convert_fusion.1
  (400 shorter events, 133.8 us)
Async XLA Ops:
  10.2 28.7 %collective-permute-start.3 = (bf16[48,1536]{1,0:T(8,128)(2,1)}, bf16[48,1536]{1,0:T(8,128)(2,1)}, u32[]{:S(2)}, u32[]{:S(2)}) collective-permute-start(bf16[48,1536]{1,0:T(8,128)(2,1)} %get-tuple-element.88), channel_id=1, source_target_pairs={{0,6},{1,7},{2,4},{3,5},{4,2},{5,3},{6,0},{7,1},{8,14},{9,15},{10,... | collective-permute-start | bytes 442376 | tf_op jit(solution)/shard_map/ppermute | solution.py:63
  14.1 24.8 %collective-permute-start.4 = (bf16[48,1536]{1,0:T(8,128)(2,1)}, bf16[48,1536]{1,0:T(8,128)(2,1)}, u32[]{:S(2)}, u32[]{:S(2)}) collective-permute-start(bf16[48,1536]{1,0:T(8,128)(2,1)} %get-tuple-element.87), channel_id=1, source_target_pairs={{0,4},{1,5},{2,6},{3,7},{4,0},{5,1},{6,2},{7,3},{8,12},{9,13},{10,... | collective-permute-start | bytes 442376 | tf_op jit(solution)/shard_map/ppermute | solution.py:63
  14.6 24.3 %collective-permute-start.5 = (bf16[48,1536]{1,0:T(8,128)(2,1)}, bf16[48,1536]{1,0:T(8,128)(2,1)}, u32[]{:S(2)}, u32[]{:S(2)}) collective-permute-start(bf16[48,1536]{1,0:T(8,128)(2,1)} %get-tuple-element.86), channel_id=1, source_target_pairs={{0,2},{1,3},{2,0},{3,1},{4,6},{5,7},{6,4},{7,5},{8,10},{9,11},{10,... | collective-permute-start | bytes 442376 | tf_op jit(solution)/shard_map/ppermute | solution.py:63
  40.1 16.6 %collective-permute-start.6 = (bf16[192,1536]{1,0:T(8,128)(2,1)S(1)}, bf16[192,1536]{1,0:T(8,128)(2,1)}, u32[]{:S(2)}, u32[]{:S(2)}) collective-permute-start(bf16[192,1536]{1,0:T(8,128)(2,1)S(1)} %pad_maximum_fusion.6), channel_id=1, source_target_pairs={{8,0},{9,1},{10,2},{11,3},{12,4},{13,5},{14,6},{15,7},{16,8},{17,9... | collective-permute-start | bytes 1769480 | tf_op jit(solution)/shard_map/ppermute | solution.py:74
  41.5 21.6 %collective-permute-start.7 = (bf16[192,1536]{1,0:T(8,128)(2,1)S(1)}, bf16[192,1536]{1,0:T(8,128)(2,1)}, u32[]{:S(2)}, u32[]{:S(2)}) collective-permute-start(bf16[192,1536]{1,0:T(8,128)(2,1)S(1)} %pad_maximum_fusion.6), channel_id=1, source_target_pairs={{0,8},{1,9},{2,10},{3,11},{4,12},{5,13},{6,14},{7,15},{8,16},{9,17... | collective-permute-start | bytes 1769480 | tf_op jit(solution)/shard_map/ppermute | solution.py:74
  56.7 22.1 %collective-permute-start.10 = (bf16[192,1536]{1,0:T(8,128)(2,1)}, bf16[192,1536]{1,0:T(8,128)(2,1)}, u32[]{:S(2)}, u32[]{:S(2)}) collective-permute-start(bf16[192,1536]{1,0:T(8,128)(2,1)} %collective-permute-done.6), channel_id=1, source_target_pairs={{8,0},{9,1},{10,2},{11,3},{12,4},{13,5},{14,6},{15,7},{16,8},{17,9... | collective-permute-start | bytes 1769480 | tf_op jit(solution)/shard_map/ppermute | solution.py:74
  58.9 80.2 %collective-permute-start.2 = (bf16[160,1536]{1,0:T(8,128)(2,1)}, bf16[160,1536]{1,0:T(8,128)(2,1)}, u32[]{:S(2)}, u32[]{:S(2)}) collective-permute-start(bf16[160,1536]{1,0:T(8,128)(2,1)} %fusion.87), channel_id=1, source_target_pairs={{0,6},{1,7},{2,4},{3,5},{4,2},{5,3},{6,0},{7,1},{8,14},{9,15},{10,... | collective-permute-start | bytes 1474568 | tf_op jit(solution)/shard_map/ppermute | solution.py:63
  61.5 80.3 %collective-permute-start.1 = (bf16[160,1536]{1,0:T(8,128)(2,1)}, bf16[160,1536]{1,0:T(8,128)(2,1)}, u32[]{:S(2)}, u32[]{:S(2)}) collective-permute-start(bf16[160,1536]{1,0:T(8,128)(2,1)} %fusion.87), channel_id=1, source_target_pairs={{0,4},{1,5},{2,6},{3,7},{4,0},{5,1},{6,2},{7,3},{8,12},{9,13},{10,... | collective-permute-start | bytes 1474568 | tf_op jit(solution)/shard_map/ppermute | solution.py:63
  62.0 80.3 %collective-permute-start = (bf16[160,1536]{1,0:T(8,128)(2,1)}, bf16[160,1536]{1,0:T(8,128)(2,1)}, u32[]{:S(2)}, u32[]{:S(2)}) collective-permute-start(bf16[160,1536]{1,0:T(8,128)(2,1)} %fusion.87), channel_id=1, source_target_pairs={{0,2},{1,3},{2,0},{3,1},{4,6},{5,7},{6,4},{7,5},{8,10},{9,11},{10,... | collective-permute-start | bytes 1474568 | tf_op jit(solution)/shard_map/ppermute | solution.py:63
  63.1 19.5 %collective-permute-start.8 = (bf16[192,1536]{1,0:T(8,128)(2,1)}, bf16[192,1536]{1,0:T(8,128)(2,1)}, u32[]{:S(2)}, u32[]{:S(2)}) collective-permute-start(bf16[192,1536]{1,0:T(8,128)(2,1)} %collective-permute-done.7), channel_id=1, source_target_pairs={{8,16},{9,17},{10,18},{11,19},{12,20},{13,21},{14,22},{15,23},{16,... | collective-permute-start | bytes 1769480 | tf_op jit(solution)/shard_map/ppermute | solution.py:74
  69.3 48.5 %all-to-all-start = ((f32[32,1,256]{2,1,0:T(1,128)}), f32[32,1,256]{2,1,0:T(1,128)}, u32[]{:S(2)}, u32[]{:S(2)}) async-start(f32[32,1,256]{2,1,0:T(1,128)} %broadcast_in_dim.46), calls=%async_computation | async-start | bytes 65536 | tf_op jit(solution)/shard_map/all_to_all | solution.py:188
  78.1 56.5 %all-gather.3.cloned.1.call-start = ((), (), s32[]{:S(2)}) async-start(), calls=%async_computation.4 | async-start | bytes 2949120 | tf_op jit(solution)/shard_map/all_gather | solution.py:211
  78.8 29.4 %collective-permute-start.11 = (bf16[192,1536]{1,0:T(8,128)(2,1)}, bf16[192,1536]{1,0:T(8,128)(2,1)}, u32[]{:S(2)}, u32[]{:S(2)}) collective-permute-start(bf16[192,1536]{1,0:T(8,128)(2,1)} %collective-permute-done.10), channel_id=1, source_target_pairs={{8,0},{9,1},{10,2},{11,3},{12,4},{13,5},{14,6},{15,7}} | collective-permute-start | bytes 1769480 | tf_op jit(solution)/shard_map/ppermute | solution.py:74
  82.6 29.7 %collective-permute-start.9 = (bf16[192,1536]{1,0:T(8,128)(2,1)}, bf16[192,1536]{1,0:T(8,128)(2,1)S(1)}, u32[]{:S(2)}, u32[]{:S(2)}) collective-permute-start(bf16[192,1536]{1,0:T(8,128)(2,1)} %collective-permute-done.8), channel_id=1, source_target_pairs={{16,24},{17,25},{18,26},{19,27},{20,28},{21,29},{22,30},{23,31}} | collective-permute-start | bytes 1769480 | tf_op jit(solution)/shard_map/ppermute | solution.py:74
  108.2 186.6 %collective-permute-start.25 = (bf16[160,1536]{1,0:T(8,128)(2,1)}, bf16[160,1536]{1,0:T(8,128)(2,1)}, u32[]{:S(2)}, u32[]{:S(2)}) collective-permute-start(bf16[160,1536]{1,0:T(8,128)(2,1)} %fusion.86), channel_id=1, source_target_pairs={{0,6},{1,7},{2,4},{3,5},{4,2},{5,3},{6,0},{7,1},{8,14},{9,15},{10,... | collective-permute-start | bytes 1474568 | tf_op jit(solution)/shard_map/ppermute | solution.py:63
  115.4 19.2 %collective-permute-start.12 = (bf16[4,4,48,1536]{3,2,1,0:T(8,128)(2,1)}, bf16[4,4,48,1536]{3,2,1,0:T(8,128)(2,1)}, u32[]{:S(2)}, u32[]{:S(2)}) collective-permute-start(bf16[4,4,48,1536]{3,2,1,0:T(8,128)(2,1)} %pad_maximum_fusion.1), channel_id=1, source_target_pairs={{0,1},{1,0},{2,3},{3,2},{4,5},{5,4},{6,7},{7,6},{8,9},{9,8},{10,11... | collective-permute-start | bytes 7077896 | tf_op jit(solution)/shard_map/ppermute | solution.py:63
  134.6 36.5 %collective-permute-start.13 = (bf16[4,192,1536]{2,1,0:T(8,128)(2,1)}, bf16[4,192,1536]{2,1,0:T(8,128)(2,1)S(1)}, u32[]{:S(2)}, u32[]{:S(2)}) collective-permute-start(bf16[4,192,1536]{2,1,0:T(8,128)(2,1)} %bitcast.334), channel_id=1, source_target_pairs={{0,1},{1,0},{2,3},{3,2},{4,5},{5,4},{6,7},{7,6},{8,9},{9,8},{10,11... | collective-permute-start | bytes 7077896 | tf_op jit(solution)/shard_map/ppermute | solution.py:63
  139.2 15.0 %collective-permute-start.19 = (bf16[160,1536]{1,0:T(8,128)(2,1)S(1)}, bf16[160,1536]{1,0:T(8,128)(2,1)S(1)}, u32[]{:S(2)}, u32[]{:S(2)}) collective-permute-start(bf16[160,1536]{1,0:T(8,128)(2,1)S(1)} %copy-done.28), channel_id=1, source_target_pairs={{0,6},{1,7},{2,4},{3,5},{4,2},{5,3},{6,0},{7,1},{8,14},{9,15},{10,... | collective-permute-start | bytes 1474568 | tf_op jit(solution)/shard_map/ppermute | solution.py:63
  141.8 22.5 %collective-permute-start.18 = (bf16[160,1536]{1,0:T(8,128)(2,1)S(1)}, bf16[160,1536]{1,0:T(8,128)(2,1)S(1)}, u32[]{:S(2)}, u32[]{:S(2)}) collective-permute-start(bf16[160,1536]{1,0:T(8,128)(2,1)S(1)} %copy-done.28), channel_id=1, source_target_pairs={{0,4},{1,5},{2,6},{3,7},{4,0},{5,1},{6,2},{7,3},{8,12},{9,13},{10,... | collective-permute-start | bytes 1474568 | tf_op jit(solution)/shard_map/ppermute | solution.py:63
  142.4 22.1 %collective-permute-start.17 = (bf16[160,1536]{1,0:T(8,128)(2,1)S(1)}, bf16[160,1536]{1,0:T(8,128)(2,1)S(1)}, u32[]{:S(2)}, u32[]{:S(2)}) collective-permute-start(bf16[160,1536]{1,0:T(8,128)(2,1)S(1)} %copy-done.28), channel_id=1, source_target_pairs={{0,2},{1,3},{2,0},{3,1},{4,6},{5,7},{6,4},{7,5},{8,10},{9,11},{10,... | collective-permute-start | bytes 1474568 | tf_op jit(solution)/shard_map/ppermute | solution.py:63
  154.2 143.2 %collective-permute-start.24 = (bf16[160,1536]{1,0:T(8,128)(2,1)}, bf16[160,1536]{1,0:T(8,128)(2,1)}, u32[]{:S(2)}, u32[]{:S(2)}) collective-permute-start(bf16[160,1536]{1,0:T(8,128)(2,1)} %fusion.86), channel_id=1, source_target_pairs={{0,4},{1,5},{2,6},{3,7},{4,0},{5,1},{6,2},{7,3},{8,12},{9,13},{10,... | collective-permute-start | bytes 1474568 | tf_op jit(solution)/shard_map/ppermute | solution.py:63
  194.2 15.7 %collective-permute-start.22 = (bf16[160,1536]{1,0:T(8,128)(2,1)}, bf16[160,1536]{1,0:T(8,128)(2,1)}, u32[]{:S(2)}, u32[]{:S(2)}) collective-permute-start(bf16[160,1536]{1,0:T(8,128)(2,1)} %get-tuple-element.53), channel_id=1, source_target_pairs={{0,6},{1,7},{2,4},{3,5},{4,2},{5,3},{6,0},{7,1},{8,14},{9,15},{10,... | collective-permute-start | bytes 1474568 | tf_op jit(solution)/shard_map/ppermute | solution.py:63
  196.4 23.6 %collective-permute-start.21 = (bf16[160,1536]{1,0:T(8,128)(2,1)}, bf16[160,1536]{1,0:T(8,128)(2,1)}, u32[]{:S(2)}, u32[]{:S(2)}) collective-permute-start(bf16[160,1536]{1,0:T(8,128)(2,1)} %get-tuple-element.54), channel_id=1, source_target_pairs={{0,4},{1,5},{2,6},{3,7},{4,0},{5,1},{6,2},{7,3},{8,12},{9,13},{10,... | collective-permute-start | bytes 1474568 | tf_op jit(solution)/shard_map/ppermute | solution.py:63
  197.1 24.3 %collective-permute-start.20 = (bf16[160,1536]{1,0:T(8,128)(2,1)}, bf16[160,1536]{1,0:T(8,128)(2,1)}, u32[]{:S(2)}, u32[]{:S(2)}) collective-permute-start(bf16[160,1536]{1,0:T(8,128)(2,1)} %get-tuple-element.52), channel_id=1, source_target_pairs={{0,2},{1,3},{2,0},{3,1},{4,6},{5,7},{6,4},{7,5},{8,10},{9,11},{10,... | collective-permute-start | bytes 1474568 | tf_op jit(solution)/shard_map/ppermute | solution.py:63
  209.9 20.6 %collective-permute-start.16 = (bf16[160,1536]{1,0:T(8,128)(2,1)S(1)}, bf16[160,1536]{1,0:T(8,128)(2,1)S(1)}, u32[]{:S(2)}, u32[]{:S(2)}) collective-permute-start(bf16[160,1536]{1,0:T(8,128)(2,1)S(1)} %get-tuple-element.56), channel_id=1, source_target_pairs={{0,6},{1,7},{2,4},{3,5},{4,2},{5,3},{6,0},{7,1},{8,14},{9,15},{10,... | collective-permute-start | bytes 1474568 | tf_op jit(solution)/shard_map/ppermute | solution.py:63
  220.0 19.9 %collective-permute-start.15 = (bf16[160,1536]{1,0:T(8,128)(2,1)S(1)}, bf16[160,1536]{1,0:T(8,128)(2,1)S(1)}, u32[]{:S(2)}, u32[]{:S(2)}) collective-permute-start(bf16[160,1536]{1,0:T(8,128)(2,1)S(1)} %get-tuple-element.57), channel_id=1, source_target_pairs={{0,4},{1,5},{2,6},{3,7},{4,0},{5,1},{6,2},{7,3},{8,12},{9,13},{10,... | collective-permute-start | bytes 1474568 | tf_op jit(solution)/shard_map/ppermute | solution.py:63
  221.5 19.6 %collective-permute-start.14 = (bf16[160,1536]{1,0:T(8,128)(2,1)S(1)}, bf16[160,1536]{1,0:T(8,128)(2,1)S(1)}, u32[]{:S(2)}, u32[]{:S(2)}) collective-permute-start(bf16[160,1536]{1,0:T(8,128)(2,1)S(1)} %get-tuple-element.55), channel_id=1, source_target_pairs={{0,2},{1,3},{2,0},{3,1},{4,6},{5,7},{6,4},{7,5},{8,10},{9,11},{10,... | collective-permute-start | bytes 1474568 | tf_op jit(solution)/shard_map/ppermute | solution.py:63
  230.5 69.6 %collective-permute-start.23 = (bf16[160,1536]{1,0:T(8,128)(2,1)}, bf16[160,1536]{1,0:T(8,128)(2,1)}, u32[]{:S(2)}, u32[]{:S(2)}) collective-permute-start(bf16[160,1536]{1,0:T(8,128)(2,1)} %fusion.86), channel_id=1, source_target_pairs={{0,2},{1,3},{2,0},{3,1},{4,6},{5,7},{6,4},{7,5},{8,10},{9,11},{10,... | collective-permute-start | bytes 1474568 | tf_op jit(solution)/shard_map/ppermute | solution.py:63
  267.2 84.7 %all-to-all-start.1 = ((f32[32,1,512]{2,1,0:T(1,128)}), f32[32,1,512]{2,1,0:T(1,128)S(1)}, u32[]{:S(2)}, u32[]{:S(2)}) async-start(f32[32,1,512]{2,1,0:T(1,128)} %broadcast_in_dim.52), calls=%async_computation.1 | async-start | bytes 131072 | tf_op jit(solution)/shard_map/all_to_all | solution.py:345
  278.5 225.3 %reduce-scatter.2.cloned.1.call-start = ((), (), s32[]{:S(2)}) async-start(), calls=%async_computation.3 | async-start | bytes 2949120 | tf_op jit(solution)/shard_map/reduce_scatter | solution.py:280
  288.0 12.7 %collective-permute-start.28 = (bf16[160,768]{1,0:T(8,128)(2,1)}, bf16[160,768]{1,0:T(8,128)(2,1)}, u32[]{:S(2)}, u32[]{:S(2)}) collective-permute-start(bf16[160,768]{1,0:T(8,128)(2,1)} %bitcast.299), channel_id=1, source_target_pairs={{0,6},{1,7},{2,4},{3,5},{4,2},{5,3},{6,0},{7,1},{8,14},{9,15},{10,... | collective-permute-start | bytes 737288 | tf_op jit(solution)/shard_map/ppermute | solution.py:63
  291.4 12.1 %collective-permute-start.27 = (bf16[160,768]{1,0:T(8,128)(2,1)}, bf16[160,768]{1,0:T(8,128)(2,1)}, u32[]{:S(2)}, u32[]{:S(2)}) collective-permute-start(bf16[160,768]{1,0:T(8,128)(2,1)} %bitcast.300), channel_id=1, source_target_pairs={{0,4},{1,5},{2,6},{3,7},{4,0},{5,1},{6,2},{7,3},{8,12},{9,13},{10,... | collective-permute-start | bytes 737288 | tf_op jit(solution)/shard_map/ppermute | solution.py:63
  294.9 10.6 %collective-permute-start.26 = (bf16[160,768]{1,0:T(8,128)(2,1)S(1)}, bf16[160,768]{1,0:T(8,128)(2,1)S(1)}, u32[]{:S(2)}, u32[]{:S(2)}) collective-permute-start(bf16[160,768]{1,0:T(8,128)(2,1)S(1)} %bitcast.346), channel_id=1, source_target_pairs={{0,2},{1,3},{2,0},{3,1},{4,6},{5,7},{6,4},{7,5},{8,10},{9,11},{10,... | collective-permute-start | bytes 737288 | tf_op jit(solution)/shard_map/ppermute | solution.py:63
  297.5 39.9 %collective-permute-start.41 = (bf16[160,1536]{1,0:T(8,128)(2,1)S(1)}, bf16[160,1536]{1,0:T(8,128)(2,1)S(1)}, u32[]{:S(2)}, u32[]{:S(2)}) collective-permute-start(bf16[160,1536]{1,0:T(8,128)(2,1)S(1)} %copy-done.27), channel_id=1, source_target_pairs={{0,6},{1,7},{2,4},{3,5},{4,2},{5,3},{6,0},{7,1},{8,14},{9,15},{10,... | collective-permute-start | bytes 1474568 | tf_op jit(solution)/shard_map/ppermute | solution.py:63
  300.2 37.2 %collective-permute-start.40 = (bf16[160,1536]{1,0:T(8,128)(2,1)S(1)}, bf16[160,1536]{1,0:T(8,128)(2,1)S(1)}, u32[]{:S(2)}, u32[]{:S(2)}) collective-permute-start(bf16[160,1536]{1,0:T(8,128)(2,1)S(1)} %copy-done.27), channel_id=1, source_target_pairs={{0,4},{1,5},{2,6},{3,7},{4,0},{5,1},{6,2},{7,3},{8,12},{9,13},{10,... | collective-permute-start | bytes 1474568 | tf_op jit(solution)/shard_map/ppermute | solution.py:63
  300.8 19.8 %collective-permute-start.44 = (bf16[160,768]{1,0:T(8,128)(2,1)S(1)}, bf16[160,768]{1,0:T(8,128)(2,1)S(1)}, u32[]{:S(2)}, u32[]{:S(2)}) collective-permute-start(bf16[160,768]{1,0:T(8,128)(2,1)S(1)} %bitcast.350), channel_id=1, source_target_pairs={{0,6},{1,7},{2,4},{3,5},{4,2},{5,3},{6,0},{7,1},{8,14},{9,15},{10,... | collective-permute-start | bytes 737288 | tf_op jit(solution)/shard_map/ppermute | solution.py:63
  303.5 30.6 %collective-permute-start.43 = (bf16[160,768]{1,0:T(8,128)(2,1)S(1)}, bf16[160,768]{1,0:T(8,128)(2,1)S(1)}, u32[]{:S(2)}, u32[]{:S(2)}) collective-permute-start(bf16[160,768]{1,0:T(8,128)(2,1)S(1)} %bitcast.348), channel_id=1, source_target_pairs={{0,4},{1,5},{2,6},{3,7},{4,0},{5,1},{6,2},{7,3},{8,12},{9,13},{10,... | collective-permute-start | bytes 737288 | tf_op jit(solution)/shard_map/ppermute | solution.py:63
  305.5 28.7 %collective-permute-start.42 = (bf16[160,768]{1,0:T(8,128)(2,1)S(1)}, bf16[160,768]{1,0:T(8,128)(2,1)S(1)}, u32[]{:S(2)}, u32[]{:S(2)}) collective-permute-start(bf16[160,768]{1,0:T(8,128)(2,1)S(1)} %bitcast.347), channel_id=1, source_target_pairs={{0,2},{1,3},{2,0},{3,1},{4,6},{5,7},{6,4},{7,5},{8,10},{9,11},{10,... | collective-permute-start | bytes 737288 | tf_op jit(solution)/shard_map/ppermute | solution.py:63
  320.6 16.9 %collective-permute-start.39 = (bf16[160,1536]{1,0:T(8,128)(2,1)S(1)}, bf16[160,1536]{1,0:T(8,128)(2,1)S(1)}, u32[]{:S(2)}, u32[]{:S(2)}) collective-permute-start(bf16[160,1536]{1,0:T(8,128)(2,1)S(1)} %copy-done.27), channel_id=1, source_target_pairs={{0,2},{1,3},{2,0},{3,1},{4,6},{5,7},{6,4},{7,5},{8,10},{9,11},{10,... | collective-permute-start | bytes 1474568 | tf_op jit(solution)/shard_map/ppermute | solution.py:63
  334.1 30.6 %collective-permute-start.65 = (bf16[4,192,1536]{2,1,0:T(8,128)(2,1)}, bf16[4,192,1536]{2,1,0:T(8,128)(2,1)}, u32[]{:S(2)}, u32[]{:S(2)}) collective-permute-start(bf16[4,192,1536]{2,1,0:T(8,128)(2,1)} %fusion.11), channel_id=1, source_target_pairs={{0,1},{1,0},{2,3},{3,2},{4,5},{5,4},{6,7},{7,6},{8,9},{9,8},{10,11... | collective-permute-start | bytes 7077896 | tf_op jit(solution)/shard_map/ppermute | solution.py:63
  334.1 45.6 %collective-permute-start.55 = (bf16[4,4,48,1536]{3,2,1,0:T(8,128)(2,1)}, bf16[4,4,48,1536]{3,2,1,0:T(8,128)(2,1)}, u32[]{:S(2)}, u32[]{:S(2)}) collective-permute-start(bf16[4,4,48,1536]{3,2,1,0:T(8,128)(2,1)} %fusion.10), channel_id=1, source_target_pairs={{0,1},{1,0},{2,3},{3,2},{4,5},{5,4},{6,7},{7,6},{8,9},{9,8},{10,11... | collective-permute-start | bytes 7077896 | tf_op jit(solution)/shard_map/ppermute | solution.py:63
  337.3 15.9 %collective-permute-start.29 = (bf16[4,4,48,768]{3,2,1,0:T(8,128)(2,1)}, bf16[4,4,48,768]{3,2,1,0:T(8,128)(2,1)}, u32[]{:S(2)}, u32[]{:S(2)}) collective-permute-start(bf16[4,4,48,768]{3,2,1,0:T(8,128)(2,1)} %fusion.29), channel_id=1, source_target_pairs={{0,1},{1,0},{2,3},{3,2},{4,5},{5,4},{6,7},{7,6},{8,9},{9,8},{10,11... | collective-permute-start | bytes 3538952 | tf_op jit(solution)/shard_map/ppermute | solution.py:63
  350.2 10.8 %collective-permute-start.45 = (bf16[4,4,48,768]{3,2,1,0:T(8,128)(2,1)}, bf16[4,4,48,768]{3,2,1,0:T(8,128)(2,1)}, u32[]{:S(2)}, u32[]{:S(2)}) collective-permute-start(bf16[4,4,48,768]{3,2,1,0:T(8,128)(2,1)} %fusion.30), channel_id=1, source_target_pairs={{0,1},{1,0},{2,3},{3,2},{4,5},{5,4},{6,7},{7,6},{8,9},{9,8},{10,11... | collective-permute-start | bytes 3538952 | tf_op jit(solution)/shard_map/ppermute | solution.py:63
  356.7 14.0 %collective-permute-start.30 = (bf16[4,48,768]{2,1,0:T(8,128)(2,1)}, bf16[4,48,768]{2,1,0:T(8,128)(2,1)S(1)}, u32[]{:S(2)}, u32[]{:S(2)}) collective-permute-start(bf16[4,48,768]{2,1,0:T(8,128)(2,1)} %get-tuple-element.50), channel_id=1, source_target_pairs={{0,8},{1,9},{2,10},{3,11},{4,12},{5,13},{6,14},{7,15}} | collective-permute-start | bytes 884744 | tf_op jit(solution)/shard_map/ppermute | solution.py:74
  360.3 10.4 %collective-permute-start.33 = (bf16[4,48,768]{2,1,0:T(8,128)(2,1)}, bf16[4,48,768]{2,1,0:T(8,128)(2,1)S(1)}, u32[]{:S(2)}, u32[]{:S(2)}) collective-permute-start(bf16[4,48,768]{2,1,0:T(8,128)(2,1)} %get-tuple-element.51), channel_id=1, source_target_pairs={{24,16},{25,17},{26,18},{27,19},{28,20},{29,21},{30,22},{31,23}} | collective-permute-start | bytes 884744 | tf_op jit(solution)/shard_map/ppermute | solution.py:74
  363.4 10.7 %collective-permute-start.46 = (bf16[4,48,768]{2,1,0:T(8,128)(2,1)}, bf16[4,48,768]{2,1,0:T(8,128)(2,1)S(1)}, u32[]{:S(2)}, u32[]{:S(2)}) collective-permute-start(bf16[4,48,768]{2,1,0:T(8,128)(2,1)} %get-tuple-element.44), channel_id=1, source_target_pairs={{0,8},{1,9},{2,10},{3,11},{4,12},{5,13},{6,14},{7,15}} | collective-permute-start | bytes 884744 | tf_op jit(solution)/shard_map/ppermute | solution.py:74
  364.7 9.4 %collective-permute-start.49 = (bf16[4,48,768]{2,1,0:T(8,128)(2,1)}, bf16[4,48,768]{2,1,0:T(8,128)(2,1)S(1)}, u32[]{:S(2)}, u32[]{:S(2)}) collective-permute-start(bf16[4,48,768]{2,1,0:T(8,128)(2,1)} %get-tuple-element.45), channel_id=1, source_target_pairs={{24,16},{25,17},{26,18},{27,19},{28,20},{29,21},{30,22},{31,23}} | collective-permute-start | bytes 884744 | tf_op jit(solution)/shard_map/ppermute | solution.py:74
  371.9 13.1 %collective-permute-start.31 = (bf16[4,48,768]{2,1,0:T(8,128)(2,1)S(1)}, bf16[4,48,768]{2,1,0:T(8,128)(2,1)S(1)}, u32[]{:S(2)}, u32[]{:S(2)}) collective-permute-start(bf16[4,48,768]{2,1,0:T(8,128)(2,1)S(1)} %get-tuple-element.48), channel_id=1, source_target_pairs={{0,8},{1,9},{2,10},{3,11},{4,12},{5,13},{6,14},{7,15},{8,16},{9,17... | collective-permute-start | bytes 884744 | tf_op jit(solution)/shard_map/ppermute | solution.py:74
  373.4 11.5 %collective-permute-start.34 = (bf16[4,48,768]{2,1,0:T(8,128)(2,1)S(1)}, bf16[4,48,768]{2,1,0:T(8,128)(2,1)S(1)}, u32[]{:S(2)}, u32[]{:S(2)}) collective-permute-start(bf16[4,48,768]{2,1,0:T(8,128)(2,1)S(1)} %get-tuple-element.49), channel_id=1, source_target_pairs={{16,8},{17,9},{18,10},{19,11},{20,12},{21,13},{22,14},{23,15},{24,... | collective-permute-start | bytes 884744 | tf_op jit(solution)/shard_map/ppermute | solution.py:74
  374.3 31.7 %collective-permute-start.47 = (bf16[4,48,768]{2,1,0:T(8,128)(2,1)S(1)}, bf16[4,48,768]{2,1,0:T(8,128)(2,1)S(1)}, u32[]{:S(2)}, u32[]{:S(2)}) collective-permute-start(bf16[4,48,768]{2,1,0:T(8,128)(2,1)S(1)} %get-tuple-element.42), channel_id=1, source_target_pairs={{0,8},{1,9},{2,10},{3,11},{4,12},{5,13},{6,14},{7,15},{8,16},{9,17... | collective-permute-start | bytes 884744 | tf_op jit(solution)/shard_map/ppermute | solution.py:74
  378.9 27.7 %collective-permute-start.50 = (bf16[4,48,768]{2,1,0:T(8,128)(2,1)S(1)}, bf16[4,48,768]{2,1,0:T(8,128)(2,1)S(1)}, u32[]{:S(2)}, u32[]{:S(2)}) collective-permute-start(bf16[4,48,768]{2,1,0:T(8,128)(2,1)S(1)} %get-tuple-element.43), channel_id=1, source_target_pairs={{16,8},{17,9},{18,10},{19,11},{20,12},{21,13},{22,14},{23,15},{24,... | collective-permute-start | bytes 884744 | tf_op jit(solution)/shard_map/ppermute | solution.py:74
  385.1 24.4 %collective-permute-start.35 = (bf16[4,48,768]{2,1,0:T(8,128)(2,1)S(1)}, bf16[4,48,768]{2,1,0:T(8,128)(2,1)S(1)}, u32[]{:S(2)}, u32[]{:S(2)}) collective-permute-start(bf16[4,48,768]{2,1,0:T(8,128)(2,1)S(1)} %get-tuple-element.47), channel_id=1, source_target_pairs={{8,0},{9,1},{10,2},{11,3},{12,4},{13,5},{14,6},{15,7},{16,8},{17,9... | collective-permute-start | bytes 884744 | tf_op jit(solution)/shard_map/ppermute | solution.py:74
  386.4 42.5 %collective-permute-start.32 = (bf16[4,48,768]{2,1,0:T(8,128)(2,1)S(1)}, bf16[4,48,768]{2,1,0:T(8,128)(2,1)S(1)}, u32[]{:S(2)}, u32[]{:S(2)}) collective-permute-start(bf16[4,48,768]{2,1,0:T(8,128)(2,1)S(1)} %get-tuple-element.46), channel_id=1, source_target_pairs={{0,8},{1,9},{2,10},{3,11},{4,12},{5,13},{6,14},{7,15},{8,16},{9,17... | collective-permute-start | bytes 884744 | tf_op jit(solution)/shard_map/ppermute | solution.py:74
  402.0 55.9 %collective-permute-start.56 = (bf16[4,48,1536]{2,1,0:T(8,128)(2,1)S(1)}, bf16[4,48,1536]{2,1,0:T(8,128)(2,1)S(1)}, u32[]{:S(2)}, u32[]{:S(2)}) collective-permute-start(bf16[4,48,1536]{2,1,0:T(8,128)(2,1)S(1)} %get-tuple-element.34), channel_id=1, source_target_pairs={{0,8},{1,9},{2,10},{3,11},{4,12},{5,13},{6,14},{7,15}} | collective-permute-start | bytes 1769480 | tf_op jit(solution)/shard_map/ppermute | solution.py:74
  405.9 52.0 %collective-permute-start.59 = (bf16[4,48,1536]{2,1,0:T(8,128)(2,1)S(1)}, bf16[4,48,1536]{2,1,0:T(8,128)(2,1)S(1)}, u32[]{:S(2)}, u32[]{:S(2)}) collective-permute-start(bf16[4,48,1536]{2,1,0:T(8,128)(2,1)S(1)} %get-tuple-element.35), channel_id=1, source_target_pairs={{24,16},{25,17},{26,18},{27,19},{28,20},{29,21},{30,22},{31,23}} | collective-permute-start | bytes 1769480 | tf_op jit(solution)/shard_map/ppermute | solution.py:74
  406.8 24.6 %collective-permute-start.51 = (bf16[4,48,768]{2,1,0:T(8,128)(2,1)S(1)}, bf16[4,48,768]{2,1,0:T(8,128)(2,1)S(1)}, u32[]{:S(2)}, u32[]{:S(2)}) collective-permute-start(bf16[4,48,768]{2,1,0:T(8,128)(2,1)S(1)} %get-tuple-element.41), channel_id=1, source_target_pairs={{8,0},{9,1},{10,2},{11,3},{12,4},{13,5},{14,6},{15,7},{16,8},{17,9... | collective-permute-start | bytes 884744 | tf_op jit(solution)/shard_map/ppermute | solution.py:74
  409.5 39.7 %collective-permute-start.48 = (bf16[4,48,768]{2,1,0:T(8,128)(2,1)S(1)}, bf16[4,48,768]{2,1,0:T(8,128)(2,1)S(1)}, u32[]{:S(2)}, u32[]{:S(2)}) collective-permute-start(bf16[4,48,768]{2,1,0:T(8,128)(2,1)S(1)} %get-tuple-element.40), channel_id=1, source_target_pairs={{0,8},{1,9},{2,10},{3,11},{4,12},{5,13},{6,14},{7,15},{8,16},{9,17... | collective-permute-start | bytes 884744 | tf_op jit(solution)/shard_map/ppermute | solution.py:74
  429.0 21.7 %collective-permute-start.36 = (bf16[48,768]{1,0:T(8,128)(2,1)S(1)}, bf16[48,768]{1,0:T(8,128)(2,1)S(1)}, u32[]{:S(2)}, u32[]{:S(2)}) collective-permute-start(bf16[48,768]{1,0:T(8,128)(2,1)S(1)} %get-tuple-element.102), channel_id=1, source_target_pairs={{0,6},{1,7},{2,4},{3,5},{4,2},{5,3},{6,0},{7,1},{8,14},{9,15},{10,... | collective-permute-start | bytes 221192 | tf_op jit(solution)/shard_map/ppermute | solution.py:63
  431.5 20.8 %collective-permute-start.37 = (bf16[48,768]{1,0:T(8,128)(2,1)S(1)}, bf16[48,768]{1,0:T(8,128)(2,1)S(1)}, u32[]{:S(2)}, u32[]{:S(2)}) collective-permute-start(bf16[48,768]{1,0:T(8,128)(2,1)S(1)} %get-tuple-element.101), channel_id=1, source_target_pairs={{0,4},{1,5},{2,6},{3,7},{4,0},{5,1},{6,2},{7,3},{8,12},{9,13},{10,... | collective-permute-start | bytes 221192 | tf_op jit(solution)/shard_map/ppermute | solution.py:63
  458.2 11.8 %collective-permute-start.57 = (bf16[4,48,1536]{2,1,0:T(8,128)(2,1)S(1)}, bf16[4,48,1536]{2,1,0:T(8,128)(2,1)S(1)}, u32[]{:S(2)}, u32[]{:S(2)}) collective-permute-start(bf16[4,48,1536]{2,1,0:T(8,128)(2,1)S(1)} %get-tuple-element.32), channel_id=1, source_target_pairs={{0,8},{1,9},{2,10},{3,11},{4,12},{5,13},{6,14},{7,15},{8,16},{9,17... | collective-permute-start | bytes 1769480 | tf_op jit(solution)/shard_map/ppermute | solution.py:74
  462.6 7.3 %collective-permute-start.60 = (bf16[4,48,1536]{2,1,0:T(8,128)(2,1)S(1)}, bf16[4,48,1536]{2,1,0:T(8,128)(2,1)S(1)}, u32[]{:S(2)}, u32[]{:S(2)}) collective-permute-start(bf16[4,48,1536]{2,1,0:T(8,128)(2,1)S(1)} %get-tuple-element.33), channel_id=1, source_target_pairs={{16,8},{17,9},{18,10},{19,11},{20,12},{21,13},{22,14},{23,15},{24,... | collective-permute-start | bytes 1769480 | tf_op jit(solution)/shard_map/ppermute | solution.py:74
  470.3 21.1 %collective-permute-start.61 = (bf16[4,48,1536]{2,1,0:T(8,128)(2,1)S(1)}, bf16[4,48,1536]{2,1,0:T(8,128)(2,1)S(1)}, u32[]{:S(2)}, u32[]{:S(2)}) collective-permute-start(bf16[4,48,1536]{2,1,0:T(8,128)(2,1)S(1)} %get-tuple-element.31), channel_id=1, source_target_pairs={{8,0},{9,1},{10,2},{11,3},{12,4},{13,5},{14,6},{15,7},{16,8},{17,9... | collective-permute-start | bytes 1769480 | tf_op jit(solution)/shard_map/ppermute | solution.py:74
  471.6 21.2 %collective-permute-start.58 = (bf16[4,48,1536]{2,1,0:T(8,128)(2,1)S(1)}, bf16[4,48,1536]{2,1,0:T(8,128)(2,1)S(1)}, u32[]{:S(2)}, u32[]{:S(2)}) collective-permute-start(bf16[4,48,1536]{2,1,0:T(8,128)(2,1)S(1)} %get-tuple-element.30), channel_id=1, source_target_pairs={{0,8},{1,9},{2,10},{3,11},{4,12},{5,13},{6,14},{7,15},{8,16},{9,17... | collective-permute-start | bytes 1769480 | tf_op jit(solution)/shard_map/ppermute | solution.py:74
  494.5 6.3 %collective-permute-start.63 = (bf16[48,1536]{1,0:T(8,128)(2,1)S(1)}, bf16[48,1536]{1,0:T(8,128)(2,1)S(1)}, u32[]{:S(2)}, u32[]{:S(2)}) collective-permute-start(bf16[48,1536]{1,0:T(8,128)(2,1)S(1)} %get-tuple-element.84), channel_id=1, source_target_pairs={{0,4},{1,5},{2,6},{3,7},{4,0},{5,1},{6,2},{7,3},{8,12},{9,13},{10,... | collective-permute-start | bytes 442376 | tf_op jit(solution)/shard_map/ppermute | solution.py:63
  (72 other events, 804.9 us)
Sparse Core Ops, SparseCore 0:
  80.5 54.0 all-gather.2
  370.8 81.8 reduce-scatter.1

commit v3 on v2

v3 whole, which is shorter than its diff:
```python
import jax
import jax.numpy as jnp
import numpy as np
from jax import lax
from jax.experimental import pallas as pl
from jax.experimental.pallas import tpu as pltpu
from jax.sharding import PartitionSpec as P

HEAD_DIM = 128
LEVELS = 4
GROUP = 8
CHIPS = 4
EPSILON = 1e-05
NEGATIVE = -1e30
BF = jnp.bfloat16
F32 = jnp.float32
WIDE = 512
VMEM_BYTES = 56 * 1024 * 1024


def dot(left, right, dims=((1,), (0,))):
    return lax.dot_general(left, right, (dims, ((), ())), preferred_element_type=F32)


def dot_t(left, right):
    return dot(left, right, ((1,), (1,)))


def t_dot(left, right):
    return dot(left, right, ((0,), (0,)))


def rope_tables(length):
    half = HEAD_DIM // 2
    rates = (10000.0 ** (-(np.arange(half, dtype=np.float64) * 2.0 / HEAD_DIM))).astype(np.float32)
    angles = np.arange(length, dtype=np.float32)[:, None] * rates[None, :]
    cosine, sine = np.cos(angles).astype(np.float32), np.sin(angles).astype(np.float32)
    return np.concatenate([cosine, cosine], axis=1), np.concatenate([-sine, sine], axis=1)


def norm_stats(values):
    center = values - jnp.mean(values, axis=-1, keepdims=True)
    inverse = lax.rsqrt(jnp.mean(center * center, axis=-1, keepdims=True) + EPSILON)
    return center * inverse, inverse


def norm_back(incoming, gain, normal, inverse):
    scaled = incoming * gain
    part = inverse * (
        scaled
        - jnp.mean(scaled, axis=-1, keepdims=True)
        - normal * jnp.mean(scaled * normal, axis=-1, keepdims=True)
    )
    return part, jnp.sum(incoming * normal, axis=0, keepdims=True), jnp.sum(incoming, axis=0, keepdims=True)


def swap(value, bit):
    count = lax.axis_size("dp")
    return lax.ppermute(value, "dp", [(i, i ^ bit) for i in range(count)])


def hop(value, step, near, far):
    groups = lax.axis_size("dp") // GROUP
    pairs = [
        (z * GROUP + t, (z + step) * GROUP + t)
        for z in range(max(near, 0), min(far, groups))
        if 0 <= z + step < groups
        for t in range(GROUP)
    ]
    return lax.ppermute(value, "dp", pairs)


def sum_all(value):
    bit = 1
    while bit < lax.axis_size("dp"):
        value = value + swap(value, bit)
        bit *= 2
    return value


def lines():
    groups = lax.axis_size("dp") // GROUP
    return [[z * GROUP + t for z in range(groups)] for t in range(GROUP)]


def spread(own):
    return [own, swap(own, 2), swap(own, 4), swap(own, 6)]


def gather_sum(parts):
    total = parts[0].astype(F32)
    for j in (1, 2, 3):
        total = total + swap(parts[j].astype(BF), 2 * j).astype(F32)
    return total


def exchange(chunks):
    chip = lax.axis_index("dp") % GROUP // 2
    got = []
    for j in range(CHIPS):
        chunk = lax.dynamic_index_in_dim(chunks, chip ^ j, 0, keepdims=False)
        got.append(chunk if j == 0 else swap(chunk, 2 * j))
    return got


def in_order(slots):
    chip = lax.axis_index("dp") % GROUP // 2
    odd, high = chip % 2 == 1, chip // 2 == 1
    a, b, c, d = slots
    a, b, c, d = jnp.where(odd, b, a), jnp.where(odd, a, b), jnp.where(odd, d, c), jnp.where(odd, c, d)
    return [jnp.where(high, c, a), jnp.where(high, d, b), jnp.where(high, a, c), jnp.where(high, b, d)]


def line_step(sides, own, s):
    groups = lax.axis_size("dp") // GROUP
    up, down = sides if s > 1 else (own, own)
    return hop(up, 1, s - 1, groups - 1), hop(down, -1, 1, groups - s + 1)


def line_stack(own, steps):
    groups = lax.axis_size("dp") // GROUP
    z = lax.axis_index("dp") // GROUP
    return jnp.stack(
        [own]
        + [jnp.where(z + s < groups, steps[s - 1][1], steps[groups - s - 1][0]) for s in range(1, groups)]
    )


def line_sum(parts):
    groups = lax.axis_size("dp") // GROUP
    total = parts[0].astype(F32)
    for s in range(1, groups):
        pairs = [
            (z * GROUP + t, (z + s) % groups * GROUP + t) for z in range(groups) for t in range(GROUP)
        ]
        total = total + lax.ppermute(parts[s].astype(BF), "dp", pairs).astype(F32)
    return total


def after(value, *others):
    return lax.optimization_barrier((value,) + others)[0]


def turn(value, shift, axis, parts):
    step = value.shape[axis] // parts
    return lax.dynamic_slice_in_dim(
        jnp.concatenate([value, value], axis=axis), shift * step, value.shape[axis], axis
    )


def core_sum(mine, other):
    return mine + swap(other.astype(BF), 1).astype(F32)


ANY = pl.BlockSpec(memory_space=pl.ANY)
VMEM = pl.BlockSpec(memory_space=pltpu.VMEM)
SMEM = pl.BlockSpec(memory_space=pltpu.SMEM)


def call(kernel, outs, args, places, scratch=(), flops=0, moved=0):
    return pl.pallas_call(
        kernel,
        out_shape=tuple(jax.ShapeDtypeStruct(shape, kind) for shape, kind in outs),
        in_specs=list(places),
        out_specs=tuple(VMEM for _ in outs),
        scratch_shapes=list(scratch),
        compiler_params=pltpu.CompilerParams(vmem_limit_bytes=VMEM_BYTES),
        cost_estimate=pl.CostEstimate(flops=flops, bytes_accessed=moved, transcendentals=0),
    )(*args)


def fetch(source, target, sem):
    copy = pltpu.make_async_copy(source, target, sem)
    copy.start()
    return copy


def turned(values, cosine, sine):
    return values * cosine + pltpu.roll(values, HEAD_DIM // 2, 1) * sine


def project_kernel(
    x_ref, gain_ref, shift_ref, cos_ref, sin_ref, wq, wk, wv, normed_ref, q_ref, k_ref, v_ref, w_ref, sems
):
    copies = [fetch(w, w_ref.at[i], sems.at[i]) for i, w in enumerate((wq, wk, wv))]
    normal, _ = norm_stats(x_ref[...].astype(F32))
    normed_ref[...] = (normal * gain_ref[...] + shift_ref[...]).astype(BF)
    cosine, sine = cos_ref[...], sin_ref[...]
    for i, out in enumerate((q_ref, k_ref, v_ref)):
        copies[i].wait()
        for low in range(0, out.shape[1], WIDE):
            raw = dot(normed_ref[...], w_ref[i, :, low : low + WIDE])
            for h in range(0, WIDE, HEAD_DIM):
                head = raw[:, h : h + HEAD_DIM]
                if i < 2:
                    head = turned(head, cosine, sine)
                out[:, low + h : low + h + HEAD_DIM] = head.astype(BF)


def attend_kernel(
    q_ref, k_ref, v_ref, x_ref, gain_ref, shift_ref, wo, context_ref, mixed_ref, normed_ref, probs_ref, w_ref, sem
):
    copy = fetch(wo, w_ref, sem)
    tokens, width = q_ref.shape
    row = lax.broadcasted_iota(jnp.int32, (tokens, tokens), 0)
    causal = row >= lax.broadcasted_iota(jnp.int32, (tokens, tokens), 1)
    for h in range(width // HEAD_DIM):
        span = slice(h * HEAD_DIM, (h + 1) * HEAD_DIM)
        scores = dot_t(q_ref[:, span], k_ref[:, span]) * HEAD_DIM**-0.5
        scores = jnp.where(causal, scores, NEGATIVE)
        weight = jnp.exp(scores - jnp.max(scores, axis=-1, keepdims=True))
        probs = weight / jnp.sum(weight, axis=-1, keepdims=True)
        probs_ref[h] = probs
        context_ref[:, span] = dot(probs.astype(BF), v_ref[:, span]).astype(BF)
    copy.wait()
    for low in range(0, width, WIDE):
        span = slice(low, low + WIDE)
        mixed_ref[:, span] = x_ref[:, span].astype(F32) + dot(context_ref[...], w_ref[:, span])
    normal, _ = norm_stats(mixed_ref[...])
    normed_ref[...] = (normal * gain_ref[...] + shift_ref[...]).astype(BF)


def hidden_kernel(*refs):
    xs, gs = refs[:CHIPS], refs[CHIPS : 2 * CHIPS]
    w_ref, bias_ref, mask_ref, active_ref, slope_ref, down_ref = refs[2 * CHIPS :]
    x = jnp.concatenate([x[...] for x in xs], axis=0)
    tokens = xs[0].shape[0]
    for low in range(0, w_ref.shape[1], WIDE):
        span = slice(low, low + WIDE)
        hidden = dot(x, w_ref[:, span]) + bias_ref[:, span]
        square = hidden * hidden
        bent = jnp.tanh(0.7978845608 * hidden * (1.0 + 0.044715 * square))
        slope = 0.5 * (1.0 + bent) + (0.5 * 0.7978845608) * hidden * (1.0 - bent * bent) * (
            1.0 + 3.0 * 0.044715 * square
        )
        value = 0.5 * hidden * (1.0 + bent)
        for j in range(CHIPS):
            part = slice(j * tokens, (j + 1) * tokens)
            keep = mask_ref[j : j + 1, span]
            active_ref[part, span] = (value[part] * keep).astype(BF)
            slope_ref[part, span] = slope[part] * keep
    grad = jnp.concatenate([g[...] for g in gs], axis=0)
    for low in range(0, w_ref.shape[1], WIDE):
        down_ref[low : low + WIDE, :] = t_dot(active_ref[:, low : low + WIDE], grad).astype(BF)


def reverse_kernel(*refs):
    gs = refs[:CHIPS]
    w1_ref, w2_ref, slope_ref, grad_ref, sum_ref, own_ref = refs[CHIPS : CHIPS + 6]
    sent = refs[CHIPS + 6 :]
    tokens = gs[0].shape[0]
    grad = jnp.concatenate([g[...] for g in gs], axis=0)
    for low in range(0, w2_ref.shape[0], WIDE):
        span = slice(low, low + WIDE)
        value = (dot_t(grad, w2_ref[span, :]) * slope_ref[:, span]).astype(BF)
        grad_ref[:, span] = value
        sum_ref[:, span] = jnp.sum(value.astype(F32), axis=0, keepdims=True)
    for low in range(0, w1_ref.shape[0], WIDE):
        span = slice(low, low + WIDE)
        part = dot_t(grad_ref[...], w1_ref[span, :])
        own_ref[:, span] = part[:tokens]
        for j in range(1, CHIPS):
            sent[j - 1][:, span] = part[j * tokens : (j + 1) * tokens].astype(BF)


def finish_kernel(*refs):
    xs = refs[:CHIPS]
    active_ref, grad_ref, w2_ref, up_ref, own_ref = refs[CHIPS : CHIPS + 5]
    sent = refs[CHIPS + 5 :]
    tokens = xs[0].shape[0]
    for low in range(0, w2_ref.shape[1], WIDE):
        span = slice(low, low + WIDE)
        part = dot(active_ref[...], w2_ref[:, span])
        own_ref[:, span] = part[:tokens]
        for j in range(1, CHIPS):
            sent[j - 1][:, span] = part[j * tokens : (j + 1) * tokens].astype(BF)
    for low in range(0, xs[0].shape[1], WIDE):
        x = jnp.concatenate([x[:, low : low + WIDE] for x in xs], axis=0)
        up_ref[low : low + WIDE, :] = t_dot(x, grad_ref[...]).astype(BF)


def mixed_kernel(
    second_ref, mixed_ref, sens_ref, gain_ref, wo, v_ref, probs_ref,
    mixgrad_ref, low_ref, cgrad_ref, vgrad_ref, norm_ref, shift_ref, w_ref, sem
):
    copy = fetch(wo, w_ref, sem)
    normal, inverse = norm_stats(mixed_ref[...])
    part, norm_sum, shift_sum = norm_back(second_ref[...].astype(F32), gain_ref[...], normal, inverse)
    norm_ref[...], shift_ref[...] = norm_sum, shift_sum
    mixed_grad = sens_ref[...].astype(F32) + part
    mixgrad_ref[...] = mixed_grad
    low_ref[...] = mixed_grad.astype(BF)
    copy.wait()
    width = v_ref.shape[1]
    for low in range(0, width, WIDE):
        cgrad_ref[:, low : low + WIDE] = dot_t(low_ref[...], w_ref[low : low + WIDE, :]).astype(BF)
    for h in range(width // HEAD_DIM):
        span = slice(h * HEAD_DIM, (h + 1) * HEAD_DIM)
        vgrad_ref[:, span] = t_dot(probs_ref[h].astype(BF), cgrad_ref[:, span]).astype(BF)


def score_kernel(cgrad_ref, q_ref, k_ref, v_ref, probs_ref, cos_ref, sin_ref, qgrad_ref, kgrad_ref):
    cosine, sine = cos_ref[...], -sin_ref[...]
    for h in range(v_ref.shape[1] // HEAD_DIM):
        span = slice(h * HEAD_DIM, (h + 1) * HEAD_DIM)
        probs = probs_ref[h]
        probs_grad = dot_t(cgrad_ref[:, span], v_ref[:, span])
        inner = jnp.sum(probs_grad * probs, axis=-1, keepdims=True)
        scores_grad = (probs * (probs_grad - inner)).astype(BF)
        scale = HEAD_DIM**-0.5
        qgrad_ref[:, span] = turned(dot(scores_grad, k_ref[:, span]) * scale, cosine, sine).astype(BF)
        kgrad_ref[:, span] = turned(t_dot(scores_grad, q_ref[:, span]) * scale, cosine, sine).astype(BF)


def leading_kernel(
    qgrad_ref, kgrad_ref, vgrad_ref, x_ref, gain_ref, mixgrad_ref, wq, wk, wv,
    out_ref, norm_ref, shift_ref, w_ref, lead_ref, sems
):
    copies = [fetch(w, w_ref.at[i], sems.at[i]) for i, w in enumerate((wq, wk, wv))]
    normal, inverse = norm_stats(x_ref[...].astype(F32))
    for copy in copies:
        copy.wait()
    for low in range(0, x_ref.shape[1], WIDE):
        span = slice(low, low + WIDE)
        lead_ref[:, span] = (
            dot_t(qgrad_ref[...], w_ref[0, span, :])
            + dot_t(kgrad_ref[...], w_ref[1, span, :])
            + dot_t(vgrad_ref[...], w_ref[2, span, :])
        )
    part, norm_sum, shift_sum = norm_back(lead_ref[...], gain_ref[...], normal, inverse)
    norm_ref[...], shift_ref[...] = norm_sum, shift_sum
    out_ref[...] = (mixgrad_ref[...] + part).astype(BF)


def outer_kernel(*refs):
    kinds = (len(refs) - 1) // CHIPS - 1
    rights, out_ref = refs[kinds * CHIPS : -1], refs[-1]
    right = jnp.concatenate([r[...] for r in rights], axis=0)
    share = right.shape[1] // kinds
    for i in range(kinds):
        lefts = refs[i * CHIPS : (i + 1) * CHIPS]
        for low in range(0, lefts[0].shape[1], WIDE):
            left = jnp.concatenate([l[:, low : low + WIDE] for l in lefts], axis=0)
            out_ref[low : low + WIDE, i * share : (i + 1) * share] = t_dot(
                left, right[:, i * share : (i + 1) * share]
            ).astype(BF)


def per_device(
    sequence_elements,
    result_sensitivity,
    mixer_gain,
    mixer_offset,
    question_matrix,
    lookup_matrix,
    content_matrix,
    mixer_projection_matrix,
    feedforward_gain,
    feedforward_offset,
    expand_matrix,
    inner_neuron_offset,
    contract_matrix,
    feedforward_result_offset,
    sequence_level_choice,
    servers_per_level,
    accepted_row_limit,
    server_selection,
):
    devices = lax.axis_size("dp")
    me = lax.axis_index("dp")
    groups = devices // GROUP
    z, chip, core = me // GROUP, me % GROUP // 2, me % 2
    tokens, width = sequence_elements.shape
    heads = width // HEAD_DIM
    rows, feed = expand_matrix.shape
    cols = contract_matrix.shape[0]
    offset_len = feedforward_result_offset.shape[0]
    levels = jnp.arange(LEVELS)
    block = 2 * cols
    units = groups * block
    gain_first, shift_first, gain_second, shift_second = (
        v.astype(F32)[None, :] for v in (mixer_gain, mixer_offset, feedforward_gain, feedforward_offset)
    )
    cosine, sine = (jnp.asarray(t) for t in rope_tables(tokens))
    flat, wide = (tokens, width), (1, width)
    square = (width, width)
    all_rows = (CHIPS * tokens, units)
    weight_space = pltpu.VMEM(square, BF)
    triple_space = pltpu.VMEM((3,) + square, BF)
    dma, dmas = pltpu.SemaphoreType.DMA, pltpu.SemaphoreType.DMA((3,))
    flops = 2 * tokens * width * width
    moved = 2 * width * width

    contract_full = lax.all_gather(contract_matrix, "dp", axis_index_groups=lines())
    expand_chunks = expand_matrix.reshape(rows, groups, CHIPS, block).transpose(2, 0, 1, 3)
    expand_pieces = exchange(expand_chunks.reshape(CHIPS, rows, units))
    level = sequence_level_choice[0]
    choice = server_selection.reshape(-1)
    info = jnp.concatenate(
        [
            feedforward_result_offset.astype(F32),
            inner_neuron_offset.astype(F32),
            level.astype(F32)[None],
            jnp.min(choice).astype(F32)[None],
        ]
    )
    info = jnp.pad(info, (0, -info.shape[0] % 128))
    table = jnp.where(jnp.arange(devices)[:, None] == me, info[None, :], 0.0)
    normed_first, query_rot, key_rot, value_rows = call(
        project_kernel,
        [(flat, BF)] * 4,
        (sequence_elements, gain_first, shift_first, cosine, sine, question_matrix, lookup_matrix, content_matrix),
        [VMEM] * 5 + [ANY] * 3,
        [triple_space, dmas],
        3 * flops,
        3 * moved,
    )
    query_rot, key_rot, value_rows, expand_pieces = lax.optimization_barrier(
        (query_rot, key_rot, value_rows, expand_pieces)
    )

    expand_plane = jnp.concatenate(in_order(expand_pieces), axis=0)
    expand_steps = [line_step(None, expand_plane, 1)]
    context, mixed, normed_second, probs = call(
        attend_kernel,
        [(flat, BF), (flat, F32), (flat, BF), ((heads, tokens, tokens), F32)],
        (query_rot, key_rot, value_rows, sequence_elements, gain_second, shift_second, mixer_projection_matrix),
        [VMEM] * 6 + [ANY],
        [weight_space, dma],
        2 * flops,
        moved,
    )
    normed_second, expand_steps[0] = lax.optimization_barrier((normed_second, expand_steps[0]))

    row_slots = spread(turn(normed_second, z, 1, groups))
    for s in range(2, groups):
        expand_steps.append(line_step(expand_steps[-1], expand_plane, s))
    table = sum_all(table)
    result_offset = table[:, :offset_len].reshape(-1)
    hidden_offsets = table[:, offset_len : offset_len + cols]
    all_levels = table[:, offset_len + cols].astype(jnp.int32)
    all_lowest = table[:, offset_len + cols + 1].astype(jnp.int32)
    size = jnp.sum(jnp.where(levels == level, servers_per_level, 0))
    limit = jnp.sum(jnp.where(levels == level, accepted_row_limit, 0))
    server = choice % size
    before = jnp.arange(tokens)[None, :] < jnp.arange(tokens)[:, None]
    local = jnp.sum((before & (server[None, :] == server[:, None])).astype(jnp.int32), axis=1)
    low = all_lowest[None, :]
    seen = (low + tokens - 1 - server[:, None] + size) // size - (low - 1 - server[:, None] + size) // size
    earlier = (jnp.arange(devices) < me) & (all_levels == level)
    arrival = local + jnp.sum(jnp.where(earlier[None, :], seen, 0), axis=1)
    kept = (arrival < limit).astype(F32)[:, None]
    kept_sensitivity = (result_sensitivity.astype(F32) * kept).astype(BF)
    grad_slots = spread(kept_sensitivity)
    slot_levels = jnp.take(all_levels, me ^ (2 * jnp.arange(CHIPS)))
    starts = (jnp.arange(groups) * CHIPS + chip) * block
    active_block = starts[None, :] < (feed // 8) * (1 << slot_levels[:, None])
    mask = jnp.repeat(active_block.astype(F32), block, axis=1)
    hidden_offset = lax.dynamic_index_in_dim(
        hidden_offsets.reshape(groups, CHIPS, block), chip, 1, keepdims=False
    ).reshape(1, -1)
    expand_mine = line_stack(expand_plane, expand_steps).reshape(groups, CHIPS, rows, units)
    expand_other = swap(expand_mine, 1)
    first_weight = jnp.where(
        core == 0,
        jnp.stack([expand_mine, expand_other], axis=2),
        jnp.stack([expand_other, expand_mine], axis=2),
    ).reshape(width, units)

    active, slope, down_part = call(
        hidden_kernel,
        [(all_rows, BF), (all_rows, F32), ((units, width), BF)],
        (*row_slots, *grad_slots, first_weight, hidden_offset, mask),
        [VMEM] * (2 * CHIPS + 3),
        (),
        8 * flops,
        6 * moved,
    )
    contract_other = swap(contract_full, 1)
    second_weight = jnp.where(
        core == 0,
        jnp.stack([contract_full, contract_other], axis=1),
        jnp.stack([contract_other, contract_full], axis=1),
    ).reshape(units, width)
    down_part = down_part.reshape(groups, 2, cols, width)
    down_other = swap(lax.dynamic_index_in_dim(down_part, 1 - core, 1, keepdims=False), 1)
    first_slots = spread(after(turn(normed_first, z, 1, groups), row_slots))
    hidden_grad, hidden_sum, second_own, *second_sent = call(
        reverse_kernel,
        [(all_rows, BF), ((1, units), F32), (flat, F32)] + [(flat, BF)] * 3,
        (*grad_slots, first_weight, second_weight, slope),
        [VMEM] * (CHIPS + 3),
        (),
        8 * flops,
        6 * moved,
    )
    second_got = [swap(second_sent[j - 1], 2 * j) for j in range(1, CHIPS)]
    contract_sum = (
        lax.dynamic_index_in_dim(down_part, core, 1, keepdims=False).astype(F32) + down_other.astype(F32)
    ).astype(BF)
    share_contract = lax.psum_scatter(
        contract_sum, "dp", scatter_dimension=0, axis_index_groups=lines()
    ).astype(F32)
    up_part, branch_own, *branch_sent = call(
        finish_kernel,
        [((width, units), BF), (flat, F32)] + [(flat, BF)] * 3,
        (*row_slots, active, hidden_grad, second_weight),
        [VMEM] * (CHIPS + 3),
        (),
        8 * flops,
        6 * moved,
    )

    def rows_both(part):
        part = part.reshape(groups, CHIPS, 2, rows, part.shape[1])
        got = swap(lax.dynamic_index_in_dim(part, 1 - core, 2, keepdims=False), 1)
        return lax.dynamic_index_in_dim(part, core, 2, keepdims=False).astype(F32) + got.astype(F32)

    expand_both = rows_both(up_part)
    second_sum = second_own + second_got[0].astype(F32) + second_got[1].astype(F32) + second_got[2].astype(F32)
    second_grad = turn(second_sum.astype(BF), (groups - z) % groups, 1, groups)
    second_grad, expand_both, branch_sent = lax.optimization_barrier((second_grad, expand_both, branch_sent))

    expand_rows = line_sum(expand_both)
    mixed_grad, mixed_low, context_grad, value_grad, midnorm_sum, midshift_sum = call(
        mixed_kernel,
        [(flat, F32), (flat, BF), (flat, BF), (flat, BF), (wide, F32), (wide, F32)],
        (second_grad, mixed, result_sensitivity, gain_second, mixer_projection_matrix, value_rows, probs),
        [VMEM] * 4 + [ANY] + [VMEM] * 2,
        [weight_space, dma],
        flops,
        moved,
    )
    share = width // CHIPS

    def split_columns(*grads):
        chunks = jnp.concatenate([grad.reshape(tokens, CHIPS, share) for grad in grads], axis=2)
        return exchange(chunks.transpose(1, 0, 2))

    context_slots = spread(after(turn(context, z, 1, groups), first_slots))
    first_pair = split_columns(mixed_low, value_grad)
    query_grad, key_grad = call(
        score_kernel,
        [(flat, BF)] * 2,
        (context_grad, query_rot, key_rot, value_rows, probs, cosine, sine),
        [VMEM] * 7,
        (),
        flops,
        moved,
    )
    second_pair = split_columns(key_grad, query_grad)
    branch_got = [swap(branch_sent[j - 1], 2 * j) for j in range(1, CHIPS)]
    branch = branch_own + branch_got[0].astype(F32) + branch_got[1].astype(F32) + branch_got[2].astype(F32)
    branch = (branch + result_offset).astype(BF).astype(F32)
    layer_output = (mixed + kept * branch).astype(BF)
    layer_input_gradient, leadnorm_sum, leadshift_sum = call(
        leading_kernel,
        [(flat, BF), (wide, F32), (wide, F32)],
        (
            query_grad, key_grad, value_grad, sequence_elements, gain_first, mixed_grad,
            question_matrix, lookup_matrix, content_matrix,
        ),
        [VMEM] * 6 + [ANY] * 3,
        [triple_space, pltpu.VMEM(flat, F32), dmas],
        3 * flops,
        3 * moved,
    )

    def outer(lefts, right):
        (part,) = call(
            outer_kernel,
            [((width, 2 * share), BF)],
            (*lefts, *right),
            [VMEM] * (len(lefts) + CHIPS),
            (),
            2 * flops,
            2 * moved,
        )
        return part

    early = line_sum(rows_both(outer(context_slots + first_slots, first_pair)))
    late = line_sum(rows_both(outer(first_slots, second_pair)))

    def home(summed):
        return in_order(exchange(summed.astype(BF)))

    expand_home = home(expand_rows)
    share_expand = (
        jnp.stack([piece.reshape(rows, groups, block) for piece in expand_home], axis=2)
        .astype(F32)
        .reshape(rows, feed)
    )
    early, late = home(early), home(late)

    def join(pieces, low):
        return jnp.concatenate([piece[:, low : low + share] for piece in pieces], axis=1).astype(F32)

    share_mixing, share_value = join(early, 0), join(early, share)
    share_key, share_query = join(late, 0), join(late, share)

    hidden_spot = (jnp.arange(CHIPS)[None, :, None] == chip).astype(F32)
    hidden_full = hidden_spot * hidden_sum.reshape(groups, 1, block)
    result_sum = jnp.sum(kept_sensitivity.astype(F32), axis=0)
    vectors = [midnorm_sum, midshift_sum, leadnorm_sum, leadshift_sum, result_sum, hidden_full]
    vectors = jnp.concatenate([vector.reshape(devices, -1) for vector in vectors], axis=1)
    vectors = jnp.pad(vectors, ((0, 0), (0, -vectors.shape[1] % 128)))
    vectors = lax.all_to_all(vectors[:, None, :], "dp", 0, 0, tiled=True)
    vectors = jnp.sum(vectors, axis=(0, 1))
    small = [vectors[i * offset_len : (i + 1) * offset_len] for i in range(5)]
    share_hidden = vectors[5 * offset_len : 5 * offset_len + cols]
    return (
        layer_output,
        layer_input_gradient,
        small[2],
        small[3],
        share_query,
        share_key,
        share_value,
        share_mixing,
        small[0],
        small[1],
        share_expand,
        share_hidden,
        share_contract,
        small[4],
    )


def solution(mesh):
    split, line, whole = P("dp", None), P("dp"), P()
    return jax.shard_map(
        per_device,
        mesh=mesh,
        in_specs=(split, split) + (whole,) * 8 + (split, line, split, line, line, whole, whole, split),
        out_specs=(split, split, line, line, split, split, split, split, line, line, split, line, split, line),
        check_vma=False,
    )
```

time: 523 us -> 485 us (0.927)
  Pallas kernels: 0 us -> 94 us
  matrix products: 77.6 us -> 0 us
  starting transfers between devices: 159 us -> 87.9 us
  waiting for transfers between devices: 142 us -> 203 us
  local copies, waits for them, and re-layouts: 55.9 us -> 27 us
  other arithmetic: 59.3 us -> 46.8 us
    pallas_call x0 -> x10, Pallas kernels: none -> 94 us  [call(): pl.pallas_call(kernel, out_shape=tuple((jax.ShapeDtypeStruct(shape, kind)...]
    ppermute x24 -> x6, starting transfers between devices: 88 us -> 10.5 us  [hop(): return lax.ppermute(value, 'dp', pairs)]
    dot_general x22 -> x0, matrix products: 74.5 us -> none  [the longest x17 69.4 us: dot(): lax.dot_general(left, right, (dims, ((), ())), preferred_element_type=F32)]
    ppermute x0 -> x9, waiting for transfers between devices: none -> 61.8 us  [line_sum(): total = total + lax.ppermute(parts[s].astype(BF), 'dp', pairs).astype(F32)]
    ppermute x0 -> x9, starting transfers between devices: none -> 16.7 us  [line_sum(): total = total + lax.ppermute(parts[s].astype(BF), 'dp', pairs).astype(F32)]
    convert_element_type x13 -> x3, local copies, waits for them, and re-layouts: 15.8 us -> 1.26 us  [line_sum(): total = total + lax.ppermute(parts[s].astype(BF), 'dp', pairs).astype(F32)]
    ppermute x42 -> x47, waiting for transfers between devices: 67.2 us -> 77.9 us  [swap(): return lax.ppermute(value, 'dp', [(i, i ^ bit) for i in range(count)])]
    all_gather x1, waiting for transfers between devices: 9.01 us -> 0.01 us  [per_device(): lax.all_gather(contract_matrix, 'dp', axis_index_groups=lines())]
  transfers between devices with their start and end apart: 70 -> 65, of which waited for: 26 -> 24; matrix products, arithmetic and copies ran while one was open for 36% -> 14% of each run, Pallas kernels for 0% -> 20%
where the time goes in v3:
time: 485 us; the launch traced here: 477 us
  waiting for transfers between devices  203 us (42%)
  Pallas kernels  94 us (19%)
  starting transfers between devices  87.9 us (18%)
  other arithmetic  46.8 us (10%)
  local copies, waits for them, and re-layouts  27 us (6%)
  between operations  18.8 us (4%)
    pallas_call x10, Pallas kernels, call(): pl.pallas_call(kernel, out_shape=tuple((jax.ShapeDtypeStruct(shape, kind)...  94 us
    ppermute x47, waiting for transfers between devices, swap(): return lax.ppermute(value, 'dp', [(i, i ^ bit) for i in range(count)])  77.9 us
    ppermute x6, waiting for transfers between devices, hop(): return lax.ppermute(value, 'dp', pairs)  63.2 us
    ppermute x9, waiting for transfers between devices, line_sum(): total = total + lax.ppermute(parts[s].astype(BF), 'dp', pairs).astype(F32)  61.8 us
    ppermute x47, starting transfers between devices, swap(): return lax.ppermute(value, 'dp', [(i, i ^ bit) for i in range(count)])  55.1 us
    ppermute x9, starting transfers between devices, line_sum(): total = total + lax.ppermute(parts[s].astype(BF), 'dp', pairs).astype(F32)  16.7 us
    ppermute x6, starting transfers between devices, hop(): return lax.ppermute(value, 'dp', pairs)  10.5 us
  transfers between devices with their start and end apart: 65, of which 24 were waited for; matrix products, arithmetic and copies ran while one was open for 14% of the time, Pallas kernels for 20%

profile of v3, /device:TPU:0, one launch (start us, length us, event | category | flops | bytes accessed | tf_op | source)
XLA Modules:
  0.0 477.5 jit_solution(2731122075621650289)
XLA Ops:
  7.3 1.5 reshape.262
  9.4 3.0 collective-permute-start
  19.0 8.0 %shard_map.299 = (bf16[160,1536]{1,0:T(8,128)(2,1)}, bf16[160,1536]{1,0:T(8,128)(2,1)}, bf16[160,1536]{1,0:T(8,128)(2,1)}, bf16[160,1536]{1,0:T(8,128)(2,1)}) custom-call(bf16[160,1536]{1,0:T(8,128)(2,1)} %x_ref.5, f32[1,1536]{1,0:T(1,128)} %reshape.280.gain_ref, f32[1,1536]{1,0:T(1,128)} %reshape.281.shift_ref, f32[160,128]{1,0:T(8,128)} %constant.259.clone.cos_ref, ...), custom_call_target="tpu_custom_call" | custom-call | flops 2264924160 | bytes 14155776 | tf_op jit(solution)/shard_map/pallas_call | solution.py:161
  27.1 4.0 collective-permute-start.8
  33.9 6.0 %shard_map.300 = (bf16[160,1536]{1,0:T(8,128)(2,1)}, f32[160,1536]{1,0:T(8,128)}, bf16[160,1536]{1,0:T(8,128)(2,1)}, f32[12,160,160]{2,1,0:T(8,128)}) custom-call(bf16[160,1536]{1,0:T(8,128)(2,1)} %get-tuple-element.67.q_ref, bf16[160,1536]{1,0:T(8,128)(2,1)} %get-tuple-element.68.k_ref, bf16[160,1536]{1,0:T(8,128)(2,1)} %get-tuple-element.69.v_ref, ...), custom_call_target="tpu_custom_call" | custom-call | flops 1509949440 | bytes 4718592 | tf_op jit(solution)/shard_map/pallas_call | solution.py:161
  39.8 3.0 collective-permute-done.8
  42.8 4.1 collective-permute-done.9
  50.3 16.3 %collective-permute-done.18 = bf16[192,1536]{1,0:T(8,128)(2,1)S(1)} collective-permute-done((bf16[192,1536]{1,0:T(8,128)(2,1)S(1)}, bf16[192,1536]{1,0:T(8,128)(2,1)S(1)}, u32[]{:S(2)}, u32[]{:S(2)}) %collective-permute-start.18) | collective-permute-done | bytes 589856 | tf_op jit(solution)/shard_map/ppermute | solution.py:70
  68.0 1.5 collective-permute-start.4
  70.8 39.7 %collective-permute-done.19 = bf16[192,1536]{1,0:T(8,128)(2,1)S(1)} collective-permute-done((bf16[192,1536]{1,0:T(8,128)(2,1)S(1)}, bf16[192,1536]{1,0:T(8,128)(2,1)S(1)}, u32[]{:S(2)}, u32[]{:S(2)}) %collective-permute-start.19) | collective-permute-done | bytes 589856 | tf_op jit(solution)/shard_map/ppermute | solution.py:70
  110.7 1.7 pad_maximum_fusion
  112.5 1.6 collective-permute-start.5
  114.7 1.7 collective-permute-done.5
  116.5 3.9 collective-permute-done.6
  120.4 8.0 %collective-permute-start.7 = (f32[32,256]{1,0:T(8,128)S(1)}, f32[32,256]{1,0:T(8,128)S(1)}, u32[]{:S(2)}, u32[]{:S(2)}) collective-permute-start(f32[32,256]{1,0:T(8,128)S(1)} %add.280), channel_id=1, source_target_pairs={{0,16},{1,17},{2,18},{3,19},{4,20},{5,21},{6,22},{7,23},{8,24},{9,... | collective-permute-start | bytes 98312 | tf_op jit(solution)/shard_map/ppermute | solution.py:59
  137.7 1.5 collective-permute-start.11
  142.0 16.5 %collective-permute-done.10.refs_1_ = bf16[160,1536]{1,0:T(8,128)(2,1)S(1)} collective-permute-done((bf16[160,1536]{1,0:T(8,128)(2,1)S(1)}, bf16[160,1536]{1,0:T(8,128)(2,1)S(1)}, u32[]{:S(2)}, u32[]{:S(2)}) %collective-permute-start.10) | collective-permute-done | bytes 491552 | tf_op jit(solution)/shard_map/ppermute | solution.py:59
  158.6 1.5 collective-permute-start.14
  161.5 8.6 %collective-permute-done.12.refs_3_ = bf16[160,1536]{1,0:T(8,128)(2,1)S(1)} collective-permute-done((bf16[160,1536]{1,0:T(8,128)(2,1)S(1)}, bf16[160,1536]{1,0:T(8,128)(2,1)S(1)}, u32[]{:S(2)}, u32[]{:S(2)}) %collective-permute-start.12) | collective-permute-done | bytes 491552 | tf_op jit(solution)/shard_map/ppermute | solution.py:59
  172.5 5.2 %maximum_select_fusion = bf16[4,4,2,48,1536]{4,3,2,1,0:T(8,128)(2,1)} fusion(bf16[4,4,1,48,1536]{4,3,2,1,0:T(8,128)(2,1)} %bitcast.22, bf16[1,4,1,48,1536]{4,3,2,1,0:T(8,128)(2,1)S(1)} %bitcast.213, bf16[1,4,1,48,1536]{4,3,2,1,0:T(8,128)(2,1)S(1)} %bitcast.211, bf16[1,4,1,48,1536]{4,3,2,1,0:T(8,128)(2,1)S(1)} %bitcast.215, ...), kind=kLoop, calls=%fused_computation.1 | loop fusion | flops 21233664 | bytes 9437185 | tf_op jit(solution)/shard_map/jit(_where)/select_n | solution.py:464
  178.3 14.9 %collective-permute-done.14.refs_6_.refs_2_ = bf16[160,1536]{1,0:T(8,128)(2,1)} collective-permute-done((bf16[160,1536]{1,0:T(8,128)(2,1)}, bf16[160,1536]{1,0:T(8,128)(2,1)}, u32[]{:S(2)}, u32[]{:S(2)}) %collective-permute-start.14) | collective-permute-done | bytes 491552 | tf_op jit(solution)/shard_map/ppermute | solution.py:59
  194.6 14.8 %shard_map.301 = (bf16[640,1536]{1,0:T(8,128)(2,1)}, f32[640,1536]{1,0:T(8,128)}, bf16[1536,1536]{1,0:T(8,128)(2,1)}) custom-call(bf16[160,1536]{1,0:T(8,128)(2,1)} %copy-done.14, bf16[160,1536]{1,0:T(8,128)(2,1)} %copy-done.31, bf16[160,1536]{1,0:T(8,128)(2,1)} %copy-done.32, bf16[160,1536]{1,0:T(8,128)(2,1)} %copy-done.33, ...), custom_call_target="tpu_custom_call" | custom-call | flops 6039797760 | bytes 28311552 | tf_op jit(solution)/shard_map/pallas_call | solution.py:161
  209.4 3.4 dynamic-slice_bitcast_fusion
  212.8 2.7 maximum_select_fusion.1
  215.6 13.0 %shard_map.302 = (bf16[640,1536]{1,0:T(8,128)(2,1)}, f32[1,1536]{1,0:T(1,128)}, f32[160,1536]{1,0:T(8,128)}, bf16[160,1536]{1,0:T(8,128)(2,1)}, bf16[160,1536]{1,0:T(8,128)(2,1)}, /*index=5*/bf16[160,1536]{1,0:T(8,128)(2,1)}) custom-call(bf16[160,1536]{1,0:T(8,128)(2,1)} %get-tuple-element.122.refs_4_.refs_0_, ...), custom_call_target="tpu_custom_call" | custom-call | flops 6039797760 | bytes 28311552 | tf_op jit(solution)/shard_map/pallas_call | solution.py:161
  228.6 13.2 %shard_map.303 = (bf16[1536,1536]{1,0:T(8,128)(2,1)}, f32[160,1536]{1,0:T(8,128)}, bf16[160,1536]{1,0:T(8,128)(2,1)}, bf16[160,1536]{1,0:T(8,128)(2,1)}, bf16[160,1536]{1,0:T(8,128)(2,1)}) custom-call(bf16[160,1536]{1,0:T(8,128)(2,1)} %copy-done.14, bf16[160,1536]{1,0:T(8,128)(2,1)} %copy-done.31, bf16[160,1536]{1,0:T(8,128)(2,1)} %copy-done.32, ...), custom_call_target="tpu_custom_call" | custom-call | flops 6039797760 | bytes 28311552 | tf_op jit(solution)/shard_map/pallas_call | solution.py:161
  241.8 3.3 dynamic-slice_bitcast_fusion.1
  251.5 9.5 %collective-permute-done.24 = bf16[160,1536]{1,0:T(8,128)(2,1)} collective-permute-done((bf16[160,1536]{1,0:T(8,128)(2,1)}, bf16[160,1536]{1,0:T(8,128)(2,1)}, u32[]{:S(2)}, u32[]{:S(2)}) %collective-permute-start.24) | collective-permute-done | bytes 491552 | tf_op jit(solution)/shard_map/ppermute | solution.py:59
  261.5 9.0 %collective-permute-done.23 = bf16[160,1536]{1,0:T(8,128)(2,1)} collective-permute-done((bf16[160,1536]{1,0:T(8,128)(2,1)}, bf16[160,1536]{1,0:T(8,128)(2,1)}, u32[]{:S(2)}, u32[]{:S(2)}) %collective-permute-start.23) | collective-permute-done | bytes 491552 | tf_op jit(solution)/shard_map/ppermute | solution.py:59
  272.5 1.8 add_convert_fusion.2
  275.3 3.8 fusion
  279.1 5.3 %convert_add_fusion.1 = f32[4,4,48,1536]{3,2,1,0:T(8,128)} fusion(bf16[4,4,48,1536]{3,2,1,0:T(8,128)(2,1)} %collective-permute-done.25, bf16[4,4,2,48,1536]{4,3,2,1,0:T(8,128)(2,1)} %bitcast.223, s32[]{:T(128)S(6)} %select_n.425), kind=kLoop, calls=%fused_computation.5 | loop fusion | flops 3538944 | bytes 9437188 | tf_op jit(solution)/shard_map/add | solution.py:517
  284.4 7.9 %shard_map.304 = (f32[160,1536]{1,0:T(8,128)}, bf16[160,1536]{1,0:T(8,128)(2,1)}, bf16[160,1536]{1,0:T(8,128)(2,1)}, bf16[160,1536]{1,0:T(8,128)(2,1)}, f32[1,1536]{1,0:T(1,128)}, /*index=5*/f32[1,1536]{1,0:T(1,128)}) custom-call(bf16[160,1536]{1,0:T(8,128)(2,1)} %fusion.14.second_ref, f32[160,1536]{1,0:T(8,128)} %get-tuple-element.70.mixed_ref, ...), custom_call_target="tpu_custom_call" | custom-call | flops 754974720 | bytes 4718592 | tf_op jit(solution)/shard_map/pallas_call | solution.py:161
  292.4 6.6 %shard_map.305 = (bf16[160,1536]{1,0:T(8,128)(2,1)}, bf16[160,1536]{1,0:T(8,128)(2,1)}) custom-call(bf16[160,1536]{1,0:T(8,128)(2,1)} %get-tuple-element.96.cgrad_ref, bf16[160,1536]{1,0:T(8,128)(2,1)} %get-tuple-element.67.q_ref, bf16[160,1536]{1,0:T(8,128)(2,1)} %get-tuple-element.68.k_ref, bf16[160,1536]{1,0:T(8,128)(2,1)} %get-tuple-element.69.v_ref, ...), custom_call_target="tpu_custom_call" | custom-call | flops 754974720 | bytes 4718592 | tf_op jit(solution)/shard_map/pallas_call | solution.py:161
  299.2 12.9 %shard_map.306 = (bf16[160,1536]{1,0:T(8,128)(2,1)}, f32[1,1536]{1,0:T(1,128)}, f32[1,1536]{1,0:T(1,128)}) custom-call(bf16[160,1536]{1,0:T(8,128)(2,1)} %get-tuple-element.97.qgrad_ref, bf16[160,1536]{1,0:T(8,128)(2,1)} %get-tuple-element.98.kgrad_ref, bf16[160,1536]{1,0:T(8,128)(2,1)} %get-tuple-element.99.vgrad_ref, bf16[160,1536]{1,0:T(8,128)(2,1)} %x_ref.5, ...), custom_call_target="tpu_custom_call" | custom-call | flops 2264924160 | bytes 14155776 | tf_op jit(solution)/shard_map/pallas_call | solution.py:161
  314.6 5.5 %all-to-all-start = ((f32[32,1,512]{2,1,0:T(1,128)}), f32[32,1,512]{2,1,0:T(1,128)S(1)}, u32[]{:S(2)}, u32[]{:S(2)}) async-start(f32[32,1,512]{2,1,0:T(1,128)} %broadcast_in_dim.102), calls=%async_computation | async-start | bytes 131072 | tf_op jit(solution)/shard_map/all_to_all | solution.py:607
  321.0 1.8 collective-permute-start.32
  324.3 2.8 convert.27
  331.2 1.5 collective-permute-start.46
  335.0 2.2 collective-permute-start.57
  337.7 2.4 collective-permute-start.56
  340.1 1.9 collective-permute-done.45.refs_9_
  342.1 1.7 collective-permute-start.55
  345.0 5.2 %shard_map.307 = bf16[1536,768]{1,0:T(8,128)(2,1)} custom-call(bf16[160,1536]{1,0:T(8,128)(2,1)} %copy-done.5, bf16[160,1536]{1,0:T(8,128)(2,1)} %collective-permute-done.29.refs_1_.refs_5_, bf16[160,1536]{1,0:T(8,128)(2,1)} %copy-done.15, bf16[160,1536]{1,0:T(8,128)(2,1)} %copy-done.16, bf16[160,768]{1,0:T(8,128)(2,1)} %get-tuple-element.143.refs_4_, ...), custom_call_target="tpu_custom_call" | custom-call | flops 1509949440 | bytes 9437184 | tf_op jit(solution)/shard_map/pallas_call | solution.py:161
  350.3 1.6 collective-permute-start.28
  352.5 6.4 %shard_map.308 = bf16[1536,768]{1,0:T(8,128)(2,1)} custom-call(bf16[160,1536]{1,0:T(8,128)(2,1)} %copy-done.6, bf16[160,1536]{1,0:T(8,128)(2,1)} %copy-done.17, bf16[160,1536]{1,0:T(8,128)(2,1)} %collective-permute-done.43.refs_2_, bf16[160,1536]{1,0:T(8,128)(2,1)} %collective-permute-done.44.refs_3_, bf16[160,1536]{1,0:T(8,128)(2,1)} %copy-done.5, ...), custom_call_target="tpu_custom_call" | custom-call | flops 1509949440 | bytes 9437184 | tf_op jit(solution)/shard_map/pallas_call | solution.py:161
  363.7 22.7 %collective-permute-done.56 = bf16[4,48,1536]{2,1,0:T(8,128)(2,1)S(1)} collective-permute-done((bf16[4,48,1536]{2,1,0:T(8,128)(2,1)}, bf16[4,48,1536]{2,1,0:T(8,128)(2,1)S(1)}, u32[]{:S(2)}, u32[]{:S(2)}) %collective-permute-start.56) | collective-permute-done | bytes 589856 | tf_op jit(solution)/shard_map/ppermute | solution.py:136
  387.0 1.6 fusion.3
  388.6 1.9 collective-permute-start.58
  393.3 2.9 collective-permute-done.58
  396.2 2.2 collective-permute-done.59
  399.4 1.5 reshape.287
  400.9 2.0 fusion.28
  403.0 3.5 collective-permute-start.37
  406.5 1.9 collective-permute-start.36
  408.4 1.6 fusion.27
  410.2 1.9 collective-permute-start.51
  412.1 3.0 collective-permute-start.49
  415.1 18.4 %collective-permute-done.37 = bf16[4,48,768]{2,1,0:T(8,128)(2,1)S(1)} collective-permute-done((bf16[4,48,768]{2,1,0:T(8,128)(2,1)S(1)}, bf16[4,48,768]{2,1,0:T(8,128)(2,1)S(1)}, u32[]{:S(2)}, u32[]{:S(2)}) %collective-permute-start.37) | collective-permute-done | bytes 294944 | tf_op jit(solution)/shard_map/ppermute | solution.py:136
  433.6 2.2 collective-permute-start.39
  437.2 20.7 %collective-permute-done.50 = bf16[4,48,768]{2,1,0:T(8,128)(2,1)S(1)} collective-permute-done((bf16[4,48,768]{2,1,0:T(8,128)(2,1)S(1)}, bf16[4,48,768]{2,1,0:T(8,128)(2,1)S(1)}, u32[]{:S(2)}, u32[]{:S(2)}) %collective-permute-start.50) | collective-permute-done | bytes 294944 | tf_op jit(solution)/shard_map/ppermute | solution.py:136
  458.1 1.7 collective-permute-start.52
  461.7 2.5 collective-permute-done.52
  468.0 2.2 bitcast_convert_fusion
  (281 shorter events, 71.6 us)
Async XLA Ops:
  7.2 165.3 %all-gather.3.cloned.1.call-start = ((), (), s32[]{:S(2)}) async-start(), calls=%async_computation.3 | async-start | bytes 2949120 | tf_op jit(solution)/shard_map/all_gather | solution.py:394
  9.4 17.6 %collective-permute-start = (bf16[48,1536]{1,0:T(8,128)(2,1)S(1)}, bf16[48,1536]{1,0:T(8,128)(2,1)S(1)}, u32[]{:S(2)}, u32[]{:S(2)}) collective-permute-start(bf16[48,1536]{1,0:T(8,128)(2,1)S(1)} %get-tuple-element.153), channel_id=1, source_target_pairs={{0,2},{1,3},{2,0},{3,1},{4,6},{5,7},{6,4},{7,5},{8,10},{9,11},{10,... | collective-permute-start | bytes 442376 | tf_op jit(solution)/shard_map/ppermute | solution.py:59
  12.4 14.6 %collective-permute-start.1 = (bf16[48,1536]{1,0:T(8,128)(2,1)S(1)}, bf16[48,1536]{1,0:T(8,128)(2,1)S(1)}, u32[]{:S(2)}, u32[]{:S(2)}) collective-permute-start(bf16[48,1536]{1,0:T(8,128)(2,1)S(1)} %get-tuple-element.152), channel_id=1, source_target_pairs={{0,4},{1,5},{2,6},{3,7},{4,0},{5,1},{6,2},{7,3},{8,12},{9,13},{10,... | collective-permute-start | bytes 442376 | tf_op jit(solution)/shard_map/ppermute | solution.py:59
  13.9 13.1 %collective-permute-start.2 = (bf16[48,1536]{1,0:T(8,128)(2,1)S(1)}, bf16[48,1536]{1,0:T(8,128)(2,1)S(1)}, u32[]{:S(2)}, u32[]{:S(2)}) collective-permute-start(bf16[48,1536]{1,0:T(8,128)(2,1)S(1)} %get-tuple-element.151), channel_id=1, source_target_pairs={{0,6},{1,7},{2,4},{3,5},{4,2},{5,3},{6,0},{7,1},{8,14},{9,15},{10,... | collective-permute-start | bytes 442376 | tf_op jit(solution)/shard_map/ppermute | solution.py:59
  27.1 15.7 %collective-permute-start.8 = (bf16[192,1536]{1,0:T(8,128)(2,1)S(1)}, bf16[192,1536]{1,0:T(8,128)(2,1)S(1)}, u32[]{:S(2)}, u32[]{:S(2)}) collective-permute-start(bf16[192,1536]{1,0:T(8,128)(2,1)S(1)} %pad_maximum_fusion.1), channel_id=1, source_target_pairs={{0,8},{1,9},{2,10},{3,11},{4,12},{5,13},{6,14},{7,15},{8,16},{9,17... | collective-permute-start | bytes 1769480 | tf_op jit(solution)/shard_map/ppermute | solution.py:70
  31.1 15.8 %collective-permute-start.9 = (bf16[192,1536]{1,0:T(8,128)(2,1)S(1)}, bf16[192,1536]{1,0:T(8,128)(2,1)S(1)}, u32[]{:S(2)}, u32[]{:S(2)}) collective-permute-start(bf16[192,1536]{1,0:T(8,128)(2,1)S(1)} %pad_maximum_fusion.1), channel_id=1, source_target_pairs={{8,0},{9,1},{10,2},{11,3},{12,4},{13,5},{14,6},{15,7},{16,8},{17,9... | collective-permute-start | bytes 1769480 | tf_op jit(solution)/shard_map/ppermute | solution.py:70
  47.0 19.7 %collective-permute-start.18 = (bf16[192,1536]{1,0:T(8,128)(2,1)S(1)}, bf16[192,1536]{1,0:T(8,128)(2,1)S(1)}, u32[]{:S(2)}, u32[]{:S(2)}) collective-permute-start(bf16[192,1536]{1,0:T(8,128)(2,1)S(1)} %collective-permute-done.9), channel_id=1, source_target_pairs={{8,0},{9,1},{10,2},{11,3},{12,4},{13,5},{14,6},{15,7},{16,8},{17,9... | collective-permute-start | bytes 1769480 | tf_op jit(solution)/shard_map/ppermute | solution.py:70
  48.3 19.6 %collective-permute-start.3 = (f32[32,256]{1,0:T(8,128)S(1)}, f32[32,256]{1,0:T(8,128)S(1)}, u32[]{:S(2)}, u32[]{:S(2)}) collective-permute-start(f32[32,256]{1,0:T(8,128)S(1)} %broadcast_select_fusion.29), channel_id=1, source_target_pairs={{0,1},{1,0},{2,3},{3,2},{4,5},{5,4},{6,7},{7,6},{8,9},{9,8},{10,11... | collective-permute-start | bytes 98312 | tf_op jit(solution)/shard_map/ppermute | solution.py:59
  48.4 419.6 %reduce-scatter.2.cloned.1.call-start = ((), (), s32[]{:S(2)}) async-start(), calls=%async_computation.2 | async-start | bytes 2949120 | tf_op jit(solution)/shard_map/reduce_scatter | solution.py:501
  48.4 21.2 %collective-permute-start.16 = (bf16[192,1536]{1,0:T(8,128)(2,1)S(1)}, bf16[192,1536]{1,0:T(8,128)(2,1)}, u32[]{:S(2)}, u32[]{:S(2)}) collective-permute-start(bf16[192,1536]{1,0:T(8,128)(2,1)S(1)} %collective-permute-done.8), channel_id=1, source_target_pairs={{8,16},{9,17},{10,18},{11,19},{12,20},{13,21},{14,22},{15,23},{16,... | collective-permute-start | bytes 1769480 | tf_op jit(solution)/shard_map/ppermute | solution.py:70
  66.7 43.9 %collective-permute-start.19 = (bf16[192,1536]{1,0:T(8,128)(2,1)S(1)}, bf16[192,1536]{1,0:T(8,128)(2,1)S(1)}, u32[]{:S(2)}, u32[]{:S(2)}) collective-permute-start(bf16[192,1536]{1,0:T(8,128)(2,1)S(1)} %collective-permute-done.18), channel_id=1, source_target_pairs={{8,0},{9,1},{10,2},{11,3},{12,4},{13,5},{14,6},{15,7}} | collective-permute-start | bytes 1769480 | tf_op jit(solution)/shard_map/ppermute | solution.py:70
  68.0 44.4 %collective-permute-start.4 = (f32[32,256]{1,0:T(8,128)S(1)}, f32[32,256]{1,0:T(8,128)S(1)}, u32[]{:S(2)}, u32[]{:S(2)}) collective-permute-start(f32[32,256]{1,0:T(8,128)S(1)} %fusion.23), channel_id=1, source_target_pairs={{0,2},{1,3},{2,0},{3,1},{4,6},{5,7},{6,4},{7,5},{8,10},{9,11},{10,... | collective-permute-start | bytes 98312 | tf_op jit(solution)/shard_map/ppermute | solution.py:59
  69.6 41.1 %collective-permute-start.17 = (bf16[192,1536]{1,0:T(8,128)(2,1)}, bf16[192,1536]{1,0:T(8,128)(2,1)S(1)}, u32[]{:S(2)}, u32[]{:S(2)}) collective-permute-start(bf16[192,1536]{1,0:T(8,128)(2,1)} %collective-permute-done.16), channel_id=1, source_target_pairs={{16,24},{17,25},{18,26},{19,27},{20,28},{21,29},{22,30},{23,31}} | collective-permute-start | bytes 1769480 | tf_op jit(solution)/shard_map/ppermute | solution.py:70
  112.4 60.0 %collective-permute-start.20 = (bf16[4,4,48,1536]{3,2,1,0:T(8,128)(2,1)}, bf16[4,4,48,1536]{3,2,1,0:T(8,128)(2,1)}, u32[]{:S(2)}, u32[]{:S(2)}) collective-permute-start(bf16[4,4,48,1536]{3,2,1,0:T(8,128)(2,1)} %pad_maximum_fusion), channel_id=1, source_target_pairs={{0,1},{1,0},{2,3},{3,2},{4,5},{5,4},{6,7},{7,6},{8,9},{9,8},{10,11... | collective-permute-start | bytes 7077896 | tf_op jit(solution)/shard_map/ppermute | solution.py:59
  112.5 3.9 collective-permute-start.5
  120.4 9.9 %collective-permute-start.7 = (f32[32,256]{1,0:T(8,128)S(1)}, f32[32,256]{1,0:T(8,128)S(1)}, u32[]{:S(2)}, u32[]{:S(2)}) collective-permute-start(f32[32,256]{1,0:T(8,128)S(1)} %add.280), channel_id=1, source_target_pairs={{0,16},{1,17},{2,18},{3,19},{4,20},{5,21},{6,22},{7,23},{8,24},{9,... | collective-permute-start | bytes 98312 | tf_op jit(solution)/shard_map/ppermute | solution.py:59
  133.7 44.0 %collective-permute-start.13 = (bf16[160,1536]{1,0:T(8,128)(2,1)}, bf16[160,1536]{1,0:T(8,128)(2,1)}, u32[]{:S(2)}, u32[]{:S(2)}) collective-permute-start(bf16[160,1536]{1,0:T(8,128)(2,1)} %get-tuple-element.122.refs_4_.refs_0_), channel_id=1, source_target_pairs={{0,2},{1,3},{2,0},{3,1},{4,6},{5,7},{6,4},{7,5},{8,10},{9,11},{10,... | collective-permute-start | bytes 1474568 | tf_op jit(solution)/shard_map/ppermute | solution.py:59
  137.1 21.4 %collective-permute-start.10 = (bf16[160,1536]{1,0:T(8,128)(2,1)S(1)}, bf16[160,1536]{1,0:T(8,128)(2,1)S(1)}, u32[]{:S(2)}, u32[]{:S(2)}) collective-permute-start(bf16[160,1536]{1,0:T(8,128)(2,1)S(1)} %fusion.15.refs_0_), channel_id=1, source_target_pairs={{0,2},{1,3},{2,0},{3,1},{4,6},{5,7},{6,4},{7,5},{8,10},{9,11},{10,... | collective-permute-start | bytes 1474568 | tf_op jit(solution)/shard_map/ppermute | solution.py:59
  137.7 22.4 %collective-permute-start.11 = (bf16[160,1536]{1,0:T(8,128)(2,1)S(1)}, bf16[160,1536]{1,0:T(8,128)(2,1)S(1)}, u32[]{:S(2)}, u32[]{:S(2)}) collective-permute-start(bf16[160,1536]{1,0:T(8,128)(2,1)S(1)} %fusion.15.refs_0_), channel_id=1, source_target_pairs={{0,4},{1,5},{2,6},{3,7},{4,0},{5,1},{6,2},{7,3},{8,12},{9,13},{10,... | collective-permute-start | bytes 1474568 | tf_op jit(solution)/shard_map/ppermute | solution.py:59
  139.2 30.9 %collective-permute-start.12 = (bf16[160,1536]{1,0:T(8,128)(2,1)S(1)}, bf16[160,1536]{1,0:T(8,128)(2,1)S(1)}, u32[]{:S(2)}, u32[]{:S(2)}) collective-permute-start(bf16[160,1536]{1,0:T(8,128)(2,1)S(1)} %fusion.15.refs_0_), channel_id=1, source_target_pairs={{0,6},{1,7},{2,4},{3,5},{4,2},{5,3},{6,0},{7,1},{8,14},{9,15},{10,... | collective-permute-start | bytes 1474568 | tf_op jit(solution)/shard_map/ppermute | solution.py:59
  158.6 34.6 %collective-permute-start.14 = (bf16[160,1536]{1,0:T(8,128)(2,1)}, bf16[160,1536]{1,0:T(8,128)(2,1)}, u32[]{:S(2)}, u32[]{:S(2)}) collective-permute-start(bf16[160,1536]{1,0:T(8,128)(2,1)} %get-tuple-element.122.refs_4_.refs_0_), channel_id=1, source_target_pairs={{0,4},{1,5},{2,6},{3,7},{4,0},{5,1},{6,2},{7,3},{8,12},{9,13},{10,... | collective-permute-start | bytes 1474568 | tf_op jit(solution)/shard_map/ppermute | solution.py:59
  160.1 34.5 %collective-permute-start.15 = (bf16[160,1536]{1,0:T(8,128)(2,1)}, bf16[160,1536]{1,0:T(8,128)(2,1)}, u32[]{:S(2)}, u32[]{:S(2)}) collective-permute-start(bf16[160,1536]{1,0:T(8,128)(2,1)} %get-tuple-element.122.refs_4_.refs_0_), channel_id=1, source_target_pairs={{0,6},{1,7},{2,4},{3,5},{4,2},{5,3},{6,0},{7,1},{8,14},{9,15},{10,... | collective-permute-start | bytes 1474568 | tf_op jit(solution)/shard_map/ppermute | solution.py:59
  171.0 74.6 %collective-permute-start.29 = (bf16[160,1536]{1,0:T(8,128)(2,1)S(1)}, bf16[160,1536]{1,0:T(8,128)(2,1)}, u32[]{:S(2)}, u32[]{:S(2)}) collective-permute-start(bf16[160,1536]{1,0:T(8,128)(2,1)S(1)} %fusion.13.refs_0_.refs_4_), channel_id=1, source_target_pairs={{0,2},{1,3},{2,0},{3,1},{4,6},{5,7},{6,4},{7,5},{8,10},{9,11},{10,... | collective-permute-start | bytes 1474568 | tf_op jit(solution)/shard_map/ppermute | solution.py:59
  172.5 40.3 %collective-permute-start.21 = (bf16[4,192,1536]{2,1,0:T(8,128)(2,1)}, bf16[4,192,1536]{2,1,0:T(8,128)(2,1)S(1)}, u32[]{:S(2)}, u32[]{:S(2)}) collective-permute-start(bf16[4,192,1536]{2,1,0:T(8,128)(2,1)} %bitcast.227), channel_id=1, source_target_pairs={{0,1},{1,0},{2,3},{3,2},{4,5},{5,4},{6,7},{7,6},{8,9},{9,8},{10,11... | collective-permute-start | bytes 7077896 | tf_op jit(solution)/shard_map/ppermute | solution.py:59
  177.7 69.4 %collective-permute-start.30 = (bf16[160,1536]{1,0:T(8,128)(2,1)S(1)}, bf16[160,1536]{1,0:T(8,128)(2,1)S(1)}, u32[]{:S(2)}, u32[]{:S(2)}) collective-permute-start(bf16[160,1536]{1,0:T(8,128)(2,1)S(1)} %fusion.13.refs_0_.refs_4_), channel_id=1, source_target_pairs={{0,4},{1,5},{2,6},{3,7},{4,0},{5,1},{6,2},{7,3},{8,12},{9,13},{10,... | collective-permute-start | bytes 1474568 | tf_op jit(solution)/shard_map/ppermute | solution.py:59
  193.2 54.5 %collective-permute-start.31 = (bf16[160,1536]{1,0:T(8,128)(2,1)S(1)}, bf16[160,1536]{1,0:T(8,128)(2,1)S(1)}, u32[]{:S(2)}, u32[]{:S(2)}) collective-permute-start(bf16[160,1536]{1,0:T(8,128)(2,1)S(1)} %fusion.13.refs_0_.refs_4_), channel_id=1, source_target_pairs={{0,6},{1,7},{2,4},{3,5},{4,2},{5,3},{6,0},{7,1},{8,14},{9,15},{10,... | collective-permute-start | bytes 1474568 | tf_op jit(solution)/shard_map/ppermute | solution.py:59
  212.8 62.5 %collective-permute-start.61 = (bf16[4,192,1536]{2,1,0:T(8,128)(2,1)}, bf16[4,192,1536]{2,1,0:T(8,128)(2,1)S(1)}, u32[]{:S(2)}, u32[]{:S(2)}) collective-permute-start(bf16[4,192,1536]{2,1,0:T(8,128)(2,1)} %dynamic-slice_bitcast_fusion), channel_id=1, source_target_pairs={{0,1},{1,0},{2,3},{3,2},{4,5},{5,4},{6,7},{7,6},{8,9},{9,8},{10,11... | collective-permute-start | bytes 7077896 | tf_op jit(solution)/shard_map/ppermute | solution.py:59
  245.1 34.0 %collective-permute-start.25 = (bf16[4,4,48,1536]{3,2,1,0:T(8,128)(2,1)}, bf16[4,4,48,1536]{3,2,1,0:T(8,128)(2,1)}, u32[]{:S(2)}, u32[]{:S(2)}) collective-permute-start(bf16[4,4,48,1536]{3,2,1,0:T(8,128)(2,1)} %dynamic-slice_bitcast_fusion.1), channel_id=1, source_target_pairs={{0,1},{1,0},{2,3},{3,2},{4,5},{5,4},{6,7},{7,6},{8,9},{9,8},{10,11... | collective-permute-start | bytes 7077896 | tf_op jit(solution)/shard_map/ppermute | solution.py:59
  245.6 15.3 %collective-permute-start.24 = (bf16[160,1536]{1,0:T(8,128)(2,1)}, bf16[160,1536]{1,0:T(8,128)(2,1)}, u32[]{:S(2)}, u32[]{:S(2)}) collective-permute-start(bf16[160,1536]{1,0:T(8,128)(2,1)} %get-tuple-element.86), channel_id=1, source_target_pairs={{0,6},{1,7},{2,4},{3,5},{4,2},{5,3},{6,0},{7,1},{8,14},{9,15},{10,... | collective-permute-start | bytes 1474568 | tf_op jit(solution)/shard_map/ppermute | solution.py:59
  247.1 23.4 %collective-permute-start.23 = (bf16[160,1536]{1,0:T(8,128)(2,1)}, bf16[160,1536]{1,0:T(8,128)(2,1)}, u32[]{:S(2)}, u32[]{:S(2)}) collective-permute-start(bf16[160,1536]{1,0:T(8,128)(2,1)} %get-tuple-element.85), channel_id=1, source_target_pairs={{0,4},{1,5},{2,6},{3,7},{4,0},{5,1},{6,2},{7,3},{8,12},{9,13},{10,... | collective-permute-start | bytes 1474568 | tf_op jit(solution)/shard_map/ppermute | solution.py:59
  248.4 23.2 %collective-permute-start.22 = (bf16[160,1536]{1,0:T(8,128)(2,1)}, bf16[160,1536]{1,0:T(8,128)(2,1)}, u32[]{:S(2)}, u32[]{:S(2)}) collective-permute-start(bf16[160,1536]{1,0:T(8,128)(2,1)} %get-tuple-element.84), channel_id=1, source_target_pairs={{0,2},{1,3},{2,0},{3,1},{4,6},{5,7},{6,4},{7,5},{8,10},{9,11},{10,... | collective-permute-start | bytes 1474568 | tf_op jit(solution)/shard_map/ppermute | solution.py:59
  261.0 67.0 %collective-permute-start.42 = (bf16[160,1536]{1,0:T(8,128)(2,1)S(1)}, bf16[160,1536]{1,0:T(8,128)(2,1)S(1)}, u32[]{:S(2)}, u32[]{:S(2)}) collective-permute-start(bf16[160,1536]{1,0:T(8,128)(2,1)S(1)} %fusion.12.refs_0_), channel_id=1, source_target_pairs={{0,2},{1,3},{2,0},{3,1},{4,6},{5,7},{6,4},{7,5},{8,10},{9,11},{10,... | collective-permute-start | bytes 1474568 | tf_op jit(solution)/shard_map/ppermute | solution.py:59
  270.5 57.6 %collective-permute-start.43 = (bf16[160,1536]{1,0:T(8,128)(2,1)S(1)}, bf16[160,1536]{1,0:T(8,128)(2,1)}, u32[]{:S(2)}, u32[]{:S(2)}) collective-permute-start(bf16[160,1536]{1,0:T(8,128)(2,1)S(1)} %fusion.12.refs_0_), channel_id=1, source_target_pairs={{0,4},{1,5},{2,6},{3,7},{4,0},{5,1},{6,2},{7,3},{8,12},{9,13},{10,... | collective-permute-start | bytes 1474568 | tf_op jit(solution)/shard_map/ppermute | solution.py:59
  271.6 59.6 %collective-permute-start.44 = (bf16[160,1536]{1,0:T(8,128)(2,1)S(1)}, bf16[160,1536]{1,0:T(8,128)(2,1)}, u32[]{:S(2)}, u32[]{:S(2)}) collective-permute-start(bf16[160,1536]{1,0:T(8,128)(2,1)S(1)} %fusion.12.refs_0_), channel_id=1, source_target_pairs={{0,6},{1,7},{2,4},{3,5},{4,2},{5,3},{6,0},{7,1},{8,14},{9,15},{10,... | collective-permute-start | bytes 1474568 | tf_op jit(solution)/shard_map/ppermute | solution.py:59
  314.6 16.5 %all-to-all-start = ((f32[32,1,512]{2,1,0:T(1,128)}), f32[32,1,512]{2,1,0:T(1,128)S(1)}, u32[]{:S(2)}, u32[]{:S(2)}) async-start(f32[32,1,512]{2,1,0:T(1,128)} %broadcast_in_dim.102), calls=%async_computation | async-start | bytes 131072 | tf_op jit(solution)/shard_map/all_to_all | solution.py:607
  321.0 11.7 %collective-permute-start.32 = (bf16[160,768]{1,0:T(8,128)(2,1)S(1)}, bf16[160,768]{1,0:T(8,128)(2,1)}, u32[]{:S(2)}, u32[]{:S(2)}) collective-permute-start(bf16[160,768]{1,0:T(8,128)(2,1)S(1)} %get-tuple-element.142), channel_id=1, source_target_pairs={{0,2},{1,3},{2,0},{3,1},{4,6},{5,7},{6,4},{7,5},{8,10},{9,11},{10,... | collective-permute-start | bytes 737288 | tf_op jit(solution)/shard_map/ppermute | solution.py:59
  322.7 12.3 %collective-permute-start.33 = (bf16[160,768]{1,0:T(8,128)(2,1)S(1)}, bf16[160,768]{1,0:T(8,128)(2,1)}, u32[]{:S(2)}, u32[]{:S(2)}) collective-permute-start(bf16[160,768]{1,0:T(8,128)(2,1)S(1)} %get-tuple-element.141), channel_id=1, source_target_pairs={{0,4},{1,5},{2,6},{3,7},{4,0},{5,1},{6,2},{7,3},{8,12},{9,13},{10,... | collective-permute-start | bytes 737288 | tf_op jit(solution)/shard_map/ppermute | solution.py:59
  327.9 9.8 %collective-permute-start.34 = (bf16[160,768]{1,0:T(8,128)(2,1)S(1)}, bf16[160,768]{1,0:T(8,128)(2,1)S(1)}, u32[]{:S(2)}, u32[]{:S(2)}) collective-permute-start(bf16[160,768]{1,0:T(8,128)(2,1)S(1)} %get-tuple-element.140), channel_id=1, source_target_pairs={{0,6},{1,7},{2,4},{3,5},{4,2},{5,3},{6,0},{7,1},{8,14},{9,15},{10,... | collective-permute-start | bytes 737288 | tf_op jit(solution)/shard_map/ppermute | solution.py:59
  328.7 13.4 %collective-permute-start.45 = (bf16[160,768]{1,0:T(8,128)(2,1)S(1)}, bf16[160,768]{1,0:T(8,128)(2,1)S(1)}, u32[]{:S(2)}, u32[]{:S(2)}) collective-permute-start(bf16[160,768]{1,0:T(8,128)(2,1)S(1)} %get-tuple-element.138), channel_id=1, source_target_pairs={{0,2},{1,3},{2,0},{3,1},{4,6},{5,7},{6,4},{7,5},{8,10},{9,11},{10,... | collective-permute-start | bytes 737288 | tf_op jit(solution)/shard_map/ppermute | solution.py:59
  331.2 19.1 %collective-permute-start.46 = (bf16[160,768]{1,0:T(8,128)(2,1)S(1)}, bf16[160,768]{1,0:T(8,128)(2,1)S(1)}, u32[]{:S(2)}, u32[]{:S(2)}) collective-permute-start(bf16[160,768]{1,0:T(8,128)(2,1)S(1)} %get-tuple-element.137), channel_id=1, source_target_pairs={{0,4},{1,5},{2,6},{3,7},{4,0},{5,1},{6,2},{7,3},{8,12},{9,13},{10,... | collective-permute-start | bytes 737288 | tf_op jit(solution)/shard_map/ppermute | solution.py:59
  332.7 19.1 %collective-permute-start.47 = (bf16[160,768]{1,0:T(8,128)(2,1)S(1)}, bf16[160,768]{1,0:T(8,128)(2,1)S(1)}, u32[]{:S(2)}, u32[]{:S(2)}) collective-permute-start(bf16[160,768]{1,0:T(8,128)(2,1)S(1)} %get-tuple-element.136), channel_id=1, source_target_pairs={{0,6},{1,7},{2,4},{3,5},{4,2},{5,3},{6,0},{7,1},{8,14},{9,15},{10,... | collective-permute-start | bytes 737288 | tf_op jit(solution)/shard_map/ppermute | solution.py:59
  335.0 27.3 %collective-permute-start.57 = (bf16[4,48,1536]{2,1,0:T(8,128)(2,1)}, bf16[4,48,1536]{2,1,0:T(8,128)(2,1)S(1)}, u32[]{:S(2)}, u32[]{:S(2)}) collective-permute-start(bf16[4,48,1536]{2,1,0:T(8,128)(2,1)} %get-tuple-element.124), channel_id=1, source_target_pairs={{0,24},{1,25},{2,26},{3,27},{4,28},{5,29},{6,30},{7,31},{8,0},{9,1... | collective-permute-start | bytes 1769480 | tf_op jit(solution)/shard_map/ppermute | solution.py:136
  337.7 48.7 %collective-permute-start.56 = (bf16[4,48,1536]{2,1,0:T(8,128)(2,1)}, bf16[4,48,1536]{2,1,0:T(8,128)(2,1)S(1)}, u32[]{:S(2)}, u32[]{:S(2)}) collective-permute-start(bf16[4,48,1536]{2,1,0:T(8,128)(2,1)} %get-tuple-element.125), channel_id=1, source_target_pairs={{0,16},{1,17},{2,18},{3,19},{4,20},{5,21},{6,22},{7,23},{8,24},{9,... | collective-permute-start | bytes 1769480 | tf_op jit(solution)/shard_map/ppermute | solution.py:136
  342.1 44.4 %collective-permute-start.55 = (bf16[4,48,1536]{2,1,0:T(8,128)(2,1)S(1)}, bf16[4,48,1536]{2,1,0:T(8,128)(2,1)S(1)}, u32[]{:S(2)}, u32[]{:S(2)}) collective-permute-start(bf16[4,48,1536]{2,1,0:T(8,128)(2,1)S(1)} %get-tuple-element.123), channel_id=1, source_target_pairs={{0,8},{1,9},{2,10},{3,11},{4,12},{5,13},{6,14},{7,15},{8,16},{9,17... | collective-permute-start | bytes 1769480 | tf_op jit(solution)/shard_map/ppermute | solution.py:136
  350.3 38.3 %collective-permute-start.28 = (bf16[160,1536]{1,0:T(8,128)(2,1)}, bf16[160,1536]{1,0:T(8,128)(2,1)S(1)}, u32[]{:S(2)}, u32[]{:S(2)}) collective-permute-start(bf16[160,1536]{1,0:T(8,128)(2,1)} %get-tuple-element.93), channel_id=1, source_target_pairs={{0,6},{1,7},{2,4},{3,5},{4,2},{5,3},{6,0},{7,1},{8,14},{9,15},{10,... | collective-permute-start | bytes 1474568 | tf_op jit(solution)/shard_map/ppermute | solution.py:59
  351.8 38.7 %collective-permute-start.27 = (bf16[160,1536]{1,0:T(8,128)(2,1)}, bf16[160,1536]{1,0:T(8,128)(2,1)S(1)}, u32[]{:S(2)}, u32[]{:S(2)}) collective-permute-start(bf16[160,1536]{1,0:T(8,128)(2,1)} %get-tuple-element.92), channel_id=1, source_target_pairs={{0,4},{1,5},{2,6},{3,7},{4,0},{5,1},{6,2},{7,3},{8,12},{9,13},{10,... | collective-permute-start | bytes 1474568 | tf_op jit(solution)/shard_map/ppermute | solution.py:59
  362.3 28.8 %collective-permute-start.26 = (bf16[160,1536]{1,0:T(8,128)(2,1)S(1)}, bf16[160,1536]{1,0:T(8,128)(2,1)S(1)}, u32[]{:S(2)}, u32[]{:S(2)}) collective-permute-start(bf16[160,1536]{1,0:T(8,128)(2,1)S(1)} %copy-done.30), channel_id=1, source_target_pairs={{0,2},{1,3},{2,0},{3,1},{4,6},{5,7},{6,4},{7,5},{8,10},{9,11},{10,... | collective-permute-start | bytes 1474568 | tf_op jit(solution)/shard_map/ppermute | solution.py:59
  386.4 14.5 %collective-permute-start.35 = (bf16[4,4,48,768]{3,2,1,0:T(8,128)(2,1)}, bf16[4,4,48,768]{3,2,1,0:T(8,128)(2,1)}, u32[]{:S(2)}, u32[]{:S(2)}) collective-permute-start(bf16[4,4,48,768]{3,2,1,0:T(8,128)(2,1)} %dynamic-slice_bitcast_fusion.3), channel_id=1, source_target_pairs={{0,1},{1,0},{2,3},{3,2},{4,5},{5,4},{6,7},{7,6},{8,9},{9,8},{10,11... | collective-permute-start | bytes 3538952 | tf_op jit(solution)/shard_map/ppermute | solution.py:59
  386.4 22.0 %collective-permute-start.48 = (bf16[4,4,48,768]{3,2,1,0:T(8,128)(2,1)}, bf16[4,4,48,768]{3,2,1,0:T(8,128)(2,1)}, u32[]{:S(2)}, u32[]{:S(2)}) collective-permute-start(bf16[4,4,48,768]{3,2,1,0:T(8,128)(2,1)} %dynamic-slice_bitcast_fusion.2), channel_id=1, source_target_pairs={{0,1},{1,0},{2,3},{3,2},{4,5},{5,4},{6,7},{7,6},{8,9},{9,8},{10,11... | collective-permute-start | bytes 3538952 | tf_op jit(solution)/shard_map/ppermute | solution.py:59
  388.6 7.7 %collective-permute-start.58 = (bf16[48,1536]{1,0:T(8,128)(2,1)S(1)}, bf16[48,1536]{1,0:T(8,128)(2,1)S(1)}, u32[]{:S(2)}, u32[]{:S(2)}) collective-permute-start(bf16[48,1536]{1,0:T(8,128)(2,1)S(1)} %get-tuple-element.146), channel_id=1, source_target_pairs={{0,6},{1,7},{2,4},{3,5},{4,2},{5,3},{6,0},{7,1},{8,14},{9,15},{10,... | collective-permute-start | bytes 442376 | tf_op jit(solution)/shard_map/ppermute | solution.py:59
  390.5 7.9 %collective-permute-start.59 = (bf16[48,1536]{1,0:T(8,128)(2,1)S(1)}, bf16[48,1536]{1,0:T(8,128)(2,1)S(1)}, u32[]{:S(2)}, u32[]{:S(2)}) collective-permute-start(bf16[48,1536]{1,0:T(8,128)(2,1)S(1)} %get-tuple-element.145), channel_id=1, source_target_pairs={{0,4},{1,5},{2,6},{3,7},{4,0},{5,1},{6,2},{7,3},{8,12},{9,13},{10,... | collective-permute-start | bytes 442376 | tf_op jit(solution)/shard_map/ppermute | solution.py:59
  391.1 7.4 %collective-permute-start.60 = (bf16[48,1536]{1,0:T(8,128)(2,1)S(1)}, bf16[48,1536]{1,0:T(8,128)(2,1)S(1)}, u32[]{:S(2)}, u32[]{:S(2)}) collective-permute-start(bf16[48,1536]{1,0:T(8,128)(2,1)S(1)} %get-tuple-element.144), channel_id=1, source_target_pairs={{0,2},{1,3},{2,0},{3,1},{4,6},{5,7},{6,4},{7,5},{8,10},{9,11},{10,... | collective-permute-start | bytes 442376 | tf_op jit(solution)/shard_map/ppermute | solution.py:59
  403.0 9.1 %collective-permute-start.38 = (bf16[4,48,768]{2,1,0:T(8,128)(2,1)S(1)}, bf16[4,48,768]{2,1,0:T(8,128)(2,1)S(1)}, u32[]{:S(2)}, u32[]{:S(2)}) collective-permute-start(bf16[4,48,768]{2,1,0:T(8,128)(2,1)S(1)} %get-tuple-element.130), channel_id=1, source_target_pairs={{0,24},{1,25},{2,26},{3,27},{4,28},{5,29},{6,30},{7,31},{8,0},{9,1... | collective-permute-start | bytes 884744 | tf_op jit(solution)/shard_map/ppermute | solution.py:136
  403.0 30.4 %collective-permute-start.37 = (bf16[4,48,768]{2,1,0:T(8,128)(2,1)S(1)}, bf16[4,48,768]{2,1,0:T(8,128)(2,1)S(1)}, u32[]{:S(2)}, u32[]{:S(2)}) collective-permute-start(bf16[4,48,768]{2,1,0:T(8,128)(2,1)S(1)} %get-tuple-element.131), channel_id=1, source_target_pairs={{0,16},{1,17},{2,18},{3,19},{4,20},{5,21},{6,22},{7,23},{8,24},{9,... | collective-permute-start | bytes 884744 | tf_op jit(solution)/shard_map/ppermute | solution.py:136
  406.5 27.0 %collective-permute-start.36 = (bf16[4,48,768]{2,1,0:T(8,128)(2,1)S(1)}, bf16[4,48,768]{2,1,0:T(8,128)(2,1)S(1)}, u32[]{:S(2)}, u32[]{:S(2)}) collective-permute-start(bf16[4,48,768]{2,1,0:T(8,128)(2,1)S(1)} %get-tuple-element.129), channel_id=1, source_target_pairs={{0,8},{1,9},{2,10},{3,11},{4,12},{5,13},{6,14},{7,15},{8,16},{9,17... | collective-permute-start | bytes 884744 | tf_op jit(solution)/shard_map/ppermute | solution.py:136
  410.2 26.1 %collective-permute-start.51 = (bf16[4,48,768]{2,1,0:T(8,128)(2,1)S(1)}, bf16[4,48,768]{2,1,0:T(8,128)(2,1)S(1)}, u32[]{:S(2)}, u32[]{:S(2)}) collective-permute-start(bf16[4,48,768]{2,1,0:T(8,128)(2,1)S(1)} %get-tuple-element.127), channel_id=1, source_target_pairs={{0,24},{1,25},{2,26},{3,27},{4,28},{5,29},{6,30},{7,31},{8,0},{9,1... | collective-permute-start | bytes 884744 | tf_op jit(solution)/shard_map/ppermute | solution.py:136
  412.1 45.8 %collective-permute-start.50 = (bf16[4,48,768]{2,1,0:T(8,128)(2,1)S(1)}, bf16[4,48,768]{2,1,0:T(8,128)(2,1)S(1)}, u32[]{:S(2)}, u32[]{:S(2)}) collective-permute-start(bf16[4,48,768]{2,1,0:T(8,128)(2,1)S(1)} %get-tuple-element.128), channel_id=1, source_target_pairs={{0,16},{1,17},{2,18},{3,19},{4,20},{5,21},{6,22},{7,23},{8,24},{9,... | collective-permute-start | bytes 884744 | tf_op jit(solution)/shard_map/ppermute | solution.py:136
  412.1 45.8 %collective-permute-start.49 = (bf16[4,48,768]{2,1,0:T(8,128)(2,1)S(1)}, bf16[4,48,768]{2,1,0:T(8,128)(2,1)S(1)}, u32[]{:S(2)}, u32[]{:S(2)}) collective-permute-start(bf16[4,48,768]{2,1,0:T(8,128)(2,1)S(1)} %get-tuple-element.126), channel_id=1, source_target_pairs={{0,8},{1,9},{2,10},{3,11},{4,12},{5,13},{6,14},{7,15},{8,16},{9,17... | collective-permute-start | bytes 884744 | tf_op jit(solution)/shard_map/ppermute | solution.py:136
  433.6 26.9 %collective-permute-start.39 = (bf16[48,768]{1,0:T(8,128)(2,1)S(1)}, bf16[48,768]{1,0:T(8,128)(2,1)S(1)}, u32[]{:S(2)}, u32[]{:S(2)}) collective-permute-start(bf16[48,768]{1,0:T(8,128)(2,1)S(1)} %get-tuple-element.168), channel_id=1, source_target_pairs={{0,6},{1,7},{2,4},{3,5},{4,2},{5,3},{6,0},{7,1},{8,14},{9,15},{10,... | collective-permute-start | bytes 221192 | tf_op jit(solution)/shard_map/ppermute | solution.py:59
  435.8 25.8 %collective-permute-start.40 = (bf16[48,768]{1,0:T(8,128)(2,1)S(1)}, bf16[48,768]{1,0:T(8,128)(2,1)S(1)}, u32[]{:S(2)}, u32[]{:S(2)}) collective-permute-start(bf16[48,768]{1,0:T(8,128)(2,1)S(1)} %get-tuple-element.167), channel_id=1, source_target_pairs={{0,4},{1,5},{2,6},{3,7},{4,0},{5,1},{6,2},{7,3},{8,12},{9,13},{10,... | collective-permute-start | bytes 221192 | tf_op jit(solution)/shard_map/ppermute | solution.py:59
  436.2 25.4 %collective-permute-start.41 = (bf16[48,768]{1,0:T(8,128)(2,1)S(1)}, bf16[48,768]{1,0:T(8,128)(2,1)S(1)}, u32[]{:S(2)}, u32[]{:S(2)}) collective-permute-start(bf16[48,768]{1,0:T(8,128)(2,1)S(1)} %get-tuple-element.166), channel_id=1, source_target_pairs={{0,2},{1,3},{2,0},{3,1},{4,6},{5,7},{6,4},{7,5},{8,10},{9,11},{10,... | collective-permute-start | bytes 221192 | tf_op jit(solution)/shard_map/ppermute | solution.py:59
  458.1 6.2 %collective-permute-start.52 = (bf16[48,768]{1,0:T(8,128)(2,1)S(1)}, bf16[48,768]{1,0:T(8,128)(2,1)S(1)}, u32[]{:S(2)}, u32[]{:S(2)}) collective-permute-start(bf16[48,768]{1,0:T(8,128)(2,1)S(1)} %get-tuple-element.165), channel_id=1, source_target_pairs={{0,6},{1,7},{2,4},{3,5},{4,2},{5,3},{6,0},{7,1},{8,14},{9,15},{10,... | collective-permute-start | bytes 221192 | tf_op jit(solution)/shard_map/ppermute | solution.py:59
  459.7 4.8 %collective-permute-start.53 = (bf16[48,768]{1,0:T(8,128)(2,1)S(1)}, bf16[48,768]{1,0:T(8,128)(2,1)S(1)}, u32[]{:S(2)}, u32[]{:S(2)}) collective-permute-start(bf16[48,768]{1,0:T(8,128)(2,1)S(1)} %get-tuple-element.164), channel_id=1, source_target_pairs={{0,4},{1,5},{2,6},{3,7},{4,0},{5,1},{6,2},{7,3},{8,12},{9,13},{10,... | collective-permute-start | bytes 221192 | tf_op jit(solution)/shard_map/ppermute | solution.py:59
  460.6 4.4 collective-permute-start.54
  (40 other events, 577.8 us)
Sparse Core Ops, SparseCore 0:
  48.5 64.2 all-gather.2
  279.2 50.1 reduce-scatter.1
